TPU v7x, 128 devices: a whole 4x4x4 slice. The times are simulated.
128 devices in a mesh: radial: 16 (over x, y), mode: 8 (over z, core).
Axes of the slice: x: 4, y: 4, z: 4, core: 2. Of those that a mesh axis runs over, the one named last changes fastest.
Arguments:
- scalar_field: float32 [512, 128, 2, 384], P('radial', 'mode'), may hold values from -48 to 48
- radial_flow: float32 [512, 128, 2, 384], P('radial', 'mode'), may hold values from -6 to 6
- legendre: bfloat16 [128, 384, 768], P('mode'), may hold values from -0.3125 to 0.3125
- diffusivity: float32 [512], P('radial'), may hold values from 1000 to 100000
Outputs:
- field_new: float32 [512, 128, 2, 384], P('radial', 'mode')
All inputs are finite; a program needn't handle non-finite values.
Results may differ from a plain program's by a relative error of at most 0.0071.
Values may be sent and summed in bfloat16 or wider, within the bound.
No kernel may reach another device: no remote copies, remote signals or barrier semaphores. Data moves between devices by JAX's collectives and lax.ppermute only.
A program may use at most 128 MiB of HBM per device.

v0:
```python
import math

import jax
import jax.numpy as jnp
from jax import lax
from jax.sharding import Mesh
from jax.sharding import PartitionSpec as P

NLON = 1536
MODE = ("mode_0", "mode_1")
RADIAL = ("radial_0", "radial_1")


def split_up(array, dim, devices):
    before, after = (array.shape[:dim], array.shape[dim + 1 :])
    return jnp.moveaxis(array.reshape(*before, devices, -1, *after), dim, 0)


def in_order(parts, dim):
    parts = jnp.moveaxis(parts, 0, dim)
    shape = parts.shape
    return parts.reshape(*shape[:dim], shape[dim] * shape[dim + 1], *shape[dim + 2 :])


def turned_blocks(parts, axes, order):
    shape = [lax.axis_size(a) for a in axes]
    parts = parts.reshape(*shape, *parts.shape[1:])
    for k in order:
        parts = lax.all_to_all(parts, axes[k], split_axis=k, concat_axis=k, tiled=True)
    return parts.reshape(-1, *parts.shape[len(axes) :])


def two_step_exchange(array, groups, order, split_dim, concat_dim):
    devices = lax.axis_size(groups[0]) * lax.axis_size(groups[1])
    parts = split_up(array, split_dim, devices)
    return in_order(turned_blocks(parts, groups, order), concat_dim)


def neutral_like(array, identity):
    return jnp.zeros_like(array) + jnp.asarray(identity, array.dtype)


def entering(array, axes, combine, identity):
    before = start = neutral_like(array, identity)
    total = array
    for axis in reversed(axes):
        devices, position = (lax.axis_size(axis), lax.axis_index(axis))
        pieces = lax.all_gather(total, axis)
        inside, total = (start, start)
        for k in range(devices):
            passed = k < position
            total = combine(total, pieces[k])
            inside = jnp.where(passed, total, inside)
        before = combine(inside, before)
    return before


def sent_to_all(array, axis):
    devices = lax.axis_size(axis)
    return lax.all_to_all(
        jnp.broadcast_to(array[None], (devices, *array.shape)), axis, 0, 0, tiled=True
    )


def joined_by_halves(pieces, combine):
    while len(jax.tree.leaves(pieces)[0]) > 1:
        pieces = jax.vmap(combine)(
            *(jax.tree.map(lambda part: part[side::2], pieces) for side in (0, 1))
        )
    return jax.tree.map(lambda part: part[0], pieces)


def entering_2(array, axis, combine, identity):
    devices, position = (lax.axis_size(axis), lax.axis_index(axis))
    passed = jnp.arange(devices) > position

    def kept(part, zero, own):
        part = jnp.where(
            passed.reshape(-1, *(1 for _ in own.shape)), part, jnp.asarray(zero, own.dtype)
        )
        return part[::-1]

    pieces = jax.tree.map(lambda part: sent_to_all(part, axis), array)
    return joined_by_halves(jax.tree.map(kept, pieces, identity, array), combine)


def longitude_tables(orders, points):
    order_ids = jnp.arange(orders, dtype=jnp.int32)
    point_ids = jnp.arange(points, dtype=jnp.int32)
    phase = order_ids[:, None] * point_ids[None, :] % points
    angle = phase.astype(jnp.float32) * (2.0 * math.pi / points)
    cosine = jnp.cos(angle)
    sine_part = jnp.sin(angle)
    paired = jnp.stack([cosine, -sine_part], axis=1)
    synth_table = (paired / math.sqrt(orders)).astype(jnp.bfloat16)
    analysis_table = (paired * math.sqrt(2.0 / points)).astype(jnp.bfloat16)
    return (synth_table, analysis_table)


def normalized(matrix):
    largest = jnp.max(jnp.abs(matrix), axis=(0, 1))
    return matrix / largest


def combine_maps(earlier, later):
    return normalized(jnp.sum(later[:, :, None] * earlier[None, :, :], axis=1))


def combine_affine(earlier, later):
    return (later[0] + later[1][:, None, :] * earlier[0], later[1] * earlier[1])


def on_device(scalar_field, radial_flow, legendre, diffusivity):
    shells, ord_dev, halves, degrees = scalar_field.shape
    orders = ord_dev * lax.axis_size(MODE)
    synth_table, analysis_table = longitude_tables(orders, NLON)
    field_lat = jnp.einsum(
        "rmcj,mjt->rmct",
        scalar_field.astype(jnp.bfloat16),
        legendre,
        preferred_element_type=jnp.float32,
    ).astype(jnp.bfloat16)
    flow_lat = jnp.einsum(
        "rmcj,mjt->rmct",
        radial_flow.astype(jnp.bfloat16),
        legendre,
        preferred_element_type=jnp.float32,
    ).astype(jnp.bfloat16)
    field_piece = lax.all_to_all(field_lat, MODE, split_axis=0, concat_axis=1, tiled=True)
    flow_piece = lax.all_to_all(flow_lat, MODE, split_axis=0, concat_axis=1, tiled=True)
    field_grid = jnp.einsum(
        "rmct,mcp->rtp", field_piece, synth_table, preferred_element_type=jnp.float32
    )
    flow_grid = jnp.einsum(
        "rmct,mcp->rtp", flow_piece, synth_table, preferred_element_type=jnp.float32
    )
    product = (field_grid * flow_grid).astype(jnp.bfloat16)
    modes_grid = jnp.einsum(
        "rtp,mcp->rmct", product, analysis_table, preferred_element_type=jnp.float32
    ).astype(jnp.bfloat16)
    spectral_back = two_step_exchange(modes_grid, ("mode_0", "mode_1"), (0, 1), 1, 0)
    forcing = jnp.einsum(
        "rmct,mjt->rmcj", spectral_back, legendre, preferred_element_type=jnp.float32
    )
    right_side = scalar_field + forcing
    radial_index = lax.axis_index(RADIAL)
    nr_total = shells * lax.axis_size(RADIAL)
    offset = nr_total * 7 // 13
    order_ids = (jnp.arange(ord_dev, dtype=jnp.int32) + lax.axis_index(MODE) * ord_dev).astype(
        jnp.float32
    )
    degree = order_ids[:, None] + jnp.arange(degrees, dtype=jnp.float32)[None, :]
    angular = degree * (degree + 1.0)
    global_shells = radial_index * shells + jnp.arange(shells, dtype=jnp.int32)

    def coefficients(kappa_shell, shell_index):
        lower = jnp.where(shell_index > 0, -kappa_shell, 0.0)
        upper = jnp.where(shell_index < nr_total - 1, -kappa_shell, 0.0)
        radius = (offset + shell_index).astype(jnp.float32)
        diagonal = 1.0 + 2.0 * kappa_shell + kappa_shell * angular / (radius * radius)
        return (lower, upper, diagonal)

    identity = jnp.broadcast_to(
        jnp.eye(4, dtype=jnp.float32)[:, :, None, None], (4, 4, ord_dev, degrees)
    )

    def compose(composite, inputs):
        kappa_shell, source, shell_index = inputs
        lower, upper, diagonal = coefficients(kappa_shell, shell_index)
        new_rows = jnp.stack(
            [
                upper * composite[3],
                -lower * composite[1] + source[:, 0, :] * composite[3],
                -lower * composite[2] + source[:, 1, :] * composite[3],
                -lower * composite[0] + diagonal * composite[3],
            ]
        )
        return (normalized(new_rows), None)

    transfer, _ = lax.scan(compose, identity, (diffusivity, right_side, global_shells))
    prefix = entering(transfer, RADIAL, combine_maps, identity)
    incoming = prefix[:, 3]
    ratio_start = incoming[0] / incoming[3]
    value_start = jnp.stack([incoming[1], incoming[2]], axis=1) / incoming[3][:, None, :]

    def sweep(carry, inputs):
        ratio_prev, value_prev = carry
        kappa_shell, source, shell_index = inputs
        lower, upper, diagonal = coefficients(kappa_shell, shell_index)
        pivot = diagonal - lower * ratio_prev
        ratio_now = upper / pivot
        value_now = (source - lower * value_prev) / pivot[:, None, :]
        return ((ratio_now, value_now), (ratio_now, value_now))

    _, (ratios, values) = lax.scan(
        sweep, (ratio_start, value_start), (diffusivity, right_side, global_shells)
    )

    def back_compose(carry, inputs):
        alpha, slope = carry
        ratio_now, value_now = inputs
        alpha = value_now - ratio_now[:, None, :] * alpha
        slope = -ratio_now * slope
        return ((alpha, slope), (alpha, slope))

    blank_value = jnp.zeros((ord_dev, halves, degrees), jnp.float32)
    unity = jnp.ones((ord_dev, degrees), jnp.float32)
    (alpha_dev, slope_dev), (alpha_all, slope_all) = lax.scan(
        back_compose, (blank_value, unity), (ratios, values), reverse=True
    )
    beyond, _ = entering_2((alpha_dev, slope_dev), RADIAL, combine_affine, (blank_value, unity))
    return alpha_all + slope_all[:, :, None, :] * beyond[None]


def solution(mesh):
    finer = Mesh(mesh.devices.reshape(4, 4, 4, 2), ("radial_0", "radial_1", "mode_0", "mode_1"))
    return jax.shard_map(
        on_device,
        mesh=finer,
        in_specs=(
            P(RADIAL, MODE, None, None),
            P(RADIAL, MODE, None, None),
            P(MODE, None, None),
            P(RADIAL),
        ),
        out_specs=P(RADIAL, MODE, None, None),
        check_vma=False,
    )
```

profile of v0, /device:TPU:0, one launch (start us, length us, event | category | flops | bytes accessed | tf_op | source)
XLA Modules:
  0.0 656.7 jit_solution(9363164226504477464)
XLA Ops:
  6.5 2.0 convert_element_type.84
  8.5 5.2 fusion.40
  13.7 2.8 copy.52
  16.5 5.5 all-to-all-start
  22.5 5.2 fusion.37
  27.8 2.8 copy.57
  30.5 13.0 %all-to-all-done = bf16[32,16,2,768]{3,2,1,0:T(2,128)(2,1)S(1)} async-done(((bf16[32,16,2,768]{3,2,1,0:T(2,128)(2,1)}), bf16[32,16,2,768]{3,2,1,0:T(2,128)(2,1)S(1)}, u32[]{:S(2)}, u32[]{:S(2)}) %all-to-all-start) | async-done | bytes 1572896 | tf_op jit(solution)/shard_map/all_to_all | solution.py:129
  43.6 3.8 all-to-all-start.1
  47.3 4.4 sine_negate_fusion
  52.2 16.5 %all-to-all-done.1 = bf16[32,16,2,768]{3,2,1,0:T(2,128)(2,1)S(1)} async-done(((bf16[32,16,2,768]{3,2,1,0:T(2,128)(2,1)}), bf16[32,16,2,768]{3,2,1,0:T(2,128)(2,1)S(1)}, u32[]{:S(2)}, u32[]{:S(2)}) %all-to-all-start.1) | async-done | bytes 1572896 | tf_op jit(solution)/shard_map/all_to_all | solution.py:130
  69.0 1.3 copy.59
  70.9 8.1 %fusion.50 = f32[4,768,1536,1]{2,1,3,0:T(8,128)} fusion(bf16[4,128,2,768]{3,1,2,0:T(8,128)(2,1)S(1)} %bitcast.170, f32[128,1,1536]{2,0,1:T(8,128)S(1)} %copy-done.2, f32[128,1,1536]{2,0,1:T(8,128)S(1)} %copy-done.3), kind=kOutput, calls=%fused_computation.71 | convolution fusion | flops 2417098752 | bytes 22020096 | tf_op jit(solution)/shard_map/rmct,mcp->rtp/dot_general | solution.py:131
  79.0 9.5 %fusion.32 = bf16[128,2,4,768]{3,0,2,1:T(8,128)(2,1)S(1)} fusion(f32[4,768,1536,1]{2,1,3,0:T(8,128)} %fusion.50, bf16[4,128,2,768]{3,1,2,0:T(8,128)(2,1)} %bitcast.172, f32[128,1,1536]{2,0,1:T(8,128)S(1)} %copy-done.2, f32[128,1,1536]{2,0,1:T(8,128)S(1)} %copy-done.3), kind=kOutput, calls=%fused_computation.48 | convolution fusion | flops 4844421120 | bytes 23592960 | tf_op jit(solution)/shard_map/rtp,mcp->rmct/dot_general | solution.py:138
  88.5 2.4 copy.62
  90.9 3.6 all-to-all-start.2
  94.5 20.7 %all-to-all-done.2 = bf16[4,2,4,16,2,768]{5,2,1,4,3,0:T(4,128)(2,1)S(1)} async-done(((bf16[4,2,4,16,2,768]{5,2,1,4,3,0:T(4,128)(2,1)}), bf16[4,2,4,16,2,768]{5,2,1,4,3,0:T(4,128)(2,1)S(1)}, u32[]{:S(2)}, u32[]{:S(2)}) %all-to-all-start.2) | async-done | bytes 1572896 | tf_op jit(solution)/shard_map/all_to_all | solution.py:29
  116.0 5.0 all_to_all.56
  121.7 1.3 reshape_reshape.3
  123.7 7.2 %bitcast_add_fusion = f32[32,16,2,384]{3,0,2,1:T(8,128)S(1)} fusion(f32[32,16,2,384]{3,2,1,0:T(2,128)S(1)} %copy-done.1, bf16[32,16,2,768]{3,0,2,1:T(8,128)(2,1)} %reshape_reshape.3, bf16[16,384,768]{2,1,0:T(8,128)(2,1)} %param.12), kind=kOutput, calls=%fused_computation.50 | convolution fusion | flops 604372992 | bytes 14155776 | tf_op jit(solution)/shard_map/rmct,mjt->rmcj/dot_general | solution.py:142
  131.0 179.1 %while.49 = (s32[]{:T(128)}, f32[4,4,16,384]{3,2,1,0:T(8,128)S(1)}, s32[32]{0:T(128)S(1)}, f32[32]{0:T(128)S(1)}, f32[32,16,2,384]{3,0,2,1:T(8,128)S(1)}, /*inde...) while((s32[]{:T(128)}, f32[4,4,16,384]{3,2,1,0:T(8,128)S(1)}, ...), condition=%wide.region_2.3_spmd.clone, body=%wide.region_0.2_spmd.clone.sunk | while | flops 1161229 | bytes 2408801 | solution.py:180
  311.2 25.9 %all-gather.6.cloned.1.call-done = f32[16,4,16,384]{3,2,1,0:T(8,128)} async-done(((f32[4,4,16,384]{3,2,1,0:T(8,128)}), f32[16,4,16,384]{3,2,1,0:T(8,128)}) %all-gather.6.cloned.1.call-update) | async-done | bytes 1572880 | tf_op jit(solution)/shard_map/all_gather | solution.py:48
  337.1 1.5 fusion.76
  340.3 0.9 select_select_fusion.1
  341.2 25.7 %all-gather.4.cloned.1.call-done = f32[4,4,4,16,384]{4,3,2,1,0:T(8,128)} async-done(((f32[1,4,4,16,384]{4,3,2,1,0:T(8,128)}), f32[4,4,4,16,384]{4,3,2,1,0:T(8,128)}) %all-gather.4.cloned.1.call-update) | async-done | bytes 1572880 | tf_op jit(solution)/shard_map/all_gather | solution.py:48
  366.9 1.5 slice_bitcast_fusion.5
  369.9 1.9 broadcast.234.clone
  371.8 187.1 %while.50 = (s32[]{:T(128)}, f32[16,384]{1,0:T(8,128)S(1)}, f32[16,2,384]{2,1,0:T(2,128)S(1)}, f32[32,16,384]{2,1,0:T(8,128)S(1)}, f32[32,16,2,384]{3,2,1,0:T(2,...) while((s32[]{:T(128)}, f32[16,384]{1,0:T(8,128)S(1)}, ...), condition=%wide.region_24.25_spmd.clone, body=%wide.region_23.24_spmd.clone.sunk | while | flops 92172 | bytes 419129 | solution.py:195
  559.0 0.9 copy-done.7
  560.6 52.2 %while.51 = (s32[]{:T(128)}, f32[16,2,384]{2,1,0:T(2,128)S(1)}, f32[16,384]{1,0:T(8,128)S(1)}, f32[32,16,2,384]{3,2,1,0:T(2,128)S(1)}, f32[32,16,384]{2,1,0:T(8,...) while((s32[]{:T(128)}, f32[16,2,384]{2,1,0:T(2,128)S(1)}, ...), condition=%wide.region_26.27_spmd.clone, body=%wide.region_25.26_spmd.clone.sunk | while | flops 55300 | bytes 344196 | solution.py:208
  561.4 0.9 bitcast_dynamic-update-slice_fusion.11
  563.0 0.9 bitcast_dynamic-update-slice_fusion.11
  564.6 0.9 bitcast_dynamic-update-slice_fusion.11
  566.3 0.9 bitcast_dynamic-update-slice_fusion.11
  567.9 0.9 bitcast_dynamic-update-slice_fusion.11
  569.5 0.9 bitcast_dynamic-update-slice_fusion.11
  571.1 0.9 bitcast_dynamic-update-slice_fusion.11
  572.8 0.9 bitcast_dynamic-update-slice_fusion.11
  574.4 0.9 bitcast_dynamic-update-slice_fusion.11
  576.0 0.9 bitcast_dynamic-update-slice_fusion.11
  577.7 0.9 bitcast_dynamic-update-slice_fusion.11
  579.3 0.9 bitcast_dynamic-update-slice_fusion.11
  580.9 0.9 bitcast_dynamic-update-slice_fusion.11
  582.6 0.9 bitcast_dynamic-update-slice_fusion.11
  584.2 0.9 bitcast_dynamic-update-slice_fusion.11
  585.8 0.9 bitcast_dynamic-update-slice_fusion.11
  587.5 0.9 bitcast_dynamic-update-slice_fusion.11
  589.1 0.9 bitcast_dynamic-update-slice_fusion.11
  590.7 0.9 bitcast_dynamic-update-slice_fusion.11
  592.4 0.9 bitcast_dynamic-update-slice_fusion.11
  594.0 0.9 bitcast_dynamic-update-slice_fusion.11
  595.6 0.9 bitcast_dynamic-update-slice_fusion.11
  597.2 0.9 bitcast_dynamic-update-slice_fusion.11
  600.5 0.9 bitcast_dynamic-update-slice_fusion.11
  602.1 0.9 bitcast_dynamic-update-slice_fusion.11
  605.4 0.9 bitcast_dynamic-update-slice_fusion.11
  607.0 0.9 bitcast_dynamic-update-slice_fusion.11
  610.3 0.9 bitcast_dynamic-update-slice_fusion.11
  613.6 5.6 all-to-all-start.5
  619.2 9.3 %all-to-all-done.5 = f32[16,16,384]{2,1,0:T(8,128)S(1)} async-done(((f32[16,16,384]{2,1,0:T(8,128)}), f32[16,16,384]{2,1,0:T(8,128)S(1)}, u32[]{:S(2)}, u32[]{:S(2)}) %all-to-all-start.5) | async-done | bytes 393248 | tf_op jit(solution)/shard_map/all_to_all | solution.py:60
  628.6 1.2 broadcast_in_dim.69
  629.8 3.7 all-to-all-start.4
  633.5 1.1 broadcast_select_fusion.1
  636.0 10.1 %all-to-all-done.4 = f32[16,16,2,384]{3,2,1,0:T(2,128)S(1)} async-done(((f32[16,16,2,384]{3,2,1,0:T(2,128)}), f32[16,16,2,384]{3,2,1,0:T(2,128)S(1)}, u32[]{:S(2)}, u32[]{:S(2)}) %all-to-all-start.4) | async-done | bytes 786464 | tf_op jit(solution)/shard_map/all_to_all | solution.py:60
  647.7 2.1 multiply_add_fusion.3
  (571 shorter events, 194.3 us)
Async XLA Ops:
  16.5 5.5 copy-start.4
  16.5 27.1 %all-to-all-start = ((bf16[32,16,2,768]{3,2,1,0:T(2,128)(2,1)}), bf16[32,16,2,768]{3,2,1,0:T(2,128)(2,1)S(1)}, u32[]{:S(2)}, u32[]{:S(2)}) async-start(bf16[32,16,2,768]{3,2,1,0:T(2,128)(2,1)} %copy.52), calls=%async_computation | async-start | bytes 3145728 | tf_op jit(solution)/shard_map/all_to_all | solution.py:129
  43.6 25.1 %all-to-all-start.1 = ((bf16[32,16,2,768]{3,2,1,0:T(2,128)(2,1)}), bf16[32,16,2,768]{3,2,1,0:T(2,128)(2,1)S(1)}, u32[]{:S(2)}, u32[]{:S(2)}) async-start(bf16[32,16,2,768]{3,2,1,0:T(2,128)(2,1)} %copy.57), calls=%async_computation.1 | async-start | bytes 3145728 | tf_op jit(solution)/shard_map/all_to_all | solution.py:130
  69.0 1.3 copy-start.2
  69.0 1.9 copy-start.3
  90.9 24.3 %all-to-all-start.2 = ((bf16[4,2,4,16,2,768]{5,2,1,4,3,0:T(4,128)(2,1)}), bf16[4,2,4,16,2,768]{5,2,1,4,3,0:T(4,128)(2,1)S(1)}, u32[]{:S(2)}, u32[]{:S(2)}) async-start(bf16[4,2,4,16,2,768]{5,2,1,4,3,0:T(4,128)(2,1)} %copy.62), calls=%async_computation.2 | async-start | bytes 3145728 | tf_op jit(solution)/shard_map/all_to_all | solution.py:29
  94.4 242.7 %all-gather.6.cloned.1.call-start = ((), (), s32[]{:S(2)}) async-start(), calls=%async_computation.7 | async-start | bytes 1966080 | tf_op jit(solution)/shard_map/all_gather | solution.py:48
  121.7 2.0 copy-start.1
  123.7 7.3 %copy-start.10 = (f32[32]{0:T(128)S(1)}, f32[32]{0:T(128)}, u32[]{:S(2)}) copy-start(f32[32]{0:T(128)} %param.13) | copy-start | bytes 388
  310.1 0.7 copy-start
  310.9 56.0 %all-gather.4.cloned.1.call-start = ((), (), s32[]{:S(2)}) async-start(), calls=%async_computation.6 | async-start | bytes 1966080 | tf_op jit(solution)/shard_map/all_gather | solution.py:48
  341.2 27.2 %copy-start.6 = (f32[4,4,16,384]{3,2,1,0:T(8,128)S(1)}, f32[4,4,16,384]{3,2,1,0:T(8,128)}, u32[]{:S(2)}) copy-start(f32[4,4,16,384]{3,2,1,0:T(8,128)} %select_select_fusion.1) | copy-start | bytes 1179652
  559.0 0.9 copy-start.7
  613.6 15.0 %all-to-all-start.5 = ((f32[16,16,384]{2,1,0:T(8,128)}), f32[16,16,384]{2,1,0:T(8,128)S(1)}, u32[]{:S(2)}, u32[]{:S(2)}) async-start(f32[16,16,384]{2,1,0:T(8,128)} %broadcast_in_dim.116), calls=%async_computation.5 | async-start | bytes 786432 | tf_op jit(solution)/shard_map/all_to_all | solution.py:60
  628.6 1.2 copy-start.5
  629.8 16.4 %all-to-all-start.4 = ((f32[16,16,2,384]{3,2,1,0:T(2,128)}), f32[16,16,2,384]{3,2,1,0:T(2,128)S(1)}, u32[]{:S(2)}, u32[]{:S(2)}) async-start(f32[16,16,2,384]{3,2,1,0:T(2,128)} %broadcast_in_dim.69), calls=%async_computation.4 | async-start | bytes 1572864 | tf_op jit(solution)/shard_map/all_to_all | solution.py:60
  636.0 10.9 %copy-start.8 = (f32[8,16,384]{2,1,0:T(8,128)S(1)}, f32[8,16,384]{2,1,0:T(8,128)}, u32[]{:S(2)}) copy-start(f32[8,16,384]{2,1,0:T(8,128)} %slice.142) | copy-start | bytes 589828
  646.6 0.9 copy-start.9
Sparse Core Ops, SparseCore 0:
  311.0 26.0 all-gather.5
  340.3 26.5 all-gather.3
where the time goes:
time: 665 us; the launch traced here: 657 us
  loops' own time  213 us (32%)
  other arithmetic  138 us (21%)
  waiting for transfers between devices  121 us (18%)
  local copies, waits for them, and re-layouts  108 us (16%)
  matrix products  35.2 us (5%)
  starting transfers between devices  22.5 us (3%)
  between operations  14 us (2%)
    another operation x1, loops' own time, on_device(): lax.scan(compose, identity, (diffusivity, right_side, global_shells))  109 us
    another operation x1, loops' own time, on_device(): lax.scan(sweep, (ratio_start, value_start), (diffusivity, right_side, glo...  103 us
    dynamic_update_slice x128, other arithmetic, on_device(): lax.scan(sweep, (ratio_start, value_start), (diffusivity, right_side, glo...  94 us
    dynamic_slice x224, local copies, waits for them, and re-layouts, on_device(): lax.scan(compose, identity, (diffusivity, right_side, global_shells))  83.5 us
    all_gather x2, waiting for transfers between devices, entering(): pieces = lax.all_gather(total, axis)  51.6 us
    add x32, other arithmetic, coefficients(): 1.0 + 2.0 * kappa_shell + kappa_shell * angular / (radius * radius)  24.5 us
    all_to_all x1, waiting for transfers between devices, turned_blocks(): lax.all_to_all(parts, axes[k], split_axis=k, concat_axis=k, tiled=True)  20.7 us
    all_to_all x2, waiting for transfers between devices, sent_to_all(): lax.all_to_all(jnp.broadcast_to(array[None], (devices, *array.shape)), ax...  19.5 us
  transfers between devices with their start and end apart: 7, of which 7 were waited for; matrix products, arithmetic and copies ran while one was open for 3% of the time, Pallas kernels for 0%

commit v1 on v0

v1 whole, which is shorter than its diff:
```python
import functools
import math

import jax
import jax.numpy as jnp
import ml_dtypes
import numpy as np
from jax import lax
from jax.experimental import pallas as pl
from jax.experimental.pallas import tpu as pltpu
from jax.sharding import Mesh
from jax.sharding import PartitionSpec as P

F32, BF16 = jnp.float32, jnp.bfloat16
MODE = ("mode_0", "mode_1")
RADIAL = ("radial_0", "radial_1")
NLON = 1536
POINTS = 384
LANES = 128
SHELLS, ORD, HALVES, DEG, NLAT = 32, 16, 2, 384, 768
TILES = DEG // LANES
ROWS = ORD * TILES * HALVES
LAT_TILES = NLAT // LANES
NMODE = 8
NSHELL = SHELLS // NMODE
PAIRS = ORD * HALVES
VMEM_LIMIT = 56 * 2**20


def params():
    return pltpu.CompilerParams(vmem_limit_bytes=VMEM_LIMIT)


def cost(flops, nbytes):
    return pl.CostEstimate(flops=flops, bytes_accessed=nbytes, transcendentals=0)


def whole(space=pltpu.VMEM):
    return pl.BlockSpec(memory_space=space)


def fixed(shape):
    return pl.BlockSpec(shape, lambda *_: (0,) * len(shape))


def longitude_tables(orders):
    step = NLON // POINTS
    points = np.arange(POINTS) * step
    phase = (np.arange(orders)[:, None] * points[None, :]) % NLON
    angle = phase * (2.0 * math.pi / NLON)
    paired = np.stack([np.cos(angle), -np.sin(angle)], axis=1).reshape(2 * orders, POINTS)
    synth = (paired / math.sqrt(orders)).astype(np.float32).astype(ml_dtypes.bfloat16)
    analysis = (paired * math.sqrt(2.0 / NLON)).astype(np.float32).astype(ml_dtypes.bfloat16)
    return synth.T.copy(), (analysis.astype(np.float32) * step).astype(ml_dtypes.bfloat16)


def to_rows(array):
    array = array.reshape(SHELLS, ORD, HALVES, TILES, LANES).transpose(0, 1, 3, 2, 4)
    return array.reshape(SHELLS * ROWS, LANES)


def from_rows(rows):
    rows = rows.reshape(SHELLS, ORD, TILES, HALVES, LANES).transpose(0, 1, 3, 2, 4)
    return rows.reshape(SHELLS, ORD, HALVES, DEG)


def row_of(order, tile, half):
    return (order * TILES + tile) * HALVES + half


SYNTH_ORDERS = 2


def synthesis_kernel(field, flow, legendre, out, held):
    step = pl.program_id(0)
    for k in range(SYNTH_ORDERS):
        order = step * SYNTH_ORDERS + k
        rows = []
        for source in (field, flow):
            for half in range(HALVES):
                parts = [
                    source[pl.ds(row_of(order, tile, half), SHELLS, stride=ROWS), :]
                    for tile in range(TILES)
                ]
                rows.append(jnp.concatenate(parts, axis=1))
        spectral = jnp.concatenate(rows, axis=0).astype(BF16)
        lat = jnp.dot(spectral, legendre[k], preferred_element_type=F32)
        for f in range(2):
            for half in range(HALVES):
                top = (f * HALVES + half) * SHELLS
                for tile in range(LAT_TILES):
                    held[
                        tile,
                        pl.ds(f * SHELLS * PAIRS + order * HALVES + half, SHELLS, stride=PAIRS),
                        :,
                    ] = lat[top : top + SHELLS, tile * LANES : (tile + 1) * LANES]

    @pl.when(step == ORD // SYNTH_ORDERS - 1)
    def _():
        for f in range(2):
            for dest in range(NMODE):
                for s in range(NSHELL):
                    top = (f * SHELLS + dest * NSHELL + s) * PAIRS
                    for tile in range(LAT_TILES):
                        out[dest, f, s, :, tile * LANES : (tile + 1) * LANES] = held[
                            tile, top : top + PAIRS, :
                        ].astype(BF16)


def synthesis(field_rows, flow_rows, legendre):
    shape = (NMODE, 2, NSHELL, PAIRS, NLAT)
    return pl.pallas_call(
        synthesis_kernel,
        out_shape=jax.ShapeDtypeStruct(shape, BF16),
        grid=(ORD // SYNTH_ORDERS,),
        in_specs=[
            fixed((SHELLS * ROWS, LANES)),
            fixed((SHELLS * ROWS, LANES)),
            pl.BlockSpec((SYNTH_ORDERS, DEG, NLAT), lambda i: (i, 0, 0)),
        ],
        out_specs=fixed(shape),
        scratch_shapes=[pltpu.VMEM((LAT_TILES, 2 * SHELLS * PAIRS, LANES), F32)],
        compiler_params=params(),
        cost_estimate=cost(2 * 128 * DEG * NLAT * ORD, 16_000_000),
        name="synthesis",
    )(field_rows, flow_rows, legendre)


def grid_kernel(synth, analysis, lat, out):
    field = jnp.dot(synth[...], lat[:, 0, 0].reshape(NMODE * PAIRS, NLAT), preferred_element_type=F32)
    flow = jnp.dot(synth[...], lat[:, 1, 0].reshape(NMODE * PAIRS, NLAT), preferred_element_type=F32)
    product = (field * flow).astype(BF16)
    modes = jnp.dot(analysis[...], product, preferred_element_type=F32).astype(BF16)
    out[:, 0] = modes.reshape(NMODE, PAIRS, NLAT)


def grid_product(synth, analysis, lat):
    return pl.pallas_call(
        grid_kernel,
        out_shape=jax.ShapeDtypeStruct((NMODE, NSHELL, PAIRS, NLAT), BF16),
        grid=(NSHELL,),
        in_specs=[
            fixed(synth.shape),
            fixed(analysis.shape),
            pl.BlockSpec((NMODE, 2, 1, PAIRS, NLAT), lambda i: (0, 0, i, 0, 0)),
        ],
        out_specs=pl.BlockSpec((NMODE, 1, PAIRS, NLAT), lambda i: (0, i, 0, 0)),
        compiler_params=params(),
        cost_estimate=cost(3 * 2 * POINTS * 256 * NLAT * NSHELL, 5_000_000),
        name="grid_product",
    )(synth, analysis, lat)


def block_matrix_kernel(shell, angular, pivots, left, right, ends):
    ang = angular[...]
    ratio = jnp.zeros((ROWS, LANES), F32)
    answer = jnp.ones((ROWS, LANES), F32)
    ratios = []
    for i in range(SHELLS):
        kappa, low, up, radius2 = shell[0, i], shell[1, i], shell[2, i], shell[3, i]
        diagonal = 1.0 + 2.0 * kappa + kappa * ang / radius2
        inverse = 1.0 / (diagonal - low * ratio)
        ratio = up * inverse
        answer = low * inverse * answer
        pivots[i] = inverse
        left[i] = answer
    before = left[SHELLS - 1]
    behind = ratio
    right[SHELLS - 1] = behind
    ends[2] = before
    ends[3] = behind
    for i in reversed(range(SHELLS - 1)):
        ratio = shell[2, i] * pivots[i]
        before = left[i] + ratio * before
        behind = ratio * behind
        left[i] = before
        right[i] = behind
    ends[0] = before
    ends[1] = behind


def block_matrix(shell, angular):
    big = jax.ShapeDtypeStruct((SHELLS, ROWS, LANES), F32)
    return pl.pallas_call(
        block_matrix_kernel,
        out_shape=(big, big, big, jax.ShapeDtypeStruct((4, ROWS, LANES), F32)),
        in_specs=[whole(pltpu.SMEM), whole()],
        out_specs=(whole(),) * 4,
        compiler_params=params(),
        cost_estimate=cost(10_000_000, 6_000_000),
        name="block_matrix",
    )(shell, angular)


CHAIN = 4


def chain_matrix(blocks):
    links = []
    beta = None
    for first_left, first_right, last_left, last_right in blocks:
        if beta is None:
            den = jnp.ones_like(first_left)
            beta = jnp.zeros_like(first_left)
        else:
            den = 1.0 / (1.0 - first_left * beta)
        extra = last_left * beta * den
        links.append(
            (den, den * first_left, den * first_right, extra, last_left * den, beta)
        )
        beta = last_right + extra * first_right
    alpha = None
    alphas = []
    for link in links:
        alphas.append(alpha)
        alpha = link[4] if alpha is None else link[4] * alpha
    before = None
    behind = None
    for link, start in zip(reversed(links), reversed(alphas)):
        own = link[1] if start is None else link[1] * start
        before = own if before is None else own + link[2] * before
        behind = link[2] if behind is None else link[2] * behind
    return links, (before, behind, alpha, beta)


def level_kernel(place, ends, inner, outer, held):
    supers = []
    for x in range(CHAIN):
        links, own = chain_matrix(
            [tuple(ends[x * CHAIN + k, n] for n in range(4)) for k in range(CHAIN)]
        )
        supers.append(own)
        for k in range(CHAIN):
            for n in range(6):
                held[x, k, n] = links[k][n]
    links, _ = chain_matrix(supers)
    for k in range(CHAIN):
        for n in range(6):
            outer[k, n] = links[k][n]
    inner[...] = held[place[0]]


def levels(place, ends):
    rows = 8
    shape = jax.ShapeDtypeStruct((CHAIN, 6, ROWS, LANES), F32)
    spec = pl.BlockSpec((CHAIN, 6, rows, LANES), lambda i: (0, 0, i, 0))
    return pl.pallas_call(
        level_kernel,
        out_shape=(shape, shape),
        grid=(ROWS // rows,),
        in_specs=[
            whole(pltpu.SMEM),
            pl.BlockSpec((CHAIN * CHAIN, 4, rows, LANES), lambda i: (0, 0, i, 0)),
        ],
        out_specs=(spec, spec),
        scratch_shapes=[pltpu.VMEM((CHAIN, CHAIN, 6, rows, LANES), F32)],
        compiler_params=params(),
        cost_estimate=cost(10_000_000, 8_000_000),
        name="levels",
    )(place, ends)


FORCING_ORDERS = 2


def forcing_kernel(shell, modes, legendre, field, pivots, solved, ends, held):
    step = pl.program_id(0)

    @pl.when(step == 0)
    def _():
        for s in range(SHELLS):
            for tile in range(LAT_TILES):
                held[tile, s * PAIRS : (s + 1) * PAIRS, :] = modes[
                    s // NSHELL, s % NSHELL, :, tile * LANES : (tile + 1) * LANES
                ].astype(F32)

    for k in range(FORCING_ORDERS):
        order = step * FORCING_ORDERS + k
        rows = []
        for half in range(HALVES):
            parts = [
                held[tile, pl.ds(order * HALVES + half, SHELLS, stride=PAIRS), :]
                for tile in range(LAT_TILES)
            ]
            rows.append(jnp.concatenate(parts, axis=1))
        lat = jnp.concatenate(rows, axis=0).astype(BF16)
        forcing = lax.dot_general(
            lat, legendre[k], (((1,), (1,)), ((), ())), preferred_element_type=F32
        )
        for half in range(HALVES):
            for tile in range(TILES):
                place = pl.ds(row_of(order, tile, half), SHELLS, stride=ROWS)
                solved[place, :] = (
                    field[place, :]
                    + forcing[
                        half * SHELLS : (half + 1) * SHELLS, tile * LANES : (tile + 1) * LANES
                    ]
                )

    @pl.when(step == ORD // FORCING_ORDERS - 1)
    def _():
        value = solved[0:ROWS, :] * pivots[0]
        solved[0:ROWS, :] = value
        for i in range(1, SHELLS):
            here = slice(i * ROWS, (i + 1) * ROWS)
            value = (solved[here, :] + shell[1, i] * value) * pivots[i]
            solved[here, :] = value
        ends[1] = value
        for i in reversed(range(SHELLS - 1)):
            here = slice(i * ROWS, (i + 1) * ROWS)
            value = solved[here, :] + (shell[2, i] * pivots[i]) * value
            solved[here, :] = value
        ends[0] = value


def forcing_solve(shell, modes, legendre, field_rows, pivots):
    return pl.pallas_call(
        forcing_kernel,
        out_shape=(
            jax.ShapeDtypeStruct((SHELLS * ROWS, LANES), F32),
            jax.ShapeDtypeStruct((2, ROWS, LANES), F32),
        ),
        grid=(ORD // FORCING_ORDERS,),
        in_specs=[
            whole(pltpu.SMEM),
            fixed((NMODE, NSHELL, PAIRS, NLAT)),
            pl.BlockSpec((FORCING_ORDERS, DEG, NLAT), lambda i: (i, 0, 0)),
            fixed((SHELLS * ROWS, LANES)),
            fixed((SHELLS, ROWS, LANES)),
        ],
        out_specs=(fixed((SHELLS * ROWS, LANES)), fixed((2, ROWS, LANES))),
        scratch_shapes=[pltpu.VMEM((LAT_TILES, SHELLS * PAIRS, LANES), F32)],
        compiler_params=params(),
        cost_estimate=cost(2 * 64 * DEG * NLAT * ORD, 16_000_000),
        name="forcing_solve",
    )(shell, modes, legendre, field_rows, pivots)


def chain_values(links, values, first, last):
    alphas = [first]
    for k in range(CHAIN):
        first_value, last_value = values[k]
        alpha = last_value + links(k, 3) * first_value
        if alphas[-1] is not None:
            alpha = alpha + links(k, 4) * alphas[-1]
        alphas.append(alpha)
    firsts = [None] * CHAIN + [last]
    for k in reversed(range(CHAIN)):
        value = links(k, 0) * values[k][0]
        if alphas[k] is not None:
            value = value + links(k, 1) * alphas[k]
        if firsts[k + 1] is not None:
            value = value + links(k, 2) * firsts[k + 1]
        firsts[k] = value
    return alphas, firsts


def boundary_values(links, alphas, firsts, shape):
    zero = jnp.zeros(shape, F32)
    pairs = []
    for k in range(CHAIN):
        before = zero if alphas[k] is None else alphas[k] + links(k, 5) * firsts[k]
        behind = zero if firsts[k + 1] is None else firsts[k + 1]
        pairs.append((before, behind))
    return pairs


def put_in_order(position, slots, held):
    for s, slot in enumerate(slots):
        held[lax.rem(position + CHAIN - s, CHAIN)] = slot[...]


def inner_kernel(place, links, a, b, c, d, out, held):
    put_in_order(place[1], (a, b, c, d), held)
    values = [(held[k, 0], held[k, 1]) for k in range(CHAIN)]
    alphas, firsts = chain_values(lambda k, n: links[k, n], values, None, None)
    out[0] = firsts[0]
    out[1] = alphas[CHAIN]


def inner_join(place, links, slots):
    return pl.pallas_call(
        inner_kernel,
        out_shape=jax.ShapeDtypeStruct((2, ROWS, LANES), F32),
        in_specs=[whole(pltpu.SMEM)] + [whole()] * 5,
        out_specs=whole(),
        scratch_shapes=[pltpu.VMEM((CHAIN, 2, ROWS, LANES), F32)],
        compiler_params=params(),
        cost_estimate=cost(1_000_000, 2_000_000),
        name="inner_join",
    )(place, links, *slots)


FINAL_SHELLS = 8


def final_kernel(place, inner, outer, a, b, c, d, e, f, g, h, solved, left, right, out, held, pairs, edge):
    @pl.when(pl.program_id(0) == 0)
    def _():
        shape = (ROWS, LANES)
        put_in_order(place[0], (e, f, g, h), held)
        values = [(held[k, 0], held[k, 1]) for k in range(CHAIN)]
        links = lambda k, n: outer[k, n]
        alphas, firsts = chain_values(links, values, None, None)
        for k, (before, behind) in enumerate(boundary_values(links, alphas, firsts, shape)):
            pairs[k, 0] = before
            pairs[k, 1] = behind
        first, last = pairs[place[0], 0], pairs[place[0], 1]
        put_in_order(place[1], (a, b, c, d), held)
        values = [(held[k, 0], held[k, 1]) for k in range(CHAIN)]
        links = lambda k, n: inner[k, n]
        alphas, firsts = chain_values(links, values, first, last)
        for k, (before, behind) in enumerate(boundary_values(links, alphas, firsts, shape)):
            pairs[k, 0] = before
            pairs[k, 1] = behind
        edge[...] = pairs[place[1]]

    before, behind = edge[0], edge[1]
    for i in range(FINAL_SHELLS):
        here = slice(i * ROWS, (i + 1) * ROWS)
        out[here, :] = solved[here, :] + left[i] * before + right[i] * behind


def final_join(place, inner, outer, slots, super_slots, solved, left, right):
    links = fixed((CHAIN, 6, ROWS, LANES))
    two = fixed((2, ROWS, LANES))
    rows = pl.BlockSpec((FINAL_SHELLS * ROWS, LANES), lambda i: (i, 0))
    answer = pl.BlockSpec((FINAL_SHELLS, ROWS, LANES), lambda i: (i, 0, 0))
    return pl.pallas_call(
        final_kernel,
        out_shape=jax.ShapeDtypeStruct((SHELLS * ROWS, LANES), F32),
        grid=(SHELLS // FINAL_SHELLS,),
        in_specs=[whole(pltpu.SMEM), links, links] + [two] * 8 + [rows, answer, answer],
        out_specs=rows,
        scratch_shapes=[
            pltpu.VMEM((CHAIN, 2, ROWS, LANES), F32),
            pltpu.VMEM((CHAIN, 2, ROWS, LANES), F32),
            pltpu.VMEM((2, ROWS, LANES), F32),
        ],
        compiler_params=params(),
        cost_estimate=cost(3_000_000, 9_000_000),
        name="final_join",
    )(place, inner, outer, *slots, *super_slots, solved, left, right)


def ring(array, axis):
    slots = [array]
    for step in range(1, CHAIN):
        pairs = [(i, (i + step) % CHAIN) for i in range(CHAIN)]
        slots.append(lax.ppermute(array, axis, pairs))
    return slots


def exchange(array):
    return lax.all_to_all(array, MODE, 0, 0, tiled=True)


def on_device(scalar_field, radial_flow, legendre, diffusivity):
    synth, analysis = longitude_tables(ORD * NMODE)
    field_rows, flow_rows = to_rows(scalar_field), to_rows(radial_flow)
    lat = exchange(synthesis(field_rows, flow_rows, legendre))

    nr_total = SHELLS * CHAIN * CHAIN
    place = jnp.stack([lax.axis_index(RADIAL[0]), lax.axis_index(RADIAL[1])]).astype(jnp.int32)
    shell_ids = lax.axis_index(RADIAL) * SHELLS + jnp.arange(SHELLS, dtype=jnp.int32)
    radius = (nr_total * 7 // 13 + shell_ids).astype(F32)
    shell = jnp.stack(
        [
            diffusivity,
            jnp.where(shell_ids > 0, diffusivity, 0.0),
            jnp.where(shell_ids < nr_total - 1, diffusivity, 0.0),
            radius * radius,
        ]
    )
    row = np.arange(ROWS)[:, None]
    local_degree = row // (TILES * HALVES) + row // HALVES % TILES * LANES + np.arange(LANES)[None]
    degree = (local_degree + lax.axis_index(MODE) * ORD).astype(F32)
    angular = degree * (degree + 1.0)
    pivots, left, right, ends = block_matrix(shell, angular)
    inner, outer = levels(place, lax.all_gather(ends, RADIAL))

    modes = exchange(grid_product(jnp.asarray(synth), jnp.asarray(analysis), lat))
    solved, own = forcing_solve(shell, modes, legendre, field_rows, pivots)
    slots = ring(own, RADIAL[1])
    super_slots = ring(inner_join(place, inner, slots), RADIAL[0])
    return from_rows(final_join(place, inner, outer, slots, super_slots, solved, left, right))


def solution(mesh):
    finer = Mesh(
        mesh.devices.reshape(4, 4, 4, 2), ("radial_0", "radial_1", "mode_0", "mode_1")
    )
    return jax.shard_map(
        on_device,
        mesh=finer,
        in_specs=(
            P(RADIAL, MODE, None, None),
            P(RADIAL, MODE, None, None),
            P(MODE, None, None),
            P(RADIAL),
        ),
        out_specs=P(RADIAL, MODE, None, None),
        check_vma=False,
    )
```

time: 665 us -> 177 us (0.27); the launches traced: 657 us -> 176 us
  loops' own time: 213 us -> 0 us
  other arithmetic: 138 us -> 3.98 us
  waiting for transfers between devices: 121 us -> 5.7 us
  local copies, waits for them, and re-layouts: 108 us -> 22.1 us
  blocking collectives: 5 us -> 70.5 us
  Pallas kernels: 0 us -> 50.6 us
  matrix products: 35.2 us -> 0 us
  starting transfers between devices: 22.5 us -> 9.14 us
    another operation x3 -> x0, loops' own time: 213 us -> none  [the longest x1 109 us: on_device(): lax.scan(compose, identity, (diffusivity, right_side, global_shells))]
    dynamic_update_slice x128 -> x0, other arithmetic: 94 us -> none  [on_device(): lax.scan(sweep, (ratio_start, value_start), (diffusivity, right_side, glo...]
    dynamic_slice x224 -> x0, local copies, waits for them, and re-layouts: 83.5 us -> none  [on_device(): lax.scan(compose, identity, (diffusivity, right_side, global_shells))]
    all_to_all x5 -> x0, waiting for transfers between devices: 69.6 us -> none  [the longest x1 20.7 us: turned_blocks(): lax.all_to_all(parts, axes[k], split_axis=k, concat_axis=k, tiled=True)]
    all_to_all x1 -> x2, blocking collectives: 5 us -> 70.5 us  [exchange(): return lax.all_to_all(array, MODE, 0, 0, tiled=True)]
    all_gather x2 -> x1, waiting for transfers between devices: 51.6 us -> 0.01 us  [on_device(): inner, outer = levels(place, lax.all_gather(ends, RADIAL))]
    pallas_call x0 -> x7, Pallas kernels: none -> 50.6 us  [the longest x1 13.6 us: synthesis(): pl.pallas_call(synthesis_kernel, out_shape=jax.ShapeDtypeStruct(shape, BF...]
    dot_general x5 -> x0, matrix products: 35.2 us -> none  [the longest x1 9.53 us: on_device(): jnp.einsum('rtp,mcp->rmct', product, analysis_table, preferred_element_ty...]
  transfers between devices with their start and end apart: 7 -> 7, of which waited for: 7 -> 3; matrix products, arithmetic and copies ran while one was open for 3% -> 8% of each run, Pallas kernels for 0% -> 22%
where the time goes in v1:
time: 177 us; the launch traced here: 176 us
  blocking collectives  70.5 us (40%)
  Pallas kernels  50.6 us (29%)
  local copies, waits for them, and re-layouts  22.1 us (12%)
  between operations  13.5 us (8%)
  starting transfers between devices  9.14 us (5%)
  waiting for transfers between devices  5.7 us (3%)
  other arithmetic  3.98 us (2%)
    all_to_all x2, blocking collectives, exchange(): return lax.all_to_all(array, MODE, 0, 0, tiled=True)  70.5 us
    pallas_call x1, Pallas kernels, synthesis(): pl.pallas_call(synthesis_kernel, out_shape=jax.ShapeDtypeStruct(shape, BF...  13.6 us
    pallas_call x1, Pallas kernels, forcing_solve(): pl.pallas_call(forcing_kernel, out_shape=(jax.ShapeDtypeStruct((SHELLS *...  11.8 us
    ppermute x6, starting transfers between devices, ring(): slots.append(lax.ppermute(array, axis, pairs))  9.14 us
    pallas_call x1, Pallas kernels, levels(): pl.pallas_call(level_kernel, out_shape=(shape, shape), grid=(ROWS // rows...  8.09 us
    pallas_call x1, Pallas kernels, grid_product(): pl.pallas_call(grid_kernel, out_shape=jax.ShapeDtypeStruct((NMODE, NSHELL...  5.81 us
    ppermute x6, waiting for transfers between devices, ring(): slots.append(lax.ppermute(array, axis, pairs))  5.68 us
    pallas_call x1, Pallas kernels, final_join(): pl.pallas_call(final_kernel, out_shape=jax.ShapeDtypeStruct((SHELLS * ROW...  5.5 us
  transfers between devices with their start and end apart: 7, of which 3 were waited for; matrix products, arithmetic and copies ran while one was open for 8% of the time, Pallas kernels for 22%

profile of v1, /device:TPU:0, one launch (start us, length us, event | category | flops | bytes accessed | tf_op | source)
XLA Modules:
  0.0 175.5 jit_solution(17906210599559819307)
XLA Ops:
  6.5 0.0 all-gather.3.cloned.1.call-start
  6.5 0.7 fusion
  7.2 1.4 add_multiply_fusion.angular
  8.6 1.3 pad_maximum_fusion.shell
  9.9 3.6 %block_matrix.1 = (f32[32,96,128]{2,1,0:T(8,128)}, f32[32,96,128]{2,1,0:T(8,128)}, f32[32,96,128]{2,1,0:T(8,128)}, f32[4,96,128]{2,1,0:T(8,128)}) custom-call(f32[4,32]{1,0:T(4,128)} %pad_maximum_fusion.shell, f32[96,128]{1,0:T(8,128)} %add_multiply_fusion.angular), custom_call_target="tpu_custom_call" | custom-call | flops 10000000 | bytes 6000000 | tf_op jit(solution)/shard_map/block_matrix/pallas_call | solution.py:184
  13.5 0.0 all-gather.3.cloned.1.call-update
  13.5 2.7 %copy.17 = f32[32,16,2,384]{3,1,2,0:T(8,128)} copy(f32[32,16,2,384]{3,2,1,0:T(2,128)} %param.7) | data formatting | bytes 3145728 | tf_op args[0]
  16.2 2.5 %reshape.34 = f32[32,16,2,3,128]{4,3,1,2,0:T(4,128)S(1)} reshape(f32[32,16,2,384]{3,1,2,0:T(8,128)} %copy.17) | data formatting | bytes 3145728 | tf_op jit(solution)/shard_map/reshape | solution.py:58
  18.7 0.0 copy-start
  18.7 2.4 %copy.18 = f32[32,16,3,2,128]{4,3,2,1,0:T(2,128)} copy(f32[32,16,3,2,128]{4,2,1,3,0:T(4,128)S(1)} %bitcast.28) | data formatting | bytes 3145728 | tf_op jit(solution)/shard_map/transpose | solution.py:58
  21.1 0.0 copy-done
  21.1 1.3 copy.19
  22.4 2.5 %reshape.36 = f32[32,16,2,3,128]{4,3,1,2,0:T(4,128)S(1)} reshape(f32[32,16,2,384]{3,1,2,0:T(8,128)} %copy.19) | data formatting | bytes 3145728 | tf_op jit(solution)/shard_map/reshape | solution.py:58
  24.9 2.4 %copy.20 = f32[32,16,3,2,128]{4,3,2,1,0:T(2,128)} copy(f32[32,16,3,2,128]{4,2,1,3,0:T(4,128)S(1)} %bitcast.29) | data formatting | bytes 3145728 | tf_op jit(solution)/shard_map/transpose | solution.py:58
  27.3 13.6 %synthesis.1 = bf16[8,2,4,32,768]{4,3,2,1,0:T(8,128)(2,1)} custom-call(f32[3072,128]{1,0:T(8,128)} %bitcast.26, f32[3072,128]{1,0:T(8,128)} %bitcast.32, bf16[16,384,768]{2,1,0:T(8,128)(2,1)} %legendre.3), custom_call_target="tpu_custom_call" | custom-call | flops 1207959552 | bytes 16000000 | tf_op jit(solution)/shard_map/synthesis/pallas_call | solution.py:112
  40.9 44.4 %all_to_all.10.lat = bf16[8,2,4,32,768]{4,3,2,1,0:T(8,128)(2,1)} all-to-all(bf16[8,2,4,32,768]{4,3,2,1,0:T(8,128)(2,1)} %synthesis.1), channel_id=1, replica_groups=mesh['radial_0'=4,'radial_1'=4,'mode_0'=4,'mode_1'=2] {'mode_0','mode_1'}, dimensions={0} | all-to-all | bytes 6291456 | tf_op jit(solution)/shard_map/all_to_all | solution.py:455
  85.3 5.8 %grid_product.1 = bf16[8,4,32,768]{3,2,1,0:T(8,128)(2,1)} custom-call(bf16[384,256]{1,0:T(8,128)(2,1)} %constant.40.clone.synth, bf16[256,384]{1,0:T(8,128)(2,1)} %constant.41.clone.analysis, bf16[8,2,4,32,768]{4,3,2,1,0:T(8,128)(2,1)} %all_to_all.10.lat), custom_call_target="tpu_custom_call" | custom-call | flops 1811939328 | bytes 5000000 | tf_op jit(solution)/shard_map/grid_product/pallas_call | solution.py:138
  91.1 26.1 %all_to_all.11.modes = bf16[8,4,32,768]{3,2,1,0:T(8,128)(2,1)} all-to-all(bf16[8,4,32,768]{3,2,1,0:T(8,128)(2,1)} %grid_product.1), channel_id=1, replica_groups=mesh['radial_0'=4,'radial_1'=4,'mode_0'=4,'mode_1'=2] {'mode_0','mode_1'}, dimensions={0} | all-to-all | bytes 3145728 | tf_op jit(solution)/shard_map/all_to_all | solution.py:455
  117.2 11.8 %forcing_solve.1 = (f32[3072,128]{1,0:T(8,128)}, f32[2,96,128]{2,1,0:T(8,128)}) custom-call(f32[4,32]{1,0:T(4,128)} %pad_maximum_fusion.shell, bf16[8,4,32,768]{3,2,1,0:T(8,128)(2,1)} %all_to_all.11.modes, bf16[16,384,768]{2,1,0:T(8,128)(2,1)} %legendre.3, f32[3072,128]{1,0:T(8,128)} %bitcast.27, f32[32,96,128]{2,1,0:T(8,128)} %get-tuple-element.16.pivots), custom_call_target="tpu_custom_call" | custom-call | flops 603979776 | bytes 16000000 | tf_op jit(solution)/shard_map/forcing_solve/pallas_call | solution.py:317
  129.0 3.0 %collective-permute-start.2 = (f32[2,96,128]{2,1,0:T(8,128)}, f32[2,96,128]{2,1,0:T(8,128)S(1)}, u32[]{:S(2)}, u32[]{:S(2)}) collective-permute-start(f32[2,96,128]{2,1,0:T(8,128)} %get-tuple-element.17.a), channel_id=1, source_target_pairs={{0,24},{8,0},{16,8},{24,16},{1,25},{9,1},{17,9},{25,17},{2,26},{10... | collective-permute-start | bytes 294920 | tf_op jit(solution)/shard_map/ppermute | solution.py:450
  132.0 0.6 collective-permute-start.1
  132.7 1.0 collective-permute-start
  133.6 0.6 pad_add_fusion.place
  134.3 0.0 all-gather.3.cloned.1.call-done
  134.3 8.1 %levels.1 = (f32[4,6,96,128]{3,2,1,0:T(8,128)}, f32[4,6,96,128]{3,2,1,0:T(8,128)}) custom-call(s32[2]{0:T(128)} %pad_add_fusion.place, f32[16,4,96,128]{3,2,1,0:T(8,128)} %bitcast.33), custom_call_target="tpu_custom_call" | custom-call | flops 10000000 | bytes 8000000 | tf_op jit(solution)/shard_map/levels/pallas_call | solution.py:247
  142.4 0.0 collective-permute-done.2.d
  142.4 0.0 copy-start.1
  142.4 0.0 collective-permute-done.1.c
  142.4 0.0 copy-start.2
  142.4 0.0 collective-permute-done.b
  142.4 0.0 copy-start.3
  142.4 0.6 copy-done.1
  143.0 0.0 copy-done.2
  143.1 0.0 copy-done.3
  143.1 2.1 %inner_join.1.e = f32[2,96,128]{2,1,0:T(8,128)} custom-call(s32[2]{0:T(128)} %pad_add_fusion.place, f32[4,6,96,128]{3,2,1,0:T(8,128)} %get-tuple-element.14.links.inner, f32[2,96,128]{2,1,0:T(8,128)} %get-tuple-element.17.a, f32[2,96,128]{2,1,0:T(8,128)} %copy-done.3, f32[2,96,128]{2,1,0:T(8,128)} %copy-done.2, f32[2,96,128]{2,1,0:T(8,128)} %copy-done.1), custom_call_target="tpu_custom_call" | custom-call | flops 1000000 | bytes 2000000 | tf_op jit(solution)/shard_map/inner_join/pallas_call | solution.py:382
  145.2 2.8 %collective-permute-start.5 = (f32[2,96,128]{2,1,0:T(8,128)}, f32[2,96,128]{2,1,0:T(8,128)S(1)}, u32[]{:S(2)}, u32[]{:S(2)}) collective-permute-start(f32[2,96,128]{2,1,0:T(8,128)} %inner_join.1.e), channel_id=1, source_target_pairs={{0,96},{32,0},{64,32},{96,64},{1,97},{33,1},{65,33},{97,65},{2,98}... | collective-permute-start | bytes 294920 | tf_op jit(solution)/shard_map/ppermute | solution.py:450
  148.0 0.8 collective-permute-start.4
  148.8 0.9 collective-permute-start.3
  149.7 1.2 collective-permute-done.5.h
  151.0 0.0 copy-start.4
  151.0 3.5 %collective-permute-done.4.g = f32[2,96,128]{2,1,0:T(8,128)S(1)} collective-permute-done((f32[2,96,128]{2,1,0:T(8,128)}, f32[2,96,128]{2,1,0:T(8,128)S(1)}, u32[]{:S(2)}, u32[]{:S(2)}) %collective-permute-start.4) | collective-permute-done | bytes 98336 | tf_op jit(solution)/shard_map/ppermute | solution.py:450
  154.4 0.0 copy-start.5
  154.4 1.0 collective-permute-done.3.f
  155.4 0.0 copy-start.6
  155.4 0.0 copy-done.4
  155.4 0.0 copy-done.5
  155.4 0.6 copy-done.6
  156.0 5.5 %final_join.1 = f32[3072,128]{1,0:T(8,128)} custom-call(s32[2]{0:T(128)} %pad_add_fusion.place, f32[4,6,96,128]{3,2,1,0:T(8,128)} %get-tuple-element.14.links.inner, f32[4,6,96,128]{3,2,1,0:T(8,128)} %get-tuple-element.15.outer, f32[2,96,128]{2,1,0:T(8,128)} %get-tuple-element.17.a, f32[2,96,128]{2,1,0:T(8,128)} %copy-done.3, f32[2,96,128]{2,1,0:T(8,128)} %copy-done.2, ...), custom_call_target="tpu_custom_call" | custom-call | flops 3000000 | bytes 9000000 | tf_op jit(solution)/shard_map/final_join/pallas_call | solution.py:429
  161.6 2.0 %copy.24 = f32[32,16,3,2,128]{4,2,1,3,0:T(4,128)S(1)} copy(f32[32,16,3,2,128]{4,3,2,1,0:T(2,128)} %bitcast.31) | data formatting | bytes 3145728 | tf_op jit(solution)/shard_map/reshape | solution.py:63
  163.5 1.8 %reshape.39 = f32[32,16,2,384]{3,1,2,0:T(8,128)} reshape(f32[32,16,2,3,128]{4,3,1,2,0:T(4,128)S(1)} %bitcast.30) | data formatting | bytes 3145728 | tf_op jit(solution)/shard_map/reshape | solution.py:64
  165.3 3.4 %copy.22 = f32[32,16,2,384]{3,2,1,0:T(2,128)} copy(f32[32,16,2,384]{3,1,2,0:T(8,128)} %reshape.39) | data formatting | bytes 3145728 | tf_op jit(solution)/shard_map/reshape | solution.py:64
  (1 shorter events, 0.0 us)
Async XLA Ops:
  6.5 127.8 %all-gather.3.cloned.1.call-start = ((), (), s32[]{:S(2)}) async-start(), calls=%async_computation.2 | async-start | bytes 3342336 | tf_op jit(solution)/shard_map/all_gather | solution.py:480
  18.7 2.4 %copy-start = (f32[32,16,2,384]{3,2,1,0:T(2,128)S(1)}, f32[32,16,2,384]{3,2,1,0:T(2,128)}, u32[]{:S(2)}) copy-start(f32[32,16,2,384]{3,2,1,0:T(2,128)} %param.8) | copy-start | bytes 4718596
  129.0 13.4 %collective-permute-start.2 = (f32[2,96,128]{2,1,0:T(8,128)}, f32[2,96,128]{2,1,0:T(8,128)S(1)}, u32[]{:S(2)}, u32[]{:S(2)}) collective-permute-start(f32[2,96,128]{2,1,0:T(8,128)} %get-tuple-element.17.a), channel_id=1, source_target_pairs={{0,24},{8,0},{16,8},{24,16},{1,25},{9,1},{17,9},{25,17},{2,26},{10... | collective-permute-start | bytes 294920 | tf_op jit(solution)/shard_map/ppermute | solution.py:450
  132.0 10.4 %collective-permute-start.1 = (f32[2,96,128]{2,1,0:T(8,128)}, f32[2,96,128]{2,1,0:T(8,128)S(1)}, u32[]{:S(2)}, u32[]{:S(2)}) collective-permute-start(f32[2,96,128]{2,1,0:T(8,128)} %get-tuple-element.17.a), channel_id=1, source_target_pairs={{0,16},{8,24},{16,0},{24,8},{1,17},{9,25},{17,1},{25,9},{2,18},{10... | collective-permute-start | bytes 294920 | tf_op jit(solution)/shard_map/ppermute | solution.py:450
  132.7 9.8 %collective-permute-start = (f32[2,96,128]{2,1,0:T(8,128)}, f32[2,96,128]{2,1,0:T(8,128)S(1)}, u32[]{:S(2)}, u32[]{:S(2)}) collective-permute-start(f32[2,96,128]{2,1,0:T(8,128)} %get-tuple-element.17.a), channel_id=1, source_target_pairs={{0,8},{8,16},{16,24},{24,0},{1,9},{9,17},{17,25},{25,1},{2,10},{10... | collective-permute-start | bytes 294920 | tf_op jit(solution)/shard_map/ppermute | solution.py:450
  142.4 0.6 copy-start.1
  142.4 0.7 copy-start.2
  142.4 0.7 copy-start.3
  145.2 5.7 %collective-permute-start.5 = (f32[2,96,128]{2,1,0:T(8,128)}, f32[2,96,128]{2,1,0:T(8,128)S(1)}, u32[]{:S(2)}, u32[]{:S(2)}) collective-permute-start(f32[2,96,128]{2,1,0:T(8,128)} %inner_join.1.e), channel_id=1, source_target_pairs={{0,96},{32,0},{64,32},{96,64},{1,97},{33,1},{65,33},{97,65},{2,98}... | collective-permute-start | bytes 294920 | tf_op jit(solution)/shard_map/ppermute | solution.py:450
  148.0 6.4 %collective-permute-start.4 = (f32[2,96,128]{2,1,0:T(8,128)}, f32[2,96,128]{2,1,0:T(8,128)S(1)}, u32[]{:S(2)}, u32[]{:S(2)}) collective-permute-start(f32[2,96,128]{2,1,0:T(8,128)} %inner_join.1.e), channel_id=1, source_target_pairs={{0,64},{32,96},{64,0},{96,32},{1,65},{33,97},{65,1},{97,33},{2,66}... | collective-permute-start | bytes 294920 | tf_op jit(solution)/shard_map/ppermute | solution.py:450
  148.8 6.6 %collective-permute-start.3 = (f32[2,96,128]{2,1,0:T(8,128)}, f32[2,96,128]{2,1,0:T(8,128)S(1)}, u32[]{:S(2)}, u32[]{:S(2)}) collective-permute-start(f32[2,96,128]{2,1,0:T(8,128)} %inner_join.1.e), channel_id=1, source_target_pairs={{0,32},{32,64},{64,96},{96,0},{1,33},{33,65},{65,97},{97,1},{2,34}... | collective-permute-start | bytes 294920 | tf_op jit(solution)/shard_map/ppermute | solution.py:450
  151.0 4.5 %copy-start.4 = (f32[2,96,128]{2,1,0:T(8,128)}, f32[2,96,128]{2,1,0:T(8,128)S(1)}, u32[]{:S(2)}) copy-start(f32[2,96,128]{2,1,0:T(8,128)S(1)} %collective-permute-done.5.h) | copy-start | bytes 294916
  154.4 1.0 copy-start.5
  155.4 0.6 copy-start.6
Sparse Core Ops, SparseCore 0:
  13.6 50.2 all-gather.2

commit v2 on v1

v2 whole, which is shorter than its diff:
```python
import functools
import math

import jax
import jax.numpy as jnp
import ml_dtypes
import numpy as np
from jax import lax
from jax.experimental import pallas as pl
from jax.experimental.pallas import tpu as pltpu
from jax.sharding import Mesh
from jax.sharding import PartitionSpec as P

F32, BF16 = jnp.float32, jnp.bfloat16
MODE = ("mode_0", "mode_1")
RADIAL = ("radial_0", "radial_1")
NLON = 1536
POINTS = 384
LANES = 128
SHELLS, ORD, HALVES, DEG, NLAT = 32, 16, 2, 384, 768
TILES = DEG // LANES
ROWS = ORD * TILES * HALVES
NMODE = 8
NSHELL = SHELLS // NMODE
PAIRS = ORD * HALVES


def params(mebibytes=56):
    return pltpu.CompilerParams(vmem_limit_bytes=mebibytes * 2**20)


def cost(flops, nbytes):
    return pl.CostEstimate(flops=flops, bytes_accessed=nbytes, transcendentals=0)


def whole(space=pltpu.VMEM):
    return pl.BlockSpec(memory_space=space)


def fixed(shape):
    return pl.BlockSpec(shape, lambda *_: (0,) * len(shape))


def longitude_tables(orders):
    step = NLON // POINTS
    points = np.arange(POINTS) * step
    phase = (np.arange(orders)[:, None] * points[None, :]) % NLON
    angle = phase * (2.0 * math.pi / NLON)
    paired = np.stack([np.cos(angle), -np.sin(angle)], axis=1).reshape(2 * orders, POINTS)
    synth = (paired / math.sqrt(orders)).astype(np.float32).astype(ml_dtypes.bfloat16)
    analysis = (paired * math.sqrt(2.0 / NLON)).astype(np.float32).astype(ml_dtypes.bfloat16)
    return synth.T.copy(), (analysis.astype(np.float32) * step).astype(ml_dtypes.bfloat16)


HALF = ORD // 2
PAIRS_HALF = HALF * HALVES


def moved(device, k, back):
    z, core = device // 2, device % 2
    ahead = 1 - 2 * core
    steps, other = (
        (0, 0),
        (ahead, 0),
        (-ahead, 0),
        (ahead, 1),
        (-ahead, 1),
        (2, 0),
        (2, 1),
        (0, 1),
    )[k]
    if back and k in (1, 2):
        steps = -steps
    core = 1 - core if other else core
    return (z + steps + 4) % 4 * 2 + core


def moved_all(arrays, back):
    sent = [arrays[0]]
    for k in range(1, NMODE):
        pairs = [(d, moved(d, k, back)) for d in range(NMODE)]
        sent.append(lax.ppermute(arrays[k], MODE, pairs))
    return sent


def synthesis_kernel(half, me, field, flow, legendre, *refs):
    outs, (fields, flows, table, lat, sems, table_sems, out_sems) = refs[:NMODE], refs[NMODE:]
    orders = pl.ds(half * HALF, HALF)
    copies = [
        pltpu.make_async_copy(field.at[:, orders], fields, sems.at[0]),
        pltpu.make_async_copy(flow.at[:, orders], flows, sems.at[1]),
    ]
    tables = [
        pltpu.make_async_copy(legendre.at[half * HALF + m], table.at[m], table_sems.at[m])
        for m in range(HALF)
    ]
    for copy in copies + tables:
        copy.start()
    for copy in copies:
        copy.wait()
    for m in range(HALF):
        spectral = jnp.concatenate(
            [source[:, m].reshape(SHELLS * HALVES, DEG) for source in (fields, flows)], axis=0
        ).astype(BF16)
        tables[m].wait()
        values = jnp.dot(spectral, table[m], preferred_element_type=F32).astype(BF16)
        for f in range(2):
            mine = values[f * SHELLS * HALVES : (f + 1) * SHELLS * HALVES]
            lat[:, f, :, HALVES * m : HALVES * (m + 1), :] = mine.reshape(
                NMODE, NSHELL, HALVES, NLAT
            )
    sent = []
    for k in range(NMODE):
        source = lat.at[moved(me[0], k, False)]
        sent.append(pltpu.make_async_copy(source, outs[k], out_sems.at[k]))
        sent[-1].start()
    for copy in sent:
        copy.wait()


def synthesis(half, me, field, flow, legendre):
    shape = jax.ShapeDtypeStruct((2, NSHELL, PAIRS_HALF, NLAT), BF16)
    return pl.pallas_call(
        functools.partial(synthesis_kernel, half),
        out_shape=(shape,) * NMODE,
        in_specs=[whole(pltpu.SMEM)] + [whole(pl.ANY)] * 3,
        out_specs=(whole(pl.ANY),) * NMODE,
        scratch_shapes=[
            pltpu.VMEM((SHELLS, HALF, HALVES, DEG), F32),
            pltpu.VMEM((SHELLS, HALF, HALVES, DEG), F32),
            pltpu.VMEM((HALF, DEG, NLAT), BF16),
            pltpu.VMEM((NMODE, 2, NSHELL, PAIRS_HALF, NLAT), BF16),
            pltpu.SemaphoreType.DMA((2,)),
            pltpu.SemaphoreType.DMA((HALF,)),
            pltpu.SemaphoreType.DMA((NMODE,)),
        ],
        compiler_params=params(),
        cost_estimate=cost(2 * 128 * DEG * NLAT * HALF, 8_000_000),
        name="synthesis",
    )(me, field, flow, legendre)


def grid_kernel(me, synth, analysis, *refs):
    firsts, seconds = refs[:NMODE], refs[NMODE : 2 * NMODE]
    outs = refs[2 * NMODE : 3 * NMODE]
    lat, modes, sems, out_sems = refs[3 * NMODE :]
    arrived = []
    for k in range(NMODE):
        top = moved(me[0], k, True) * PAIRS
        for h, source in enumerate((firsts[k], seconds[k])):
            place = lat.at[:, :, pl.ds(pl.multiple_of(top + h * PAIRS_HALF, PAIRS_HALF), PAIRS_HALF)]
            arrived.append(pltpu.make_async_copy(source, place, sems.at[k, h]))
            arrived[-1].start()
    for copy in arrived:
        copy.wait()
    sent = []
    for r in range(NSHELL):
        field = jnp.dot(synth[...], lat[0, r], preferred_element_type=F32)
        flow = jnp.dot(synth[...], lat[1, r], preferred_element_type=F32)
        product = (field * flow).astype(BF16)
        found = jnp.dot(analysis[...], product, preferred_element_type=F32).astype(BF16)
        modes[:, r] = found.reshape(NMODE, PAIRS, NLAT)
        for k in range(NMODE):
            source = modes.at[moved(me[0], k, True), r]
            sent.append(pltpu.make_async_copy(source, outs[k].at[r], out_sems.at[r, k]))
            sent[-1].start()
    for copy in sent:
        copy.wait()


def grid_product(me, synth, analysis, firsts, seconds):
    shape = jax.ShapeDtypeStruct((NSHELL, PAIRS, NLAT), BF16)
    return pl.pallas_call(
        grid_kernel,
        out_shape=(shape,) * NMODE,
        in_specs=[whole(pltpu.SMEM), whole(), whole()] + [whole(pl.ANY)] * (2 * NMODE),
        out_specs=(whole(pl.ANY),) * NMODE,
        scratch_shapes=[
            pltpu.VMEM((2, NSHELL, NMODE * PAIRS, NLAT), BF16),
            pltpu.VMEM((NMODE, NSHELL, PAIRS, NLAT), BF16),
            pltpu.SemaphoreType.DMA((NMODE, 2)),
            pltpu.SemaphoreType.DMA((NSHELL, NMODE)),
        ],
        compiler_params=params(16),
        cost_estimate=cost(3 * 2 * POINTS * 256 * NLAT * NSHELL, 5_000_000),
        name="grid_product",
    )(me, synth, analysis, *firsts, *seconds)


def block_matrix_kernel(shell, angular, pivots, left, right, ends):
    ang = angular[...]
    ratio = jnp.zeros((ROWS, LANES), F32)
    answer = jnp.ones((ROWS, LANES), F32)
    ratios = []
    for i in range(SHELLS):
        kappa, low, up, radius2 = shell[0, i], shell[1, i], shell[2, i], shell[3, i]
        diagonal = 1.0 + 2.0 * kappa + kappa * ang / radius2
        inverse = 1.0 / (diagonal - low * ratio)
        ratio = up * inverse
        answer = low * inverse * answer
        pivots[i] = inverse
        left[i] = answer
    before = left[SHELLS - 1]
    behind = ratio
    right[SHELLS - 1] = behind
    ends[2] = before
    ends[3] = behind
    for i in reversed(range(SHELLS - 1)):
        ratio = shell[2, i] * pivots[i]
        before = left[i] + ratio * before
        behind = ratio * behind
        left[i] = before
        right[i] = behind
    ends[0] = before
    ends[1] = behind


def block_matrix(shell, angular):
    big = jax.ShapeDtypeStruct((SHELLS, ROWS, LANES), F32)
    return pl.pallas_call(
        block_matrix_kernel,
        out_shape=(big, big, big, jax.ShapeDtypeStruct((4, ROWS, LANES), F32)),
        in_specs=[whole(pltpu.SMEM), whole()],
        out_specs=(whole(),) * 4,
        compiler_params=params(16),
        cost_estimate=cost(10_000_000, 6_000_000),
        name="block_matrix",
    )(shell, angular)


CHAIN = 4


def chain_matrix(blocks):
    links = []
    beta = None
    for first_left, first_right, last_left, last_right in blocks:
        if beta is None:
            den = jnp.ones_like(first_left)
            beta = jnp.zeros_like(first_left)
        else:
            den = 1.0 / (1.0 - first_left * beta)
        extra = last_left * beta * den
        links.append(
            (den, den * first_left, den * first_right, extra, last_left * den, beta)
        )
        beta = last_right + extra * first_right
    alpha = None
    alphas = []
    for link in links:
        alphas.append(alpha)
        alpha = link[4] if alpha is None else link[4] * alpha
    before = None
    behind = None
    for link, start in zip(reversed(links), reversed(alphas)):
        own = link[1] if start is None else link[1] * start
        before = own if before is None else own + link[2] * before
        behind = link[2] if behind is None else link[2] * behind
    return links, (before, behind, alpha, beta)


def level_kernel(place, ends, inner, outer, held):
    supers = []
    for x in range(CHAIN):
        links, own = chain_matrix(
            [tuple(ends[x * CHAIN + k, n] for n in range(4)) for k in range(CHAIN)]
        )
        supers.append(own)
        for k in range(CHAIN):
            for n in range(6):
                held[x, k, n] = links[k][n]
    links, _ = chain_matrix(supers)
    for k in range(CHAIN):
        for n in range(6):
            outer[k, n] = links[k][n]
    inner[...] = held[place[0]]


def levels(place, ends):
    rows = 8
    shape = jax.ShapeDtypeStruct((CHAIN, 6, ROWS, LANES), F32)
    spec = pl.BlockSpec((CHAIN, 6, rows, LANES), lambda i: (0, 0, i, 0))
    return pl.pallas_call(
        level_kernel,
        out_shape=(shape, shape),
        grid=(ROWS // rows,),
        in_specs=[
            whole(pltpu.SMEM),
            pl.BlockSpec((CHAIN * CHAIN, 4, rows, LANES), lambda i: (0, 0, i, 0)),
        ],
        out_specs=(spec, spec),
        scratch_shapes=[pltpu.VMEM((CHAIN, CHAIN, 6, rows, LANES), F32)],
        compiler_params=params(12),
        cost_estimate=cost(10_000_000, 8_000_000),
        name="levels",
    )(place, ends)


def forcing_kernel(me, shell, field, pivots, legendre, *refs):
    slots = refs[:NMODE]
    solved, ends, modes, sems = refs[NMODE:]
    copies = [
        pltpu.make_async_copy(
            slots[k], modes.at[pl.ds(moved(me[0], k, False) * NSHELL, NSHELL)], sems.at[k]
        )
        for k in range(NMODE)
    ]
    for copy in copies:
        copy.start()
    for copy in copies:
        copy.wait()
    for m in range(ORD):
        lat = modes[:, HALVES * m : HALVES * (m + 1), :].reshape(SHELLS * HALVES, NLAT)
        forcing = lax.dot_general(
            lat, legendre[m], (((1,), (1,)), ((), ())), preferred_element_type=F32
        )
        right_side = field[:, m].reshape(SHELLS * HALVES, DEG) + forcing
        for tile in range(TILES):
            row = (m * TILES + tile) * HALVES
            solved[:, row : row + HALVES, :] = right_side[
                :, tile * LANES : (tile + 1) * LANES
            ].reshape(SHELLS, HALVES, LANES)
    value = solved[0] * pivots[0]
    solved[0] = value
    for i in range(1, SHELLS):
        value = (solved[i] + shell[1, i] * value) * pivots[i]
        solved[i] = value
    ends[1] = value.astype(BF16)
    for i in reversed(range(SHELLS - 1)):
        value = solved[i] + (shell[2, i] * pivots[i]) * value
        solved[i] = value
    ends[0] = value.astype(BF16)


def forcing_solve(me, shell, slots, legendre, field, pivots):
    return pl.pallas_call(
        forcing_kernel,
        out_shape=(
            jax.ShapeDtypeStruct((SHELLS, ROWS, LANES), F32),
            jax.ShapeDtypeStruct((2, ROWS, LANES), BF16),
        ),
        in_specs=[whole(pltpu.SMEM)] * 2 + [whole()] * 3 + [whole(pl.ANY)] * NMODE,
        out_specs=(whole(), whole()),
        scratch_shapes=[
            pltpu.VMEM((SHELLS, PAIRS, NLAT), BF16),
            pltpu.SemaphoreType.DMA((NMODE,)),
        ],
        compiler_params=params(24),
        cost_estimate=cost(2 * 64 * DEG * NLAT * ORD, 16_000_000),
        name="forcing_solve",
    )(me, shell, field, pivots, legendre, *slots)


def chain_values(links, values, first, last):
    alphas = [first]
    for k in range(CHAIN):
        first_value, last_value = values[k]
        alpha = last_value + links(k, 3) * first_value
        if alphas[-1] is not None:
            alpha = alpha + links(k, 4) * alphas[-1]
        alphas.append(alpha)
    firsts = [None] * CHAIN + [last]
    for k in reversed(range(CHAIN)):
        value = links(k, 0) * values[k][0]
        if alphas[k] is not None:
            value = value + links(k, 1) * alphas[k]
        if firsts[k + 1] is not None:
            value = value + links(k, 2) * firsts[k + 1]
        firsts[k] = value
    return alphas, firsts


def boundary_values(links, alphas, firsts, shape):
    zero = jnp.zeros(shape, F32)
    pairs = []
    for k in range(CHAIN):
        before = zero if alphas[k] is None else alphas[k] + links(k, 5) * firsts[k]
        behind = zero if firsts[k + 1] is None else firsts[k + 1]
        pairs.append((before, behind))
    return pairs


def slot_copies(position, slots, held, sems):
    return [
        pltpu.make_async_copy(slot, held.at[lax.rem(position + CHAIN - s, CHAIN)], sems.at[s])
        for s, slot in enumerate(slots)
    ]


def inner_kernel(place, links, a, b, c, d, out, held, coefficients, sems):
    copies = slot_copies(place[1], (a, b, c, d), held, sems)
    copies.append(pltpu.make_async_copy(links, coefficients, sems.at[CHAIN]))
    for copy in copies:
        copy.start()
    for copy in copies:
        copy.wait()
    values = [(held[k, 0].astype(F32), held[k, 1].astype(F32)) for k in range(CHAIN)]
    alphas, firsts = chain_values(lambda k, n: coefficients[k, n], values, None, None)
    out[0] = firsts[0].astype(BF16)
    out[1] = alphas[CHAIN].astype(BF16)


def inner_join(place, links, slots):
    return pl.pallas_call(
        inner_kernel,
        out_shape=jax.ShapeDtypeStruct((2, ROWS, LANES), BF16),
        in_specs=[whole(pltpu.SMEM)] + [whole(pl.ANY)] * 5,
        out_specs=whole(),
        scratch_shapes=[
            pltpu.VMEM((CHAIN, 2, ROWS, LANES), BF16),
            pltpu.VMEM((CHAIN, 6, ROWS, LANES), F32),
            pltpu.SemaphoreType.DMA((CHAIN + 1,)),
        ],
        compiler_params=params(12),
        cost_estimate=cost(1_000_000, 2_000_000),
        name="inner_join",
    )(place, links, *slots)


PIECES = 4
PIECE = SHELLS // PIECES


def final_kernel(place, inner, outer, a, b, c, d, e, f, g, h, solved, left, right, out, *scratch):
    near, far, near_links, far_links, pairs, terms, result, sems, term_sems, out_sems = scratch
    copies = slot_copies(place[0], (e, f, g, h), far, sems.at[0])
    copies.append(pltpu.make_async_copy(outer, far_links, sems.at[0, CHAIN]))
    copies += slot_copies(place[1], (a, b, c, d), near, sems.at[1])
    copies.append(pltpu.make_async_copy(inner, near_links, sems.at[1, CHAIN]))
    term_copies = [
        pltpu.make_async_copy(source, terms.at[n], term_sems.at[n])
        for n, source in enumerate((solved, left, right))
    ]
    for copy in copies + term_copies:
        copy.start()
    for copy in copies:
        copy.wait()
    first = last = None
    for level, (held, links) in enumerate(((far, far_links), (near, near_links))):
        values = [(held[k, 0].astype(F32), held[k, 1].astype(F32)) for k in range(CHAIN)]
        read = lambda k, n, links=links: links[k, n]
        alphas, firsts = chain_values(read, values, first, last)
        found = boundary_values(read, alphas, firsts, (ROWS, LANES))
        for k, (before, behind) in enumerate(found):
            pairs[k, 0] = before
            pairs[k, 1] = behind
        first, last = pairs[place[level], 0], pairs[place[level], 1]
    for copy in term_copies:
        copy.wait()
    sent = []
    for piece in range(PIECES):
        for i in range(piece * PIECE, (piece + 1) * PIECE):
            value = terms[0, i] + terms[1, i] * first + terms[2, i] * last
            value = value.reshape(ORD, TILES, HALVES, LANES)
            for tile in range(TILES):
                result[i, :, :, tile * LANES : (tile + 1) * LANES] = value[:, tile]
        here = pl.ds(piece * PIECE, PIECE)
        sent.append(pltpu.make_async_copy(result.at[here], out.at[here], out_sems.at[piece]))
        sent[-1].start()
    for copy in sent:
        copy.wait()


def final_join(place, inner, outer, slots, super_slots, solved, left, right):
    return pl.pallas_call(
        final_kernel,
        out_shape=jax.ShapeDtypeStruct((SHELLS, ORD, HALVES, DEG), F32),
        in_specs=[whole(pltpu.SMEM)] + [whole(pl.ANY)] * 13,
        out_specs=whole(pl.ANY),
        scratch_shapes=[
            pltpu.VMEM((CHAIN, 2, ROWS, LANES), BF16),
            pltpu.VMEM((CHAIN, 2, ROWS, LANES), BF16),
            pltpu.VMEM((CHAIN, 6, ROWS, LANES), F32),
            pltpu.VMEM((CHAIN, 6, ROWS, LANES), F32),
            pltpu.VMEM((CHAIN, 2, ROWS, LANES), F32),
            pltpu.VMEM((3, SHELLS, ROWS, LANES), F32),
            pltpu.VMEM((SHELLS, ORD, HALVES, DEG), F32),
            pltpu.SemaphoreType.DMA((2, CHAIN + 1)),
            pltpu.SemaphoreType.DMA((3,)),
            pltpu.SemaphoreType.DMA((PIECES,)),
        ],
        compiler_params=params(24),
        cost_estimate=cost(3_000_000, 9_000_000),
        name="final_join",
    )(place, inner, outer, *slots, *super_slots, solved, left, right)


def shifted(array, axis, step):
    size = lax.axis_size(axis)
    return lax.ppermute(array, axis, [(i, (i + step) % size) for i in range(size)])


def ring(array, axis):
    return [array] + [shifted(array, axis, step) for step in range(1, CHAIN)]


def on_device(scalar_field, radial_flow, legendre, diffusivity):
    synth, analysis = (jnp.asarray(table) for table in longitude_tables(ORD * NMODE))
    mode = lax.axis_index(MODE).astype(jnp.int32)
    me = mode.reshape(1)
    firsts = list(synthesis(0, me, scalar_field, radial_flow, legendre))
    later, firsts[0] = lax.optimization_barrier((me, firsts[0]))
    seconds = synthesis(1, later, scalar_field, radial_flow, legendre)
    firsts, seconds = moved_all(firsts, False), moved_all(seconds, False)
    diffusivity, mode, firsts[7] = lax.optimization_barrier((diffusivity, mode, firsts[7]))

    nr_total = SHELLS * CHAIN * CHAIN
    place = jnp.stack([lax.axis_index(RADIAL[0]), lax.axis_index(RADIAL[1])]).astype(jnp.int32)
    shell_ids = lax.axis_index(RADIAL) * SHELLS + jnp.arange(SHELLS, dtype=jnp.int32)
    radius = (nr_total * 7 // 13 + shell_ids).astype(F32)
    shell = jnp.stack(
        [
            diffusivity,
            jnp.where(shell_ids > 0, diffusivity, 0.0),
            jnp.where(shell_ids < nr_total - 1, diffusivity, 0.0),
            radius * radius,
        ]
    )
    row = np.arange(ROWS)[:, None]
    local_degree = row // (TILES * HALVES) + row // HALVES % TILES * LANES + np.arange(LANES)[None]
    degree = (local_degree + mode * ORD).astype(F32)
    angular = degree * (degree + 1.0)
    pivots, left, right, ends = block_matrix(shell, angular)
    inner, outer = levels(place, lax.all_gather(ends, RADIAL))

    modes = moved_all(grid_product(me, synth, analysis, firsts, seconds), True)
    pivots, inner, outer = lax.optimization_barrier((pivots, inner, outer))
    solved, own = forcing_solve(me, shell, modes, legendre, scalar_field, pivots)
    slots = ring(own, RADIAL[1])
    super_slots = ring(inner_join(place, inner, slots), RADIAL[0])
    return final_join(place, inner, outer, slots, super_slots, solved, left, right)


def solution(mesh):
    finer = Mesh(
        mesh.devices.reshape(4, 4, 4, 2), ("radial_0", "radial_1", "mode_0", "mode_1")
    )
    return jax.shard_map(
        on_device,
        mesh=finer,
        in_specs=(
            P(RADIAL, MODE, None, None),
            P(RADIAL, MODE, None, None),
            P(MODE, None, None),
            P(RADIAL),
        ),
        out_specs=P(RADIAL, MODE, None, None),
        check_vma=False,
    )
```

time: 177 us -> 129 us (0.73)
  blocking collectives: 70.5 us -> 0 us
  waiting for transfers between devices: 5.7 us -> 35.6 us
  starting transfers between devices: 9.14 us -> 34.7 us
  Pallas kernels: 50.6 us -> 34.9 us
  local copies, waits for them, and re-layouts: 22.1 us -> 9.95 us
  other arithmetic: 3.98 us -> 0.11 us
    all_to_all x2 -> x0, blocking collectives: 70.5 us -> none  [exchange(): return lax.all_to_all(array, MODE, 0, 0, tiled=True)]
    ppermute x6 -> x27, waiting for transfers between devices: 5.68 us -> 35.6 us  [the longest x21 26.5 us: moved_all(): sent.append(lax.ppermute(arrays[k], MODE, pairs))]
    ppermute x6 -> x27, starting transfers between devices: 9.14 us -> 34.7 us  [the longest x21 25.4 us: moved_all(): sent.append(lax.ppermute(arrays[k], MODE, pairs))]
    reshape x5 -> x0, local copies, waits for them, and re-layouts: 12.1 us -> none  [the longest x2 5.14 us: from_rows(): return rows.reshape(SHELLS, ORD, HALVES, DEG)]
    pallas_call x4 -> x5, Pallas kernels: 36.7 us -> 29.4 us  [the longest x2 13.8 us: synthesis(): pl.pallas_call(functools.partial(synthesis_kernel, half), out_shape=(shap...]
    pallas_call x1, Pallas kernels: 8.09 us -> 2.21 us  [levels(): pl.pallas_call(level_kernel, out_shape=(shape, shape), grid=(ROWS // rows...]
    transpose x2 -> x0, local copies, waits for them, and re-layouts: 4.82 us -> none  [to_rows(): array.reshape(SHELLS, ORD, HALVES, TILES, LANES).transpose(0, 1, 3, 2, 4)]
    unnamed x16 -> x32, local copies, waits for them, and re-layouts: 5.23 us -> 9.95 us
  transfers between devices with their start and end apart: 7 -> 28, of which waited for: 3 -> 17; matrix products, arithmetic and copies ran while one was open for 8% -> 0% of each run, Pallas kernels for 22% -> 12%
where the time goes in v2:
time: 129 us
  waiting for transfers between devices  35.6 us (28%)
  Pallas kernels  34.9 us (27%)
  starting transfers between devices  34.7 us (27%)
  between operations  13.6 us (11%)
  local copies, waits for them, and re-layouts  9.95 us (8%)
    ppermute x21, waiting for transfers between devices, moved_all(): sent.append(lax.ppermute(arrays[k], MODE, pairs))  26.5 us
    ppermute x21, starting transfers between devices, moved_all(): sent.append(lax.ppermute(arrays[k], MODE, pairs))  25.4 us
    pallas_call x2, Pallas kernels, synthesis(): pl.pallas_call(functools.partial(synthesis_kernel, half), out_shape=(shap...  13.8 us
    unnamed x32, local copies, waits for them, and re-layouts  9.95 us
    ppermute x6, starting transfers between devices, shifted(): lax.ppermute(array, axis, [(i, (i + step) % size) for i in range(size)])  9.22 us
    ppermute x6, waiting for transfers between devices, shifted(): lax.ppermute(array, axis, [(i, (i + step) % size) for i in range(size)])  9.1 us
    pallas_call x1, Pallas kernels, forcing_solve(): pl.pallas_call(forcing_kernel, out_shape=(jax.ShapeDtypeStruct((SHELLS, R...  6.23 us
    pallas_call x1, Pallas kernels, grid_product(): pl.pallas_call(grid_kernel, out_shape=(shape,) * NMODE, in_specs=[whole(p...  5.84 us
  transfers between devices with their start and end apart: 28, of which 17 were waited for; matrix products, arithmetic and copies ran while one was open for 0% of the time, Pallas kernels for 12%

profile of v2, /device:TPU:0, one launch (start us, length us, event | category | flops | bytes accessed | tf_op | source)
XLA Modules:
  0.0 128.8 jit_solution(4299895179938321190)
XLA Ops:
  6.5 6.8 %synthesis.2 = (bf16[2,4,16,768]{3,2,1,0:T(8,128)(2,1)}, bf16[2,4,16,768]{3,2,1,0:T(8,128)(2,1)}, bf16[2,4,16,768]{3,2,1,0:T(8,128)(2,1)}, bf16[2,4,16,768]{3,2,...) custom-call(s32[1]{0:T(128)} %bitcast.2.me, ...), custom_call_target="tpu_custom_call" | custom-call | flops 603979776 | bytes 8000000 | tf_op jit(solution)/shard_map/synthesis/pallas_call | solution.py:123
  13.4 0.1 collective-permute-start
  13.5 1.6 %collective-permute-done.refs_7_ = bf16[2,4,16,768]{3,2,1,0:T(8,128)(2,1)S(1)} collective-permute-done((bf16[2,4,16,768]{3,2,1,0:T(8,128)(2,1)}, bf16[2,4,16,768]{3,2,1,0:T(8,128)(2,1)S(1)}, u32[]{:S(2)}, u32[]{:S(2)}) %collective-permute-start) | collective-permute-done | bytes 196640 | tf_op jit(solution)/shard_map/ppermute | solution.py:82
  15.1 0.7 copy-done.8
  15.8 2.1 %block_matrix.1 = (f32[32,96,128]{2,1,0:T(8,128)S(1)}, f32[32,96,128]{2,1,0:T(8,128)S(1)}, f32[32,96,128]{2,1,0:T(8,128)S(1)}, f32[4,96,128]{2,1,0:T(8,128)}) custom-call(f32[4,32]{1,0:T(4,128)S(1)} %pad_maximum_fusion.shell, f32[96,128]{1,0:T(8,128)S(1)} %add_multiply_fusion.angular), custom_call_target="tpu_custom_call" | custom-call | flops 10000000 | bytes 6000000 | tf_op jit(solution)/shard_map/block_matrix/pallas_call | solution.py:220
  17.9 1.1 copy-done.3
  19.0 0.0 all-gather.3.cloned.1.call-update
  19.1 2.1 %collective-permute-start.1 = (bf16[2,4,16,768]{3,2,1,0:T(8,128)(2,1)}, bf16[2,4,16,768]{3,2,1,0:T(8,128)(2,1)S(1)}, u32[]{:S(2)}, u32[]{:S(2)}) collective-permute-start(bf16[2,4,16,768]{3,2,1,0:T(8,128)(2,1)} %get-tuple-element.57), channel_id=1, source_target_pairs={{0,2},{1,7},{2,4},{3,1},{4,6},{5,3},{6,0},{7,5},{8,10},{9,15},{10,... | collective-permute-start | bytes 589832 | tf_op jit(solution)/shard_map/ppermute | solution.py:82
  21.1 2.2 %collective-permute-start.2 = (bf16[2,4,16,768]{3,2,1,0:T(8,128)(2,1)}, bf16[2,4,16,768]{3,2,1,0:T(8,128)(2,1)S(1)}, u32[]{:S(2)}, u32[]{:S(2)}) collective-permute-start(bf16[2,4,16,768]{3,2,1,0:T(8,128)(2,1)} %get-tuple-element.58), channel_id=1, source_target_pairs={{0,6},{1,3},{2,0},{3,5},{4,2},{5,7},{6,4},{7,1},{8,14},{9,11},{10,... | collective-permute-start | bytes 589832 | tf_op jit(solution)/shard_map/ppermute | solution.py:82
  23.3 0.0 collective-permute-start.3
  23.3 2.3 %collective-permute-start.4 = (bf16[2,4,16,768]{3,2,1,0:T(8,128)(2,1)}, bf16[2,4,16,768]{3,2,1,0:T(8,128)(2,1)S(1)}, u32[]{:S(2)}, u32[]{:S(2)}) collective-permute-start(bf16[2,4,16,768]{3,2,1,0:T(8,128)(2,1)} %get-tuple-element.60), channel_id=1, source_target_pairs={{0,7},{1,2},{2,1},{3,4},{4,3},{5,6},{6,5},{7,0},{8,15},{9,10},{10,... | collective-permute-start | bytes 589832 | tf_op jit(solution)/shard_map/ppermute | solution.py:82
  25.7 1.5 %collective-permute-start.5 = (bf16[2,4,16,768]{3,2,1,0:T(8,128)(2,1)}, bf16[2,4,16,768]{3,2,1,0:T(8,128)(2,1)S(1)}, u32[]{:S(2)}, u32[]{:S(2)}) collective-permute-start(bf16[2,4,16,768]{3,2,1,0:T(8,128)(2,1)} %get-tuple-element.61), channel_id=1, source_target_pairs={{0,4},{1,5},{2,6},{3,7},{4,0},{5,1},{6,2},{7,3},{8,12},{9,13},{10,... | collective-permute-start | bytes 589832 | tf_op jit(solution)/shard_map/ppermute | solution.py:82
  27.2 0.0 copy-start.12
  27.2 7.0 %synthesis.3 = (bf16[2,4,16,768]{3,2,1,0:T(8,128)(2,1)}, bf16[2,4,16,768]{3,2,1,0:T(8,128)(2,1)}, bf16[2,4,16,768]{3,2,1,0:T(8,128)(2,1)}, bf16[2,4,16,768]{3,2,...) custom-call(s32[1]{0:T(128)} %bitcast.2.me, ...), custom_call_target="tpu_custom_call" | custom-call | flops 603979776 | bytes 8000000 | tf_op jit(solution)/shard_map/synthesis/pallas_call | solution.py:123
  34.2 0.0 collective-permute-done.1.refs_1_
  34.2 1.2 collective-permute-start.6
  35.4 0.0 collective-permute-done.2.refs_2_
  35.4 1.8 %collective-permute-start.7 = (bf16[2,4,16,768]{3,2,1,0:T(8,128)(2,1)}, bf16[2,4,16,768]{3,2,1,0:T(8,128)(2,1)S(1)}, u32[]{:S(2)}, u32[]{:S(2)}) collective-permute-start(bf16[2,4,16,768]{3,2,1,0:T(8,128)(2,1)} %get-tuple-element.66), channel_id=1, source_target_pairs={{0,2},{1,7},{2,4},{3,1},{4,6},{5,3},{6,0},{7,5},{8,10},{9,15},{10,... | collective-permute-start | bytes 589832 | tf_op jit(solution)/shard_map/ppermute | solution.py:82
  37.2 0.0 collective-permute-done.3.refs_3_
  37.2 2.0 %collective-permute-start.8 = (bf16[2,4,16,768]{3,2,1,0:T(8,128)(2,1)}, bf16[2,4,16,768]{3,2,1,0:T(8,128)(2,1)S(1)}, u32[]{:S(2)}, u32[]{:S(2)}) collective-permute-start(bf16[2,4,16,768]{3,2,1,0:T(8,128)(2,1)} %get-tuple-element.67), channel_id=1, source_target_pairs={{0,6},{1,3},{2,0},{3,5},{4,2},{5,7},{6,4},{7,1},{8,14},{9,11},{10,... | collective-permute-start | bytes 589832 | tf_op jit(solution)/shard_map/ppermute | solution.py:82
  39.2 0.0 collective-permute-done.5.refs_5_
  39.2 0.7 collective-permute-start.10
  39.9 2.9 %collective-permute-done.6.refs_6_ = bf16[2,4,16,768]{3,2,1,0:T(8,128)(2,1)S(1)} collective-permute-done((bf16[2,4,16,768]{3,2,1,0:T(8,128)(2,1)S(1)}, bf16[2,4,16,768]{3,2,1,0:T(8,128)(2,1)S(1)}, u32[]{:S(2)}, u32[]{:S(2)}) %collective-permute-start.6) | collective-permute-done | bytes 196640 | tf_op jit(solution)/shard_map/ppermute | solution.py:82
  42.7 2.2 %collective-permute-start.11 = (bf16[2,4,16,768]{3,2,1,0:T(8,128)(2,1)}, bf16[2,4,16,768]{3,2,1,0:T(8,128)(2,1)S(1)}, u32[]{:S(2)}, u32[]{:S(2)}) collective-permute-start(bf16[2,4,16,768]{3,2,1,0:T(8,128)(2,1)} %get-tuple-element.70), channel_id=1, source_target_pairs={{0,4},{1,5},{2,6},{3,7},{4,0},{5,1},{6,2},{7,3},{8,12},{9,13},{10,... | collective-permute-start | bytes 589832 | tf_op jit(solution)/shard_map/ppermute | solution.py:82
  45.0 2.2 %collective-permute-done.7.refs_9_ = bf16[2,4,16,768]{3,2,1,0:T(8,128)(2,1)S(1)} collective-permute-done((bf16[2,4,16,768]{3,2,1,0:T(8,128)(2,1)}, bf16[2,4,16,768]{3,2,1,0:T(8,128)(2,1)S(1)}, u32[]{:S(2)}, u32[]{:S(2)}) %collective-permute-start.7) | collective-permute-done | bytes 196640 | tf_op jit(solution)/shard_map/ppermute | solution.py:82
  47.1 0.0 collective-permute-start.12
  47.1 0.0 collective-permute-done.8.refs_10_
  47.2 1.7 %collective-permute-start.13 = (bf16[2,4,16,768]{3,2,1,0:T(8,128)(2,1)}, bf16[2,4,16,768]{3,2,1,0:T(8,128)(2,1)S(1)}, u32[]{:S(2)}, u32[]{:S(2)}) collective-permute-start(bf16[2,4,16,768]{3,2,1,0:T(8,128)(2,1)} %get-tuple-element.72), channel_id=1, source_target_pairs={{0,1},{1,0},{2,3},{3,2},{4,5},{5,4},{6,7},{7,6},{8,9},{9,8},{10,11... | collective-permute-start | bytes 589832 | tf_op jit(solution)/shard_map/ppermute | solution.py:82
  48.9 2.4 %collective-permute-done.9.refs_11_ = bf16[2,4,16,768]{3,2,1,0:T(8,128)(2,1)S(1)} collective-permute-done((bf16[2,4,16,768]{3,2,1,0:T(8,128)(2,1)}, bf16[2,4,16,768]{3,2,1,0:T(8,128)(2,1)S(1)}, u32[]{:S(2)}, u32[]{:S(2)}) %collective-permute-start.9) | collective-permute-done | bytes 196640 | tf_op jit(solution)/shard_map/ppermute | solution.py:82
  51.2 0.4 collective-permute-done.10.refs_12_
  51.7 4.3 %collective-permute-done.11.refs_13_ = bf16[2,4,16,768]{3,2,1,0:T(8,128)(2,1)S(1)} collective-permute-done((bf16[2,4,16,768]{3,2,1,0:T(8,128)(2,1)}, bf16[2,4,16,768]{3,2,1,0:T(8,128)(2,1)S(1)}, u32[]{:S(2)}, u32[]{:S(2)}) %collective-permute-start.11) | collective-permute-done | bytes 196640 | tf_op jit(solution)/shard_map/ppermute | solution.py:82
  56.0 3.6 %collective-permute-done.12.refs_14_ = bf16[2,4,16,768]{3,2,1,0:T(8,128)(2,1)S(1)} collective-permute-done((bf16[2,4,16,768]{3,2,1,0:T(8,128)(2,1)}, bf16[2,4,16,768]{3,2,1,0:T(8,128)(2,1)S(1)}, u32[]{:S(2)}, u32[]{:S(2)}) %collective-permute-start.12) | collective-permute-done | bytes 196640 | tf_op jit(solution)/shard_map/ppermute | solution.py:82
  59.6 0.9 copy-done.10
  60.5 5.8 %grid_product.1 = (bf16[4,32,768]{2,1,0:T(8,128)(2,1)S(1)}, bf16[4,32,768]{2,1,0:T(8,128)(2,1)S(1)}, bf16[4,32,768]{2,1,0:T(8,128)(2,1)S(1)}, bf16[4,32,768]{2,1...) custom-call(s32[1]{0:T(128)} %bitcast.2.me, ...), custom_call_target="tpu_custom_call" | custom-call | flops 1811939328 | bytes 5000000 | tf_op jit(solution)/shard_map/grid_product/pallas_call | solution.py:173
  66.3 2.9 %collective-permute-start.14 = (bf16[4,32,768]{2,1,0:T(8,128)(2,1)S(1)}, bf16[4,32,768]{2,1,0:T(8,128)(2,1)S(1)}, u32[]{:S(2)}, u32[]{:S(2)}) collective-permute-start(bf16[4,32,768]{2,1,0:T(8,128)(2,1)S(1)} %get-tuple-element.74), channel_id=1, source_target_pairs={{0,6},{1,3},{2,0},{3,5},{4,2},{5,7},{6,4},{7,1},{8,14},{9,11},{10,... | collective-permute-start | bytes 589832 | tf_op jit(solution)/shard_map/ppermute | solution.py:82
  69.2 1.8 %collective-permute-start.17 = (bf16[4,32,768]{2,1,0:T(8,128)(2,1)}, bf16[4,32,768]{2,1,0:T(8,128)(2,1)}, u32[]{:S(2)}, u32[]{:S(2)}) collective-permute-start(bf16[4,32,768]{2,1,0:T(8,128)(2,1)} %get-tuple-element.77), channel_id=1, source_target_pairs={{0,7},{1,2},{2,1},{3,4},{4,3},{5,6},{6,5},{7,0},{8,15},{9,10},{10,... | collective-permute-start | bytes 589832 | tf_op jit(solution)/shard_map/ppermute | solution.py:82
  71.0 2.0 %collective-permute-start.18 = (bf16[4,32,768]{2,1,0:T(8,128)(2,1)}, bf16[4,32,768]{2,1,0:T(8,128)(2,1)}, u32[]{:S(2)}, u32[]{:S(2)}) collective-permute-start(bf16[4,32,768]{2,1,0:T(8,128)(2,1)} %get-tuple-element.78), channel_id=1, source_target_pairs={{0,4},{1,5},{2,6},{3,7},{4,0},{5,1},{6,2},{7,3},{8,12},{9,13},{10,... | collective-permute-start | bytes 589832 | tf_op jit(solution)/shard_map/ppermute | solution.py:82
  73.0 1.4 %collective-permute-done.14.refs_1_ = bf16[4,32,768]{2,1,0:T(8,128)(2,1)S(1)} collective-permute-done((bf16[4,32,768]{2,1,0:T(8,128)(2,1)S(1)}, bf16[4,32,768]{2,1,0:T(8,128)(2,1)S(1)}, u32[]{:S(2)}, u32[]{:S(2)}) %collective-permute-start.14) | collective-permute-done | bytes 196640 | tf_op jit(solution)/shard_map/ppermute | solution.py:82
  74.5 1.0 collective-permute-start.19
  75.4 2.4 %collective-permute-done.15.refs_2_ = bf16[4,32,768]{2,1,0:T(8,128)(2,1)S(1)} collective-permute-done((bf16[4,32,768]{2,1,0:T(8,128)(2,1)S(1)}, bf16[4,32,768]{2,1,0:T(8,128)(2,1)S(1)}, u32[]{:S(2)}, u32[]{:S(2)}) %collective-permute-start.15) | collective-permute-done | bytes 196640 | tf_op jit(solution)/shard_map/ppermute | solution.py:82
  77.9 0.7 copy-done.5
  78.5 0.1 pad_add_fusion.place
  78.6 1.9 %copy-done.2 = f32[64,96,128]{2,1,0:T(8,128)S(1)} copy-done((f32[64,96,128]{2,1,0:T(8,128)S(1)}, f32[64,96,128]{2,1,0:T(8,128)}, u32[]{:S(2)}) %copy-start.2) | copy-done | bytes 3145752
  80.5 2.2 %levels.1 = (f32[4,6,96,128]{3,2,1,0:T(8,128)S(1)}, f32[4,6,96,128]{3,2,1,0:T(8,128)S(1)}) custom-call(s32[2]{0:T(128)S(1)} %pad_add_fusion.place, f32[16,4,96,128]{3,2,1,0:T(8,128)S(1)} %bitcast.9), custom_call_target="tpu_custom_call" | custom-call | flops 10000000 | bytes 8000000 | tf_op jit(solution)/shard_map/levels/pallas_call | solution.py:283
  82.7 3.9 %collective-permute-done.17.refs_4_ = bf16[4,32,768]{2,1,0:T(8,128)(2,1)} collective-permute-done((bf16[4,32,768]{2,1,0:T(8,128)(2,1)}, bf16[4,32,768]{2,1,0:T(8,128)(2,1)}, u32[]{:S(2)}, u32[]{:S(2)}) %collective-permute-start.17) | collective-permute-done | bytes 196640 | tf_op jit(solution)/shard_map/ppermute | solution.py:82
  86.6 1.4 %collective-permute-done.19.refs_6_ = bf16[4,32,768]{2,1,0:T(8,128)(2,1)} collective-permute-done((bf16[4,32,768]{2,1,0:T(8,128)(2,1)}, bf16[4,32,768]{2,1,0:T(8,128)(2,1)}, u32[]{:S(2)}, u32[]{:S(2)}) %collective-permute-start.19) | collective-permute-done | bytes 196640 | tf_op jit(solution)/shard_map/ppermute | solution.py:82
  88.0 0.0 copy-start
  88.0 3.7 %copy-done = bf16[16,384,768]{2,1,0:T(8,128)(2,1)S(1)} copy-done((bf16[16,384,768]{2,1,0:T(8,128)(2,1)S(1)}, bf16[16,384,768]{2,1,0:T(8,128)(2,1)}, u32[]{:S(2)}) %copy-start) | copy-done | bytes 9437208
  91.7 0.9 copy-done.6
  92.6 6.2 %forcing_solve.1 = (f32[32,96,128]{2,1,0:T(8,128)S(1)}, bf16[2,96,128]{2,1,0:T(8,128)(2,1)S(1)}) custom-call(s32[1]{0:T(128)} %bitcast.2.me, f32[4,32]{1,0:T(4,128)S(1)} %pad_maximum_fusion.shell, f32[32,16,2,384]{3,2,1,0:T(2,128)S(1)} %copy-done.1, f32[32,96,128]{2,1,0:T(8,128)S(1)} %copy-done.4, bf16[16,384,768]{2,1,0:T(8,128)(2,1)S(1)} %copy-done, ...), custom_call_target="tpu_custom_call" | custom-call | flops 603979776 | bytes 16000000 | tf_op jit(solution)/shard_map/forcing_solve/pallas_call | solution.py:336
  98.9 3.1 %collective-permute-start.23 = (bf16[2,96,128]{2,1,0:T(8,128)(2,1)S(1)}, bf16[2,96,128]{2,1,0:T(8,128)(2,1)S(1)}, u32[]{:S(2)}, u32[]{:S(2)}) collective-permute-start(bf16[2,96,128]{2,1,0:T(8,128)(2,1)S(1)} %get-tuple-element.81.a), channel_id=1, source_target_pairs={{0,24},{8,0},{16,8},{24,16},{1,25},{9,1},{17,9},{25,17},{2,26},{10... | collective-permute-start | bytes 147464 | tf_op jit(solution)/shard_map/ppermute | solution.py:490
  101.9 0.6 collective-permute-start.22
  102.6 1.0 collective-permute-start.21
  103.6 0.6 collective-permute-done.23.d
  104.1 3.6 %collective-permute-done.22.c = bf16[2,96,128]{2,1,0:T(8,128)(2,1)S(1)} collective-permute-done((bf16[2,96,128]{2,1,0:T(8,128)(2,1)S(1)}, bf16[2,96,128]{2,1,0:T(8,128)(2,1)S(1)}, u32[]{:S(2)}, u32[]{:S(2)}) %collective-permute-start.22) | collective-permute-done | bytes 49184 | tf_op jit(solution)/shard_map/ppermute | solution.py:490
  107.7 0.5 collective-permute-done.21.b
  108.2 1.2 inner_join.1.e
  109.4 2.8 %collective-permute-start.26 = (bf16[2,96,128]{2,1,0:T(8,128)(2,1)S(1)}, bf16[2,96,128]{2,1,0:T(8,128)(2,1)S(1)}, u32[]{:S(2)}, u32[]{:S(2)}) collective-permute-start(bf16[2,96,128]{2,1,0:T(8,128)(2,1)S(1)} %inner_join.1.e), channel_id=1, source_target_pairs={{0,96},{32,0},{64,32},{96,64},{1,97},{33,1},{65,33},{97,65},{2,98}... | collective-permute-start | bytes 147464 | tf_op jit(solution)/shard_map/ppermute | solution.py:490
  112.2 0.8 collective-permute-start.25
  113.0 0.9 collective-permute-start.24
  113.9 0.1 collective-permute-done.26.h
  114.0 3.8 %collective-permute-done.25.g = bf16[2,96,128]{2,1,0:T(8,128)(2,1)S(1)} collective-permute-done((bf16[2,96,128]{2,1,0:T(8,128)(2,1)S(1)}, bf16[2,96,128]{2,1,0:T(8,128)(2,1)S(1)}, u32[]{:S(2)}, u32[]{:S(2)}) %collective-permute-start.25) | collective-permute-done | bytes 49184 | tf_op jit(solution)/shard_map/ppermute | solution.py:490
  117.8 0.5 collective-permute-done.24.f
  118.4 3.6 %final_join.1 = f32[32,16,2,384]{3,2,1,0:T(2,128)} custom-call(s32[2]{0:T(128)S(1)} %pad_add_fusion.place, f32[4,6,96,128]{3,2,1,0:T(8,128)S(1)} %get-tuple-element.52.links.inner, f32[4,6,96,128]{3,2,1,0:T(8,128)S(1)} %get-tuple-element.53.outer, bf16[2,96,128]{2,1,0:T(8,128)(2,1)S(1)} %get-tuple-element.81.a, ...), custom_call_target="tpu_custom_call" | custom-call | flops 3000000 | bytes 9000000 | tf_op jit(solution)/shard_map/final_join/pallas_call | solution.py:465
  (38 shorter events, 0.1 us)
Async XLA Ops:
  6.5 72.1 %all-gather.3.cloned.1.call-start = ((), (), s32[]{:S(2)}) async-start(), calls=%async_computation | async-start | bytes 3342336 | tf_op jit(solution)/shard_map/all_gather | solution.py:524
  6.5 9.3 %copy-start.14 = (f32[32]{0:T(128)S(1)}, f32[32]{0:T(128)}, u32[]{:S(2)}) copy-start(f32[32]{0:T(128)} %param.10) | copy-start | bytes 388
  6.5 9.3 %copy-start.13 = (s32[96,128]{1,0:T(8,128)S(1)}, s32[96,128]{1,0:T(8,128)}, u32[]{:S(2)}) copy-start(s32[96,128]{1,0:T(8,128)} %constant.41.clone) | copy-start | bytes 147460
  13.4 1.7 %collective-permute-start = (bf16[2,4,16,768]{3,2,1,0:T(8,128)(2,1)}, bf16[2,4,16,768]{3,2,1,0:T(8,128)(2,1)S(1)}, u32[]{:S(2)}, u32[]{:S(2)}) collective-permute-start(bf16[2,4,16,768]{3,2,1,0:T(8,128)(2,1)} %get-tuple-element.45), channel_id=1, source_target_pairs={{0,1},{1,0},{2,3},{3,2},{4,5},{5,4},{6,7},{7,6},{8,9},{9,8},{10,11... | collective-permute-start | bytes 589832 | tf_op jit(solution)/shard_map/ppermute | solution.py:82
  15.1 0.7 copy-start.8
  17.9 1.1 copy-start.3
  19.1 15.1 %collective-permute-start.1 = (bf16[2,4,16,768]{3,2,1,0:T(8,128)(2,1)}, bf16[2,4,16,768]{3,2,1,0:T(8,128)(2,1)S(1)}, u32[]{:S(2)}, u32[]{:S(2)}) collective-permute-start(bf16[2,4,16,768]{3,2,1,0:T(8,128)(2,1)} %get-tuple-element.57), channel_id=1, source_target_pairs={{0,2},{1,7},{2,4},{3,1},{4,6},{5,3},{6,0},{7,5},{8,10},{9,15},{10,... | collective-permute-start | bytes 589832 | tf_op jit(solution)/shard_map/ppermute | solution.py:82
  21.1 14.2 %collective-permute-start.2 = (bf16[2,4,16,768]{3,2,1,0:T(8,128)(2,1)}, bf16[2,4,16,768]{3,2,1,0:T(8,128)(2,1)S(1)}, u32[]{:S(2)}, u32[]{:S(2)}) collective-permute-start(bf16[2,4,16,768]{3,2,1,0:T(8,128)(2,1)} %get-tuple-element.58), channel_id=1, source_target_pairs={{0,6},{1,3},{2,0},{3,5},{4,2},{5,7},{6,4},{7,1},{8,14},{9,11},{10,... | collective-permute-start | bytes 589832 | tf_op jit(solution)/shard_map/ppermute | solution.py:82
  23.3 13.8 %collective-permute-start.3 = (bf16[2,4,16,768]{3,2,1,0:T(8,128)(2,1)}, bf16[2,4,16,768]{3,2,1,0:T(8,128)(2,1)S(1)}, u32[]{:S(2)}, u32[]{:S(2)}) collective-permute-start(bf16[2,4,16,768]{3,2,1,0:T(8,128)(2,1)} %get-tuple-element.59), channel_id=1, source_target_pairs={{0,3},{1,6},{2,5},{3,0},{4,7},{5,2},{6,1},{7,4},{8,11},{9,14},{10,... | collective-permute-start | bytes 589832 | tf_op jit(solution)/shard_map/ppermute | solution.py:82
  23.3 15.8 %collective-permute-start.4 = (bf16[2,4,16,768]{3,2,1,0:T(8,128)(2,1)}, bf16[2,4,16,768]{3,2,1,0:T(8,128)(2,1)S(1)}, u32[]{:S(2)}, u32[]{:S(2)}) collective-permute-start(bf16[2,4,16,768]{3,2,1,0:T(8,128)(2,1)} %get-tuple-element.60), channel_id=1, source_target_pairs={{0,7},{1,2},{2,1},{3,4},{4,3},{5,6},{6,5},{7,0},{8,15},{9,10},{10,... | collective-permute-start | bytes 589832 | tf_op jit(solution)/shard_map/ppermute | solution.py:82
  25.7 13.5 %collective-permute-start.5 = (bf16[2,4,16,768]{3,2,1,0:T(8,128)(2,1)}, bf16[2,4,16,768]{3,2,1,0:T(8,128)(2,1)S(1)}, u32[]{:S(2)}, u32[]{:S(2)}) collective-permute-start(bf16[2,4,16,768]{3,2,1,0:T(8,128)(2,1)} %get-tuple-element.61), channel_id=1, source_target_pairs={{0,4},{1,5},{2,6},{3,7},{4,0},{5,1},{6,2},{7,3},{8,12},{9,13},{10,... | collective-permute-start | bytes 589832 | tf_op jit(solution)/shard_map/ppermute | solution.py:82
  27.2 7.0 %copy-start.15 = (bf16[2,4,16,768]{3,2,1,0:T(8,128)(2,1)S(1)}, bf16[2,4,16,768]{3,2,1,0:T(8,128)(2,1)}, u32[]{:S(2)}) copy-start(bf16[2,4,16,768]{3,2,1,0:T(8,128)(2,1)} %get-tuple-element.62) | copy-start | bytes 589828
  27.2 32.4 %copy-start.7 = (bf16[2,4,16,768]{3,2,1,0:T(8,128)(2,1)S(1)}, bf16[2,4,16,768]{3,2,1,0:T(8,128)(2,1)}, u32[]{:S(2)}) copy-start(bf16[2,4,16,768]{3,2,1,0:T(8,128)(2,1)} %get-tuple-element.56.refs_0_) | copy-start | bytes 589828
  27.2 32.4 %copy-start.9 = (bf16[2,4,16,768]{3,2,1,0:T(8,128)(2,1)S(1)}, bf16[2,4,16,768]{3,2,1,0:T(8,128)(2,1)}, u32[]{:S(2)}) copy-start(bf16[2,4,16,768]{3,2,1,0:T(8,128)(2,1)} %copy-done.8) | copy-start | bytes 589828
  27.2 32.4 %copy-start.11 = (bf16[256,384]{1,0:T(8,128)(2,1)S(1)}, bf16[256,384]{1,0:T(8,128)(2,1)}, u32[]{:S(2)}) copy-start(bf16[256,384]{1,0:T(8,128)(2,1)} %constant.40.clone.analysis) | copy-start | bytes 589828
  27.2 32.4 %copy-start.12 = (bf16[384,256]{1,0:T(8,128)(2,1)S(1)}, bf16[384,256]{1,0:T(8,128)(2,1)}, u32[]{:S(2)}) copy-start(bf16[384,256]{1,0:T(8,128)(2,1)} %constant.39.clone.synth) | copy-start | bytes 589828
  34.2 8.6 %collective-permute-start.6 = (bf16[2,4,16,768]{3,2,1,0:T(8,128)(2,1)S(1)}, bf16[2,4,16,768]{3,2,1,0:T(8,128)(2,1)S(1)}, u32[]{:S(2)}, u32[]{:S(2)}) collective-permute-start(bf16[2,4,16,768]{3,2,1,0:T(8,128)(2,1)S(1)} %copy-done.15), channel_id=1, source_target_pairs={{0,5},{1,4},{2,7},{3,6},{4,1},{5,0},{6,3},{7,2},{8,13},{9,12},{10,... | collective-permute-start | bytes 589832 | tf_op jit(solution)/shard_map/ppermute | solution.py:82
  35.4 11.8 %collective-permute-start.7 = (bf16[2,4,16,768]{3,2,1,0:T(8,128)(2,1)}, bf16[2,4,16,768]{3,2,1,0:T(8,128)(2,1)S(1)}, u32[]{:S(2)}, u32[]{:S(2)}) collective-permute-start(bf16[2,4,16,768]{3,2,1,0:T(8,128)(2,1)} %get-tuple-element.66), channel_id=1, source_target_pairs={{0,2},{1,7},{2,4},{3,1},{4,6},{5,3},{6,0},{7,5},{8,10},{9,15},{10,... | collective-permute-start | bytes 589832 | tf_op jit(solution)/shard_map/ppermute | solution.py:82
  37.2 10.0 %collective-permute-start.8 = (bf16[2,4,16,768]{3,2,1,0:T(8,128)(2,1)}, bf16[2,4,16,768]{3,2,1,0:T(8,128)(2,1)S(1)}, u32[]{:S(2)}, u32[]{:S(2)}) collective-permute-start(bf16[2,4,16,768]{3,2,1,0:T(8,128)(2,1)} %get-tuple-element.67), channel_id=1, source_target_pairs={{0,6},{1,3},{2,0},{3,5},{4,2},{5,7},{6,4},{7,1},{8,14},{9,11},{10,... | collective-permute-start | bytes 589832 | tf_op jit(solution)/shard_map/ppermute | solution.py:82
  39.2 12.1 %collective-permute-start.9 = (bf16[2,4,16,768]{3,2,1,0:T(8,128)(2,1)}, bf16[2,4,16,768]{3,2,1,0:T(8,128)(2,1)S(1)}, u32[]{:S(2)}, u32[]{:S(2)}) collective-permute-start(bf16[2,4,16,768]{3,2,1,0:T(8,128)(2,1)} %get-tuple-element.68), channel_id=1, source_target_pairs={{0,3},{1,6},{2,5},{3,0},{4,7},{5,2},{6,1},{7,4},{8,11},{9,14},{10,... | collective-permute-start | bytes 589832 | tf_op jit(solution)/shard_map/ppermute | solution.py:82
  39.2 12.5 %collective-permute-start.10 = (bf16[2,4,16,768]{3,2,1,0:T(8,128)(2,1)}, bf16[2,4,16,768]{3,2,1,0:T(8,128)(2,1)S(1)}, u32[]{:S(2)}, u32[]{:S(2)}) collective-permute-start(bf16[2,4,16,768]{3,2,1,0:T(8,128)(2,1)} %get-tuple-element.69), channel_id=1, source_target_pairs={{0,7},{1,2},{2,1},{3,4},{4,3},{5,6},{6,5},{7,0},{8,15},{9,10},{10,... | collective-permute-start | bytes 589832 | tf_op jit(solution)/shard_map/ppermute | solution.py:82
  42.7 13.2 %collective-permute-start.11 = (bf16[2,4,16,768]{3,2,1,0:T(8,128)(2,1)}, bf16[2,4,16,768]{3,2,1,0:T(8,128)(2,1)S(1)}, u32[]{:S(2)}, u32[]{:S(2)}) collective-permute-start(bf16[2,4,16,768]{3,2,1,0:T(8,128)(2,1)} %get-tuple-element.70), channel_id=1, source_target_pairs={{0,4},{1,5},{2,6},{3,7},{4,0},{5,1},{6,2},{7,3},{8,12},{9,13},{10,... | collective-permute-start | bytes 589832 | tf_op jit(solution)/shard_map/ppermute | solution.py:82
  47.1 12.4 %collective-permute-start.12 = (bf16[2,4,16,768]{3,2,1,0:T(8,128)(2,1)}, bf16[2,4,16,768]{3,2,1,0:T(8,128)(2,1)S(1)}, u32[]{:S(2)}, u32[]{:S(2)}) collective-permute-start(bf16[2,4,16,768]{3,2,1,0:T(8,128)(2,1)} %get-tuple-element.71), channel_id=1, source_target_pairs={{0,5},{1,4},{2,7},{3,6},{4,1},{5,0},{6,3},{7,2},{8,13},{9,12},{10,... | collective-permute-start | bytes 589832 | tf_op jit(solution)/shard_map/ppermute | solution.py:82
  47.2 12.3 %collective-permute-start.13 = (bf16[2,4,16,768]{3,2,1,0:T(8,128)(2,1)}, bf16[2,4,16,768]{3,2,1,0:T(8,128)(2,1)S(1)}, u32[]{:S(2)}, u32[]{:S(2)}) collective-permute-start(bf16[2,4,16,768]{3,2,1,0:T(8,128)(2,1)} %get-tuple-element.72), channel_id=1, source_target_pairs={{0,1},{1,0},{2,3},{3,2},{4,5},{5,4},{6,7},{7,6},{8,9},{9,8},{10,11... | collective-permute-start | bytes 589832 | tf_op jit(solution)/shard_map/ppermute | solution.py:82
  59.6 0.9 copy-start.10
  66.3 8.1 %collective-permute-start.14 = (bf16[4,32,768]{2,1,0:T(8,128)(2,1)S(1)}, bf16[4,32,768]{2,1,0:T(8,128)(2,1)S(1)}, u32[]{:S(2)}, u32[]{:S(2)}) collective-permute-start(bf16[4,32,768]{2,1,0:T(8,128)(2,1)S(1)} %get-tuple-element.74), channel_id=1, source_target_pairs={{0,6},{1,3},{2,0},{3,5},{4,2},{5,7},{6,4},{7,1},{8,14},{9,11},{10,... | collective-permute-start | bytes 589832 | tf_op jit(solution)/shard_map/ppermute | solution.py:82
  69.2 8.7 %collective-permute-start.15 = (bf16[4,32,768]{2,1,0:T(8,128)(2,1)S(1)}, bf16[4,32,768]{2,1,0:T(8,128)(2,1)S(1)}, u32[]{:S(2)}, u32[]{:S(2)}) collective-permute-start(bf16[4,32,768]{2,1,0:T(8,128)(2,1)S(1)} %get-tuple-element.75), channel_id=1, source_target_pairs={{0,2},{1,7},{2,4},{3,1},{4,6},{5,3},{6,0},{7,5},{8,10},{9,15},{10,... | collective-permute-start | bytes 589832 | tf_op jit(solution)/shard_map/ppermute | solution.py:82
  69.2 13.5 %collective-permute-start.16 = (bf16[4,32,768]{2,1,0:T(8,128)(2,1)}, bf16[4,32,768]{2,1,0:T(8,128)(2,1)}, u32[]{:S(2)}, u32[]{:S(2)}) collective-permute-start(bf16[4,32,768]{2,1,0:T(8,128)(2,1)} %get-tuple-element.76), channel_id=1, source_target_pairs={{0,3},{1,6},{2,5},{3,0},{4,7},{5,2},{6,1},{7,4},{8,11},{9,14},{10,... | collective-permute-start | bytes 589832 | tf_op jit(solution)/shard_map/ppermute | solution.py:82
  69.2 17.4 %collective-permute-start.17 = (bf16[4,32,768]{2,1,0:T(8,128)(2,1)}, bf16[4,32,768]{2,1,0:T(8,128)(2,1)}, u32[]{:S(2)}, u32[]{:S(2)}) collective-permute-start(bf16[4,32,768]{2,1,0:T(8,128)(2,1)} %get-tuple-element.77), channel_id=1, source_target_pairs={{0,7},{1,2},{2,1},{3,4},{4,3},{5,6},{6,5},{7,0},{8,15},{9,10},{10,... | collective-permute-start | bytes 589832 | tf_op jit(solution)/shard_map/ppermute | solution.py:82
  71.0 15.6 %collective-permute-start.18 = (bf16[4,32,768]{2,1,0:T(8,128)(2,1)}, bf16[4,32,768]{2,1,0:T(8,128)(2,1)}, u32[]{:S(2)}, u32[]{:S(2)}) collective-permute-start(bf16[4,32,768]{2,1,0:T(8,128)(2,1)} %get-tuple-element.78), channel_id=1, source_target_pairs={{0,4},{1,5},{2,6},{3,7},{4,0},{5,1},{6,2},{7,3},{8,12},{9,13},{10,... | collective-permute-start | bytes 589832 | tf_op jit(solution)/shard_map/ppermute | solution.py:82
  74.5 13.5 %collective-permute-start.19 = (bf16[4,32,768]{2,1,0:T(8,128)(2,1)}, bf16[4,32,768]{2,1,0:T(8,128)(2,1)}, u32[]{:S(2)}, u32[]{:S(2)}) collective-permute-start(bf16[4,32,768]{2,1,0:T(8,128)(2,1)} %get-tuple-element.79), channel_id=1, source_target_pairs={{0,5},{1,4},{2,7},{3,6},{4,1},{5,0},{6,3},{7,2},{8,13},{9,12},{10,... | collective-permute-start | bytes 589832 | tf_op jit(solution)/shard_map/ppermute | solution.py:82
  77.9 0.7 copy-start.5
  78.5 9.5 %collective-permute-start.20 = (bf16[4,32,768]{2,1,0:T(8,128)(2,1)}, bf16[4,32,768]{2,1,0:T(8,128)(2,1)}, u32[]{:S(2)}, u32[]{:S(2)}) collective-permute-start(bf16[4,32,768]{2,1,0:T(8,128)(2,1)} %get-tuple-element.80), channel_id=1, source_target_pairs={{0,1},{1,0},{2,3},{3,2},{4,5},{5,4},{6,7},{7,6},{8,9},{9,8},{10,11... | collective-permute-start | bytes 589832 | tf_op jit(solution)/shard_map/ppermute | solution.py:82
  78.6 1.9 %copy-start.2 = (f32[64,96,128]{2,1,0:T(8,128)S(1)}, f32[64,96,128]{2,1,0:T(8,128)}, u32[]{:S(2)}) copy-start(f32[64,96,128]{2,1,0:T(8,128)} %all-gather.3.cloned.1.call-done) | copy-start | bytes 9437188
  80.5 7.5 %copy-start.1 = (f32[32,16,2,384]{3,2,1,0:T(2,128)S(1)}, f32[32,16,2,384]{3,2,1,0:T(2,128)}, u32[]{:S(2)}) copy-start(f32[32,16,2,384]{3,2,1,0:T(2,128)} %field.5) | copy-start | bytes 4718596
  80.5 7.5 %copy-start.4 = (f32[32,96,128]{2,1,0:T(8,128)S(1)}, f32[32,96,128]{2,1,0:T(8,128)}, u32[]{:S(2)}) copy-start(f32[32,96,128]{2,1,0:T(8,128)} %copy-done.3) | copy-start | bytes 4718596
  88.0 3.7 %copy-start = (bf16[16,384,768]{2,1,0:T(8,128)(2,1)S(1)}, bf16[16,384,768]{2,1,0:T(8,128)(2,1)}, u32[]{:S(2)}) copy-start(bf16[16,384,768]{2,1,0:T(8,128)(2,1)} %legendre.5) | copy-start | bytes 28311556
  91.7 0.9 copy-start.6
  98.9 5.3 %collective-permute-start.23 = (bf16[2,96,128]{2,1,0:T(8,128)(2,1)S(1)}, bf16[2,96,128]{2,1,0:T(8,128)(2,1)S(1)}, u32[]{:S(2)}, u32[]{:S(2)}) collective-permute-start(bf16[2,96,128]{2,1,0:T(8,128)(2,1)S(1)} %get-tuple-element.81.a), channel_id=1, source_target_pairs={{0,24},{8,0},{16,8},{24,16},{1,25},{9,1},{17,9},{25,17},{2,26},{10... | collective-permute-start | bytes 147464 | tf_op jit(solution)/shard_map/ppermute | solution.py:490
  101.9 5.8 %collective-permute-start.22 = (bf16[2,96,128]{2,1,0:T(8,128)(2,1)S(1)}, bf16[2,96,128]{2,1,0:T(8,128)(2,1)S(1)}, u32[]{:S(2)}, u32[]{:S(2)}) collective-permute-start(bf16[2,96,128]{2,1,0:T(8,128)(2,1)S(1)} %get-tuple-element.81.a), channel_id=1, source_target_pairs={{0,16},{8,24},{16,0},{24,8},{1,17},{9,25},{17,1},{25,9},{2,18},{10... | collective-permute-start | bytes 147464 | tf_op jit(solution)/shard_map/ppermute | solution.py:490
  102.6 5.6 %collective-permute-start.21 = (bf16[2,96,128]{2,1,0:T(8,128)(2,1)S(1)}, bf16[2,96,128]{2,1,0:T(8,128)(2,1)S(1)}, u32[]{:S(2)}, u32[]{:S(2)}) collective-permute-start(bf16[2,96,128]{2,1,0:T(8,128)(2,1)S(1)} %get-tuple-element.81.a), channel_id=1, source_target_pairs={{0,8},{8,16},{16,24},{24,0},{1,9},{9,17},{17,25},{25,1},{2,10},{10... | collective-permute-start | bytes 147464 | tf_op jit(solution)/shard_map/ppermute | solution.py:490
  109.4 4.6 %collective-permute-start.26 = (bf16[2,96,128]{2,1,0:T(8,128)(2,1)S(1)}, bf16[2,96,128]{2,1,0:T(8,128)(2,1)S(1)}, u32[]{:S(2)}, u32[]{:S(2)}) collective-permute-start(bf16[2,96,128]{2,1,0:T(8,128)(2,1)S(1)} %inner_join.1.e), channel_id=1, source_target_pairs={{0,96},{32,0},{64,32},{96,64},{1,97},{33,1},{65,33},{97,65},{2,98}... | collective-permute-start | bytes 147464 | tf_op jit(solution)/shard_map/ppermute | solution.py:490
  112.2 5.6 %collective-permute-start.25 = (bf16[2,96,128]{2,1,0:T(8,128)(2,1)S(1)}, bf16[2,96,128]{2,1,0:T(8,128)(2,1)S(1)}, u32[]{:S(2)}, u32[]{:S(2)}) collective-permute-start(bf16[2,96,128]{2,1,0:T(8,128)(2,1)S(1)} %inner_join.1.e), channel_id=1, source_target_pairs={{0,64},{32,96},{64,0},{96,32},{1,65},{33,97},{65,1},{97,33},{2,66}... | collective-permute-start | bytes 147464 | tf_op jit(solution)/shard_map/ppermute | solution.py:490
  113.0 5.3 %collective-permute-start.24 = (bf16[2,96,128]{2,1,0:T(8,128)(2,1)S(1)}, bf16[2,96,128]{2,1,0:T(8,128)(2,1)S(1)}, u32[]{:S(2)}, u32[]{:S(2)}) collective-permute-start(bf16[2,96,128]{2,1,0:T(8,128)(2,1)S(1)} %inner_join.1.e), channel_id=1, source_target_pairs={{0,32},{32,64},{64,96},{96,0},{1,33},{33,65},{65,97},{97,1},{2,34}... | collective-permute-start | bytes 147464 | tf_op jit(solution)/shard_map/ppermute | solution.py:490
Sparse Core Ops, SparseCore 0:
  19.2 50.3 all-gather.2

commit v3 on v2

--- a/solution.py
+++ b/solution.py
@@ -52,8 +52,13 @@
     return synth.T.copy(), (analysis.astype(np.float32) * step).astype(ml_dtypes.bfloat16)
 
 
+def row_of(order, tile, half):
+    return (order * TILES + tile) * HALVES + half
+
+
 HALF = ORD // 2
 PAIRS_HALF = HALF * HALVES
+AHEAD = 7
 
 
 def moved(device, k, back):
@@ -94,11 +99,13 @@
         pltpu.make_async_copy(legendre.at[half * HALF + m], table.at[m], table_sems.at[m])
         for m in range(HALF)
     ]
-    for copy in copies + tables:
+    for copy in copies + tables[:AHEAD]:
         copy.start()
     for copy in copies:
         copy.wait()
     for m in range(HALF):
+        if m + AHEAD < HALF:
+            tables[m + AHEAD].start()
         spectral = jnp.concatenate(
             [source[:, m].reshape(SHELLS * HALVES, DEG) for source in (fields, flows)], axis=0
         ).astype(BF16)
@@ -134,7 +141,7 @@
             pltpu.SemaphoreType.DMA((HALF,)),
             pltpu.SemaphoreType.DMA((NMODE,)),
         ],
-        compiler_params=params(),
+        compiler_params=params(58),
         cost_estimate=cost(2 * 128 * DEG * NLAT * HALF, 8_000_000),
         name="synthesis",
     )(me, field, flow, legendre)
@@ -181,13 +188,13 @@
             pltpu.SemaphoreType.DMA((NMODE, 2)),
             pltpu.SemaphoreType.DMA((NSHELL, NMODE)),
         ],
-        compiler_params=params(16),
+        compiler_params=params(58),
         cost_estimate=cost(3 * 2 * POINTS * 256 * NLAT * NSHELL, 5_000_000),
         name="grid_product",
     )(me, synth, analysis, *firsts, *seconds)
 
 
-def block_matrix_kernel(shell, angular, pivots, left, right, ends):
+def block_matrix_kernel(shell, angular, pivots, left, right):
     ang = angular[...]
     ratio = jnp.zeros((ROWS, LANES), F32)
     answer = jnp.ones((ROWS, LANES), F32)
@@ -203,25 +210,21 @@
     before = left[SHELLS - 1]
     behind = ratio
     right[SHELLS - 1] = behind
-    ends[2] = before
-    ends[3] = behind
     for i in reversed(range(SHELLS - 1)):
         ratio = shell[2, i] * pivots[i]
         before = left[i] + ratio * before
         behind = ratio * behind
         left[i] = before
         right[i] = behind
-    ends[0] = before
-    ends[1] = behind
 
 
 def block_matrix(shell, angular):
     big = jax.ShapeDtypeStruct((SHELLS, ROWS, LANES), F32)
     return pl.pallas_call(
         block_matrix_kernel,
-        out_shape=(big, big, big, jax.ShapeDtypeStruct((4, ROWS, LANES), F32)),
+        out_shape=(big, big, big),
         in_specs=[whole(pltpu.SMEM), whole()],
-        out_specs=(whole(),) * 4,
+        out_specs=(whole(),) * 3,
         compiler_params=params(16),
         cost_estimate=cost(10_000_000, 6_000_000),
         name="block_matrix",
@@ -259,75 +262,136 @@
     return links, (before, behind, alpha, beta)
 
 
-def level_kernel(place, ends, inner, outer, held):
-    supers = []
-    for x in range(CHAIN):
-        links, own = chain_matrix(
-            [tuple(ends[x * CHAIN + k, n] for n in range(4)) for k in range(CHAIN)]
-        )
-        supers.append(own)
-        for k in range(CHAIN):
-            for n in range(6):
-                held[x, k, n] = links[k][n]
-    links, _ = chain_matrix(supers)
+DEGREES = 512
+LINKS = 6
+
+
+def level_kernel(where, diffusivity, inner, outer, ordered, factors, links_held, table):
+    x, y, mode = where[0], where[1], where[2]
     for k in range(CHAIN):
-        for n in range(6):
-            outer[k, n] = links[k][n]
-    inner[...] = held[place[0]]
-
-
-def levels(place, ends):
-    rows = 8
-    shape = jax.ShapeDtypeStruct((CHAIN, 6, ROWS, LANES), F32)
-    spec = pl.BlockSpec((CHAIN, 6, rows, LANES), lambda i: (0, 0, i, 0))
-    return pl.pallas_call(
+        for first in range(8):
+            slot = lax.rem(x + CHAIN - first % CHAIN, CHAIN) * CHAIN + lax.rem(y + CHAIN - k, CHAIN)
+            ordered[k, first : first + 1, :] = diffusivity[pl.ds(slot, 1), :]
+    degree = lax.broadcasted_iota(jnp.int32, (1, 1, DEGREES), 2).astype(F32)
+    angular = degree * (degree + 1.0)
+    shape = (CHAIN, 8, 1)
+    block = lax.broadcasted_iota(jnp.int32, shape, 1) % CHAIN * CHAIN
+    block = block + lax.broadcasted_iota(jnp.int32, shape, 0)
+    total = CHAIN * CHAIN * SHELLS
+
+    def kappas(i):
+        kappa = ordered[:, :, i : i + 1]
+        low, up = kappa, kappa
+        if i == 0:
+            low = jnp.where(block == 0, 0.0, kappa)
+        if i == SHELLS - 1:
+            up = jnp.where(block == CHAIN * CHAIN - 1, 0.0, kappa)
+        return kappa, low, up
+
+    ratio = jnp.zeros((CHAIN, 8, DEGREES), F32)
+    answer = jnp.ones((CHAIN, 8, DEGREES), F32)
+    for i in range(SHELLS):
+        kappa, low, up = kappas(i)
+        radius = (total * 7 // 13 + block * SHELLS + i).astype(F32)
+        diagonal = 1.0 + 2.0 * kappa + kappa * angular / (radius * radius)
+        inverse = 1.0 / (diagonal - low * ratio)
+        ratio = up * inverse
+        answer = low * inverse * answer
+        factors[0, i] = ratio
+        factors[1, i] = answer
+    before, behind = answer, ratio
+    last_left, last_right = before, behind
+    for i in reversed(range(SHELLS - 1)):
+        before = factors[1, i] + factors[0, i] * before
+        behind = factors[0, i] * behind
+    ends = (before, behind, last_left, last_right)
+    links, supers = chain_matrix([tuple(end[k] for end in ends) for k in range(CHAIN)])
+    for k in range(CHAIN):
+        for n in range(LINKS):
+            links_held[k * LINKS + n] = links[k][n]
+    far, _ = chain_matrix([tuple(end[k : k + 1] for end in supers) for k in range(CHAIN)])
+    for k in range(CHAIN):
+        for n in range(LINKS):
+            row = k * LINKS + n
+            table[row : row + 1, :] = links_held[row, pl.ds(x, 1), :]
+            row_far = CHAIN * LINKS + row
+            table[row_far : row_far + 1, :] = far[k][n]
+    values = table[...]
+    count = CHAIN * LINKS
+    for m in range(ORD):
+        here = pltpu.roll(values, DEGREES - (mode * ORD + m), 1)
+        for tile in range(TILES):
+            found = here[:, tile * LANES : (tile + 1) * LANES]
+            for half in range(HALVES):
+                rows = pl.ds(row_of(m, tile, half), count, stride=ROWS)
+                inner[rows, :] = found[:count]
+                outer[rows, :] = found[count:]
+
+
+def levels(where, diffusivity):
+    count = CHAIN * LINKS
+    shape = jax.ShapeDtypeStruct((count * ROWS, LANES), F32)
+    outs = pl.pallas_call(
         level_kernel,
         out_shape=(shape, shape),
-        grid=(ROWS // rows,),
-        in_specs=[
-            whole(pltpu.SMEM),
-            pl.BlockSpec((CHAIN * CHAIN, 4, rows, LANES), lambda i: (0, 0, i, 0)),
+        in_specs=[whole(pltpu.SMEM), whole()],
+        out_specs=(whole(), whole()),
+        scratch_shapes=[
+            pltpu.VMEM((CHAIN, 8, SHELLS), F32),
+            pltpu.VMEM((2, SHELLS, CHAIN, 8, DEGREES), F32),
+            pltpu.VMEM((count, 8, DEGREES), F32),
+            pltpu.VMEM((2 * count, DEGREES), F32),
         ],
-        out_specs=(spec, spec),
-        scratch_shapes=[pltpu.VMEM((CHAIN, CHAIN, 6, rows, LANES), F32)],
-        compiler_params=params(12),
+        compiler_params=params(20),
         cost_estimate=cost(10_000_000, 8_000_000),
         name="levels",
-    )(place, ends)
+    )(where, diffusivity)
+    return [out.reshape(CHAIN, LINKS, ROWS, LANES) for out in outs]
 
 
 def forcing_kernel(me, shell, field, pivots, legendre, *refs):
     slots = refs[:NMODE]
-    solved, ends, modes, sems = refs[NMODE:]
+    solved, ends, modes, table, fields, inverses, sems, table_sems = refs[NMODE:]
     copies = [
         pltpu.make_async_copy(
             slots[k], modes.at[pl.ds(moved(me[0], k, False) * NSHELL, NSHELL)], sems.at[k]
         )
         for k in range(NMODE)
     ]
-    for copy in copies:
+    copies.append(pltpu.make_async_copy(field, fields, sems.at[NMODE]))
+    last = pltpu.make_async_copy(pivots, inverses, sems.at[NMODE + 1])
+    tables = [
+        pltpu.make_async_copy(legendre.at[m], table.at[m], table_sems.at[m]) for m in range(ORD)
+    ]
+    for copy in copies + tables[:AHEAD]:
         copy.start()
     for copy in copies:
         copy.wait()
     for m in range(ORD):
+        if m + AHEAD < ORD:
+            tables[m + AHEAD].start()
+        if m == ORD // 2:
+            last.start()
+        tables[m].wait()
         lat = modes[:, HALVES * m : HALVES * (m + 1), :].reshape(SHELLS * HALVES, NLAT)
         forcing = lax.dot_general(
-            lat, legendre[m], (((1,), (1,)), ((), ())), preferred_element_type=F32
+            lat, table[m], (((1,), (1,)), ((), ())), preferred_element_type=F32
         )
-        right_side = field[:, m].reshape(SHELLS * HALVES, DEG) + forcing
+        right_side = fields[:, m].reshape(SHELLS * HALVES, DEG) + forcing
         for tile in range(TILES):
             row = (m * TILES + tile) * HALVES
             solved[:, row : row + HALVES, :] = right_side[
                 :, tile * LANES : (tile + 1) * LANES
             ].reshape(SHELLS, HALVES, LANES)
-    value = solved[0] * pivots[0]
+    last.wait()
+    value = solved[0] * inverses[0]
     solved[0] = value
     for i in range(1, SHELLS):
-        value = (solved[i] + shell[1, i] * value) * pivots[i]
+        value = (solved[i] + shell[1, i] * value) * inverses[i]
         solved[i] = value
     ends[1] = value.astype(BF16)
     for i in reversed(range(SHELLS - 1)):
-        value = solved[i] + (shell[2, i] * pivots[i]) * value
+        value = solved[i] + (shell[2, i] * inverses[i]) * value
         solved[i] = value
     ends[0] = value.astype(BF16)
 
@@ -339,13 +403,17 @@
             jax.ShapeDtypeStruct((SHELLS, ROWS, LANES), F32),
             jax.ShapeDtypeStruct((2, ROWS, LANES), BF16),
         ),
-        in_specs=[whole(pltpu.SMEM)] * 2 + [whole()] * 3 + [whole(pl.ANY)] * NMODE,
+        in_specs=[whole(pltpu.SMEM)] * 2 + [whole(pl.ANY)] * (3 + NMODE),
         out_specs=(whole(), whole()),
         scratch_shapes=[
             pltpu.VMEM((SHELLS, PAIRS, NLAT), BF16),
-            pltpu.SemaphoreType.DMA((NMODE,)),
+            pltpu.VMEM((ORD, DEG, NLAT), BF16),
+            pltpu.VMEM((SHELLS, ORD, HALVES, DEG), F32),
+            pltpu.VMEM((SHELLS, ROWS, LANES), F32),
+            pltpu.SemaphoreType.DMA((NMODE + 2,)),
+            pltpu.SemaphoreType.DMA((ORD,)),
         ],
-        compiler_params=params(24),
+        compiler_params=params(58),
         cost_estimate=cost(2 * 64 * DEG * NLAT * ORD, 16_000_000),
         name="forcing_solve",
     )(me, shell, field, pivots, legendre, *slots)
@@ -502,7 +570,7 @@
     later, firsts[0] = lax.optimization_barrier((me, firsts[0]))
     seconds = synthesis(1, later, scalar_field, radial_flow, legendre)
     firsts, seconds = moved_all(firsts, False), moved_all(seconds, False)
-    diffusivity, mode, firsts[7] = lax.optimization_barrier((diffusivity, mode, firsts[7]))
+    diffusivity, mode, firsts[4] = lax.optimization_barrier((diffusivity, mode, firsts[4]))
 
     nr_total = SHELLS * CHAIN * CHAIN
     place = jnp.stack([lax.axis_index(RADIAL[0]), lax.axis_index(RADIAL[1])]).astype(jnp.int32)
@@ -520,8 +588,10 @@
     local_degree = row // (TILES * HALVES) + row // HALVES % TILES * LANES + np.arange(LANES)[None]
     degree = (local_degree + mode * ORD).astype(F32)
     angular = degree * (degree + 1.0)
-    pivots, left, right, ends = block_matrix(shell, angular)
-    inner, outer = levels(place, lax.all_gather(ends, RADIAL))
+    pivots, left, right = block_matrix(shell, angular)
+    near = jnp.concatenate(ring(diffusivity.reshape(1, SHELLS), RADIAL[1]))
+    blocks = jnp.concatenate(ring(near, RADIAL[0]))
+    inner, outer = levels(jnp.concatenate([place, mode.reshape(1)]), blocks)
 
     modes = moved_all(grid_product(me, synth, analysis, firsts, seconds), True)
     pivots, inner, outer = lax.optimization_barrier((pivots, inner, outer))

time: 129 us -> 116 us (0.90)
  between operations: 13.6 us -> 0.54 us
  waiting for transfers between devices: 35.6 us -> 26.3 us
  starting transfers between devices: 34.7 us -> 42.6 us
  Pallas kernels: 34.9 us -> 40.6 us
  local copies, waits for them, and re-layouts: 9.95 us -> 5.47 us
    ppermute x21, waiting for transfers between devices: 26.5 us -> 12.5 us  [moved_all(): sent.append(lax.ppermute(arrays[k], MODE, pairs))]
    ppermute x6 -> x12, starting transfers between devices: 9.22 us -> 18.1 us  [shifted(): lax.ppermute(array, axis, [(i, (i + step) % size) for i in range(size)])]
    unnamed x32 -> x60, local copies, waits for them, and re-layouts: 9.95 us -> 4.08 us
    pallas_call x1, Pallas kernels: 6.23 us -> 11.5 us  [forcing_solve(): pl.pallas_call(forcing_kernel, out_shape=(jax.ShapeDtypeStruct((SHELLS, R...]
    ppermute x6 -> x12, waiting for transfers between devices: 9.1 us -> 13.8 us  [shifted(): lax.ppermute(array, axis, [(i, (i + step) % size) for i in range(size)])]
    concatenate x0 -> x1, local copies, waits for them, and re-layouts: none -> 1.39 us  [on_device(): blocks = jnp.concatenate(ring(near, RADIAL[0]))]
  transfers between devices with their start and end apart: 28 -> 33, of which waited for: 17 -> 15; matrix products, arithmetic and copies ran while one was open for 0% -> 1% of each run, Pallas kernels for 12% -> 15%
where the time goes in v3:
time: 116 us
  starting transfers between devices  42.6 us (37%)
  Pallas kernels  40.6 us (35%)
  waiting for transfers between devices  26.3 us (23%)
  local copies, waits for them, and re-layouts  5.47 us (5%)
    ppermute x21, starting transfers between devices, moved_all(): sent.append(lax.ppermute(arrays[k], MODE, pairs))  24.5 us
    ppermute x12, starting transfers between devices, shifted(): lax.ppermute(array, axis, [(i, (i + step) % size) for i in range(size)])  18.1 us
    ppermute x12, waiting for transfers between devices, shifted(): lax.ppermute(array, axis, [(i, (i + step) % size) for i in range(size)])  13.8 us
    pallas_call x2, Pallas kernels, synthesis(): pl.pallas_call(functools.partial(synthesis_kernel, half), out_shape=(shap...  13.4 us
    ppermute x21, waiting for transfers between devices, moved_all(): sent.append(lax.ppermute(arrays[k], MODE, pairs))  12.5 us
    pallas_call x1, Pallas kernels, forcing_solve(): pl.pallas_call(forcing_kernel, out_shape=(jax.ShapeDtypeStruct((SHELLS, R...  11.5 us
    pallas_call x1, Pallas kernels, grid_product(): pl.pallas_call(grid_kernel, out_shape=(shape,) * NMODE, in_specs=[whole(p...  6.63 us
    unnamed x60, local copies, waits for them, and re-layouts  4.08 us
  transfers between devices with their start and end apart: 33, of which 15 were waited for; matrix products, arithmetic and copies ran while one was open for 1% of the time, Pallas kernels for 15%

profile of v3, /device:TPU:0, one launch (start us, length us, event | category | flops | bytes accessed | tf_op | source)
XLA Modules:
  0.0 115.7 jit_solution(5304584315020345686)
XLA Ops:
  0.0 6.6 %synthesis.2 = (bf16[2,4,16,768]{3,2,1,0:T(8,128)(2,1)}, bf16[2,4,16,768]{3,2,1,0:T(8,128)(2,1)}, bf16[2,4,16,768]{3,2,1,0:T(8,128)(2,1)}, bf16[2,4,16,768]{3,2,...) custom-call(s32[1]{0:T(128)} %bitcast.2.me, ...), custom_call_target="tpu_custom_call" | custom-call | flops 603979776 | bytes 8000000 | tf_op jit(solution)/shard_map/synthesis/pallas_call | solution.py:130
  6.6 3.6 %collective-permute-start = (bf16[2,4,16,768]{3,2,1,0:T(8,128)(2,1)}, bf16[2,4,16,768]{3,2,1,0:T(8,128)(2,1)S(1)}, u32[]{:S(2)}, u32[]{:S(2)}) collective-permute-start(bf16[2,4,16,768]{3,2,1,0:T(8,128)(2,1)} %get-tuple-element.44), channel_id=1, source_target_pairs={{0,7},{1,2},{2,1},{3,4},{4,3},{5,6},{6,5},{7,0},{8,15},{9,10},{10,... | collective-permute-start | bytes 589832 | tf_op jit(solution)/shard_map/ppermute | solution.py:87
  10.3 0.0 collective-permute-start.7
  10.3 3.2 %collective-permute-start.8 = (bf16[2,4,16,768]{3,2,1,0:T(8,128)(2,1)}, bf16[2,4,16,768]{3,2,1,0:T(8,128)(2,1)S(1)}, u32[]{:S(2)}, u32[]{:S(2)}) collective-permute-start(bf16[2,4,16,768]{3,2,1,0:T(8,128)(2,1)} %get-tuple-element.56), channel_id=1, source_target_pairs={{0,6},{1,3},{2,0},{3,5},{4,2},{5,7},{6,4},{7,1},{8,14},{9,11},{10,... | collective-permute-start | bytes 589832 | tf_op jit(solution)/shard_map/ppermute | solution.py:87
  13.5 0.0 collective-permute-start.9
  13.5 1.0 collective-permute-start.10
  14.5 6.7 %synthesis.3 = (bf16[2,4,16,768]{3,2,1,0:T(8,128)(2,1)}, bf16[2,4,16,768]{3,2,1,0:T(8,128)(2,1)}, bf16[2,4,16,768]{3,2,1,0:T(8,128)(2,1)}, bf16[2,4,16,768]{3,2,...) custom-call(s32[1]{0:T(128)} %bitcast.2.me, ...), custom_call_target="tpu_custom_call" | custom-call | flops 603979776 | bytes 8000000 | tf_op jit(solution)/shard_map/synthesis/pallas_call | solution.py:130
  21.3 2.1 %collective-permute-start.11 = (bf16[2,4,16,768]{3,2,1,0:T(8,128)(2,1)S(1)}, bf16[2,4,16,768]{3,2,1,0:T(8,128)(2,1)S(1)}, u32[]{:S(2)}, u32[]{:S(2)}) collective-permute-start(bf16[2,4,16,768]{3,2,1,0:T(8,128)(2,1)S(1)} %copy-done.24), channel_id=1, source_target_pairs={{0,5},{1,4},{2,7},{3,6},{4,1},{5,0},{6,3},{7,2},{8,13},{9,12},{10,... | collective-permute-start | bytes 589832 | tf_op jit(solution)/shard_map/ppermute | solution.py:87
  23.4 0.7 collective-permute-start.12
  24.1 0.0 collective-permute-done.8.refs_2_
  24.1 1.4 %collective-permute-start.13 = (bf16[2,4,16,768]{3,2,1,0:T(8,128)(2,1)}, bf16[2,4,16,768]{3,2,1,0:T(8,128)(2,1)S(1)}, u32[]{:S(2)}, u32[]{:S(2)}) collective-permute-start(bf16[2,4,16,768]{3,2,1,0:T(8,128)(2,1)} %get-tuple-element.64), channel_id=1, source_target_pairs={{0,2},{1,7},{2,4},{3,1},{4,6},{5,3},{6,0},{7,5},{8,10},{9,15},{10,... | collective-permute-start | bytes 589832 | tf_op jit(solution)/shard_map/ppermute | solution.py:87
  25.6 1.9 %collective-permute-start.14 = (bf16[2,4,16,768]{3,2,1,0:T(8,128)(2,1)}, bf16[2,4,16,768]{3,2,1,0:T(8,128)(2,1)S(1)}, u32[]{:S(2)}, u32[]{:S(2)}) collective-permute-start(bf16[2,4,16,768]{3,2,1,0:T(8,128)(2,1)} %get-tuple-element.65), channel_id=1, source_target_pairs={{0,6},{1,3},{2,0},{3,5},{4,2},{5,7},{6,4},{7,1},{8,14},{9,11},{10,... | collective-permute-start | bytes 589832 | tf_op jit(solution)/shard_map/ppermute | solution.py:87
  27.5 0.0 collective-permute-done.10.refs_5_
  27.5 0.1 collective-permute-start.15
  27.6 2.6 %collective-permute-done.11.refs_6_ = bf16[2,4,16,768]{3,2,1,0:T(8,128)(2,1)S(1)} collective-permute-done((bf16[2,4,16,768]{3,2,1,0:T(8,128)(2,1)S(1)}, bf16[2,4,16,768]{3,2,1,0:T(8,128)(2,1)S(1)}, u32[]{:S(2)}, u32[]{:S(2)}) %collective-permute-start.11) | collective-permute-done | bytes 196640 | tf_op jit(solution)/shard_map/ppermute | solution.py:87
  30.2 2.9 %collective-permute-start.16 = (bf16[2,4,16,768]{3,2,1,0:T(8,128)(2,1)}, bf16[2,4,16,768]{3,2,1,0:T(8,128)(2,1)S(1)}, u32[]{:S(2)}, u32[]{:S(2)}) collective-permute-start(bf16[2,4,16,768]{3,2,1,0:T(8,128)(2,1)} %get-tuple-element.67), channel_id=1, source_target_pairs={{0,7},{1,2},{2,1},{3,4},{4,3},{5,6},{6,5},{7,0},{8,15},{9,10},{10,... | collective-permute-start | bytes 589832 | tf_op jit(solution)/shard_map/ppermute | solution.py:87
  33.1 1.4 %collective-permute-done.13.refs_9_ = bf16[2,4,16,768]{3,2,1,0:T(8,128)(2,1)S(1)} collective-permute-done((bf16[2,4,16,768]{3,2,1,0:T(8,128)(2,1)}, bf16[2,4,16,768]{3,2,1,0:T(8,128)(2,1)S(1)}, u32[]{:S(2)}, u32[]{:S(2)}) %collective-permute-start.13) | collective-permute-done | bytes 196640 | tf_op jit(solution)/shard_map/ppermute | solution.py:87
  34.5 0.7 collective-permute-done.14.refs_10_
  35.2 1.6 %collective-permute-start.19 = (bf16[2,4,16,768]{3,2,1,0:T(8,128)(2,1)}, bf16[2,4,16,768]{3,2,1,0:T(8,128)(2,1)S(1)}, u32[]{:S(2)}, u32[]{:S(2)}) collective-permute-start(bf16[2,4,16,768]{3,2,1,0:T(8,128)(2,1)} %get-tuple-element.70), channel_id=1, source_target_pairs={{0,1},{1,0},{2,3},{3,2},{4,5},{5,4},{6,7},{7,6},{8,9},{9,8},{10,11... | collective-permute-start | bytes 589832 | tf_op jit(solution)/shard_map/ppermute | solution.py:87
  36.9 0.4 collective-permute-done.15.refs_11_
  37.3 3.0 %collective-permute-start.3 = (f32[1,32]{1,0:T(1,128)S(1)}, f32[1,32]{1,0:T(1,128)S(1)}, u32[]{:S(2)}, u32[]{:S(2)}) collective-permute-start(f32[1,32]{1,0:T(1,128)S(1)} %bitcast.15), channel_id=1, source_target_pairs={{0,24},{8,0},{16,8},{24,16},{1,25},{9,1},{17,9},{25,17},{2,26},{10... | collective-permute-start | bytes 392 | tf_op jit(solution)/shard_map/ppermute | solution.py:558
  40.3 2.0 %collective-permute-start.2 = (f32[1,32]{1,0:T(1,128)S(1)}, f32[1,32]{1,0:T(1,128)S(1)}, u32[]{:S(2)}, u32[]{:S(2)}) collective-permute-start(f32[1,32]{1,0:T(1,128)S(1)} %bitcast.16), channel_id=1, source_target_pairs={{0,16},{8,24},{16,0},{24,8},{1,17},{9,25},{17,1},{25,9},{2,18},{10... | collective-permute-start | bytes 392 | tf_op jit(solution)/shard_map/ppermute | solution.py:558
  42.3 1.0 collective-permute-done.17.refs_13_
  43.3 1.6 %collective-permute-start.1 = (f32[1,32]{1,0:T(1,128)S(1)}, f32[1,32]{1,0:T(1,128)S(1)}, u32[]{:S(2)}, u32[]{:S(2)}) collective-permute-start(f32[1,32]{1,0:T(1,128)S(1)} %bitcast.17), channel_id=1, source_target_pairs={{0,8},{8,16},{16,24},{24,0},{1,9},{9,17},{17,25},{25,1},{2,10},{10... | collective-permute-start | bytes 392 | tf_op jit(solution)/shard_map/ppermute | solution.py:558
  44.9 1.9 %collective-permute-done.18.refs_14_ = bf16[2,4,16,768]{3,2,1,0:T(8,128)(2,1)S(1)} collective-permute-done((bf16[2,4,16,768]{3,2,1,0:T(8,128)(2,1)}, bf16[2,4,16,768]{3,2,1,0:T(8,128)(2,1)S(1)}, u32[]{:S(2)}, u32[]{:S(2)}) %collective-permute-start.18) | collective-permute-done | bytes 196640 | tf_op jit(solution)/shard_map/ppermute | solution.py:87
  46.9 0.6 copy-done.28
  47.5 0.1 copy-done.29
  47.6 6.6 %grid_product.1 = (bf16[4,32,768]{2,1,0:T(8,128)(2,1)}, bf16[4,32,768]{2,1,0:T(8,128)(2,1)}, bf16[4,32,768]{2,1,0:T(8,128)(2,1)}, bf16[4,32,768]{2,1,0:T(8,128)(...) custom-call(s32[1]{0:T(128)} %bitcast.2.me, ...), custom_call_target="tpu_custom_call" | custom-call | flops 1811939328 | bytes 5000000 | tf_op jit(solution)/shard_map/grid_product/pallas_call | solution.py:180
  54.2 1.2 %collective-permute-start.20 = (bf16[4,32,768]{2,1,0:T(8,128)(2,1)}, bf16[4,32,768]{2,1,0:T(8,128)(2,1)S(1)}, u32[]{:S(2)}, u32[]{:S(2)}) collective-permute-start(bf16[4,32,768]{2,1,0:T(8,128)(2,1)} %get-tuple-element.72), channel_id=1, source_target_pairs={{0,6},{1,3},{2,0},{3,5},{4,2},{5,7},{6,4},{7,1},{8,14},{9,11},{10,... | collective-permute-start | bytes 589832 | tf_op jit(solution)/shard_map/ppermute | solution.py:87
  55.4 0.9 collective-permute-start.21
  56.4 2.8 %collective-permute-start.6 = (f32[4,32]{1,0:T(4,128)S(1)}, f32[4,32]{1,0:T(4,128)S(1)}, u32[]{:S(2)}, u32[]{:S(2)}) collective-permute-start(f32[4,32]{1,0:T(4,128)S(1)} %get-tuple-element.83), channel_id=1, source_target_pairs={{0,96},{32,0},{64,32},{96,64},{1,97},{33,1},{65,33},{97,65},{2,98}... | collective-permute-start | bytes 1544 | tf_op jit(solution)/shard_map/ppermute | solution.py:558
  59.2 0.8 collective-permute-start.5
  60.0 0.9 collective-permute-start.4
  60.9 0.1 pad_add_fusion.1.where
  61.0 0.1 collective-permute-start.22
  61.1 3.2 %collective-permute-done.5 = f32[4,32]{1,0:T(4,128)S(1)} collective-permute-done((f32[4,32]{1,0:T(4,128)S(1)}, f32[4,32]{1,0:T(4,128)S(1)}, u32[]{:S(2)}, u32[]{:S(2)}) %collective-permute-start.5) | collective-permute-done | bytes 544 | tf_op jit(solution)/shard_map/ppermute | solution.py:558
  64.3 0.5 collective-permute-done.4
  64.8 2.6 %collective-permute-start.24 = (bf16[4,32,768]{2,1,0:T(8,128)(2,1)}, bf16[4,32,768]{2,1,0:T(8,128)(2,1)}, u32[]{:S(2)}, u32[]{:S(2)}) collective-permute-start(bf16[4,32,768]{2,1,0:T(8,128)(2,1)} %get-tuple-element.76), channel_id=1, source_target_pairs={{0,4},{1,5},{2,6},{3,7},{4,0},{5,1},{6,2},{7,3},{8,12},{9,13},{10,... | collective-permute-start | bytes 589832 | tf_op jit(solution)/shard_map/ppermute | solution.py:87
  67.5 0.5 collective-permute-start.25
  68.0 0.5 collective-permute-start.26
  68.5 1.4 %block_matrix.1 = (f32[32,96,128]{2,1,0:T(8,128)S(1)}, f32[32,96,128]{2,1,0:T(8,128)S(1)}, f32[32,96,128]{2,1,0:T(8,128)S(1)}) custom-call(f32[4,32]{1,0:T(4,128)S(1)} %get-tuple-element.84.shell, f32[96,128]{1,0:T(8,128)S(1)} %add_multiply_fusion.angular), custom_call_target="tpu_custom_call" | custom-call | flops 10000000 | bytes 6000000 | tf_op jit(solution)/shard_map/block_matrix/pallas_call | solution.py:223
  69.9 0.0 copy-start.1
  69.9 1.1 copy-done.1
  71.0 1.4 %concatenate.13.diffusivity = f32[16,32]{1,0:T(8,128)S(1)} concatenate(f32[1,32]{1,0:T(1,128)} %bitcast.14, f32[1,32]{1,0:T(1,128)} %copy-done.13, f32[1,32]{1,0:T(1,128)} %copy-done.12, f32[1,32]{1,0:T(1,128)} %copy-done.11, f32[4,32]{1,0:T(4,128)} %copy-done.10, f32[4,32]{1,0:T(4,128)} %copy-done.9, f32[4,32]{1,0:T(4,128)} %copy-done.8), dimensions={0} | concatenate | bytes 4096 | tf_op jit(solution)/shard_map/concatenate | solution.py:593
  72.4 3.0 %levels.1 = (f32[2304,128]{1,0:T(8,128)S(1)}, f32[2304,128]{1,0:T(8,128)S(1)}) custom-call(s32[3]{0:T(128)S(1)} %pad_add_fusion.1.where, f32[16,32]{1,0:T(8,128)S(1)} %concatenate.13.diffusivity), custom_call_target="tpu_custom_call" | custom-call | flops 10000000 | bytes 8000000 | tf_op jit(solution)/shard_map/levels/pallas_call | solution.py:334
  75.5 4.5 %collective-permute-done.25.refs_6_ = bf16[4,32,768]{2,1,0:T(8,128)(2,1)} collective-permute-done((bf16[4,32,768]{2,1,0:T(8,128)(2,1)}, bf16[4,32,768]{2,1,0:T(8,128)(2,1)}, u32[]{:S(2)}, u32[]{:S(2)}) %collective-permute-start.25) | collective-permute-done | bytes 196640 | tf_op jit(solution)/shard_map/ppermute | solution.py:87
  80.0 11.5 %forcing_solve.1 = (f32[32,96,128]{2,1,0:T(8,128)}, bf16[2,96,128]{2,1,0:T(8,128)(2,1)}) custom-call(s32[1]{0:T(128)} %bitcast.2.me, f32[4,32]{1,0:T(4,128)} %copy-done.3, f32[32,16,2,384]{3,2,1,0:T(2,128)} %field.5, f32[32,96,128]{2,1,0:T(8,128)} %copy-done.1, bf16[16,384,768]{2,1,0:T(8,128)(2,1)} %legendre.5, ...), custom_call_target="tpu_custom_call" | custom-call | flops 603979776 | bytes 16000000 | tf_op jit(solution)/shard_map/forcing_solve/pallas_call | solution.py:400
  91.5 2.5 %collective-permute-start.29 = (bf16[2,96,128]{2,1,0:T(8,128)(2,1)}, bf16[2,96,128]{2,1,0:T(8,128)(2,1)S(1)}, u32[]{:S(2)}, u32[]{:S(2)}) collective-permute-start(bf16[2,96,128]{2,1,0:T(8,128)(2,1)} %get-tuple-element.79.a), channel_id=1, source_target_pairs={{0,24},{8,0},{16,8},{24,16},{1,25},{9,1},{17,9},{25,17},{2,26},{10... | collective-permute-start | bytes 147464 | tf_op jit(solution)/shard_map/ppermute | solution.py:558
  94.0 1.2 %collective-permute-start.28 = (bf16[2,96,128]{2,1,0:T(8,128)(2,1)}, bf16[2,96,128]{2,1,0:T(8,128)(2,1)S(1)}, u32[]{:S(2)}, u32[]{:S(2)}) collective-permute-start(bf16[2,96,128]{2,1,0:T(8,128)(2,1)} %get-tuple-element.79.a), channel_id=1, source_target_pairs={{0,16},{8,24},{16,0},{24,8},{1,17},{9,25},{17,1},{25,9},{2,18},{10... | collective-permute-start | bytes 147464 | tf_op jit(solution)/shard_map/ppermute | solution.py:558
  95.2 0.7 collective-permute-start.27
  95.9 0.1 pad_add_fusion.place
  96.0 0.3 collective-permute-done.29.d
  96.3 3.5 %collective-permute-done.28.c = bf16[2,96,128]{2,1,0:T(8,128)(2,1)S(1)} collective-permute-done((bf16[2,96,128]{2,1,0:T(8,128)(2,1)}, bf16[2,96,128]{2,1,0:T(8,128)(2,1)S(1)}, u32[]{:S(2)}, u32[]{:S(2)}) %collective-permute-start.28) | collective-permute-done | bytes 49184 | tf_op jit(solution)/shard_map/ppermute | solution.py:558
  99.8 0.9 collective-permute-done.27.b
  100.7 0.8 copy-done.2
  101.5 1.2 %inner_join.1.e = bf16[2,96,128]{2,1,0:T(8,128)(2,1)S(1)} custom-call(s32[2]{0:T(128)S(1)} %pad_add_fusion.place, f32[4,6,96,128]{3,2,1,0:T(8,128)S(1)} %bitcast.11, bf16[2,96,128]{2,1,0:T(8,128)(2,1)S(1)} %copy-done.2, bf16[2,96,128]{2,1,0:T(8,128)(2,1)S(1)} %collective-permute-done.27.b, bf16[2,96,128]{2,1,0:T(8,128)(2,1)S(1)} %collective-permute-done.28.c, ...), custom_call_target="tpu_custom_call" | custom-call | flops 1000000 | bytes 2000000 | tf_op jit(solution)/shard_map/inner_join/pallas_call | solution.py:472
  102.7 1.7 %collective-permute-start.32 = (bf16[2,96,128]{2,1,0:T(8,128)(2,1)S(1)}, bf16[2,96,128]{2,1,0:T(8,128)(2,1)S(1)}, u32[]{:S(2)}, u32[]{:S(2)}) collective-permute-start(bf16[2,96,128]{2,1,0:T(8,128)(2,1)S(1)} %inner_join.1.e), channel_id=1, source_target_pairs={{0,96},{32,0},{64,32},{96,64},{1,97},{33,1},{65,33},{97,65},{2,98}... | collective-permute-start | bytes 147464 | tf_op jit(solution)/shard_map/ppermute | solution.py:558
  104.4 0.9 collective-permute-start.31
  105.3 0.0 collective-permute-start.30
  105.3 1.6 %collective-permute-done.32.h = bf16[2,96,128]{2,1,0:T(8,128)(2,1)S(1)} collective-permute-done((bf16[2,96,128]{2,1,0:T(8,128)(2,1)S(1)}, bf16[2,96,128]{2,1,0:T(8,128)(2,1)S(1)}, u32[]{:S(2)}, u32[]{:S(2)}) %collective-permute-start.32) | collective-permute-done | bytes 49184 | tf_op jit(solution)/shard_map/ppermute | solution.py:558
  106.9 3.1 %collective-permute-done.31.g = bf16[2,96,128]{2,1,0:T(8,128)(2,1)S(1)} collective-permute-done((bf16[2,96,128]{2,1,0:T(8,128)(2,1)S(1)}, bf16[2,96,128]{2,1,0:T(8,128)(2,1)S(1)}, u32[]{:S(2)}, u32[]{:S(2)}) %collective-permute-start.31) | collective-permute-done | bytes 49184 | tf_op jit(solution)/shard_map/ppermute | solution.py:558
  110.0 0.6 collective-permute-done.30.f
  110.6 1.4 %copy-done = f32[32,96,128]{2,1,0:T(8,128)S(1)} copy-done((f32[32,96,128]{2,1,0:T(8,128)S(1)}, f32[32,96,128]{2,1,0:T(8,128)}, u32[]{:S(2)}) %copy-start) | copy-done | bytes 1572888
  112.0 3.6 %final_join.1 = f32[32,16,2,384]{3,2,1,0:T(2,128)} custom-call(s32[2]{0:T(128)S(1)} %pad_add_fusion.place, f32[4,6,96,128]{3,2,1,0:T(8,128)S(1)} %bitcast.12, f32[4,6,96,128]{3,2,1,0:T(8,128)S(1)} %bitcast.13, bf16[2,96,128]{2,1,0:T(8,128)(2,1)S(1)} %copy-done.2, bf16[2,96,128]{2,1,0:T(8,128)(2,1)S(1)} %collective-permute-done.27.b, ...), custom_call_target="tpu_custom_call" | custom-call | flops 3000000 | bytes 9000000 | tf_op jit(solution)/shard_map/final_join/pallas_call | solution.py:533
  (77 shorter events, 0.2 us)
Async XLA Ops:
  6.6 14.6 %collective-permute-start = (bf16[2,4,16,768]{3,2,1,0:T(8,128)(2,1)}, bf16[2,4,16,768]{3,2,1,0:T(8,128)(2,1)S(1)}, u32[]{:S(2)}, u32[]{:S(2)}) collective-permute-start(bf16[2,4,16,768]{3,2,1,0:T(8,128)(2,1)} %get-tuple-element.44), channel_id=1, source_target_pairs={{0,7},{1,2},{2,1},{3,4},{4,3},{5,6},{6,5},{7,0},{8,15},{9,10},{10,... | collective-permute-start | bytes 589832 | tf_op jit(solution)/shard_map/ppermute | solution.py:87
  10.3 13.1 %collective-permute-start.7 = (bf16[2,4,16,768]{3,2,1,0:T(8,128)(2,1)}, bf16[2,4,16,768]{3,2,1,0:T(8,128)(2,1)S(1)}, u32[]{:S(2)}, u32[]{:S(2)}) collective-permute-start(bf16[2,4,16,768]{3,2,1,0:T(8,128)(2,1)} %get-tuple-element.55), channel_id=1, source_target_pairs={{0,2},{1,7},{2,4},{3,1},{4,6},{5,3},{6,0},{7,5},{8,10},{9,15},{10,... | collective-permute-start | bytes 589832 | tf_op jit(solution)/shard_map/ppermute | solution.py:87
  10.3 13.8 %collective-permute-start.8 = (bf16[2,4,16,768]{3,2,1,0:T(8,128)(2,1)}, bf16[2,4,16,768]{3,2,1,0:T(8,128)(2,1)S(1)}, u32[]{:S(2)}, u32[]{:S(2)}) collective-permute-start(bf16[2,4,16,768]{3,2,1,0:T(8,128)(2,1)} %get-tuple-element.56), channel_id=1, source_target_pairs={{0,6},{1,3},{2,0},{3,5},{4,2},{5,7},{6,4},{7,1},{8,14},{9,11},{10,... | collective-permute-start | bytes 589832 | tf_op jit(solution)/shard_map/ppermute | solution.py:87
  13.5 12.1 %collective-permute-start.9 = (bf16[2,4,16,768]{3,2,1,0:T(8,128)(2,1)}, bf16[2,4,16,768]{3,2,1,0:T(8,128)(2,1)S(1)}, u32[]{:S(2)}, u32[]{:S(2)}) collective-permute-start(bf16[2,4,16,768]{3,2,1,0:T(8,128)(2,1)} %get-tuple-element.57), channel_id=1, source_target_pairs={{0,3},{1,6},{2,5},{3,0},{4,7},{5,2},{6,1},{7,4},{8,11},{9,14},{10,... | collective-permute-start | bytes 589832 | tf_op jit(solution)/shard_map/ppermute | solution.py:87
  13.5 14.0 %collective-permute-start.10 = (bf16[2,4,16,768]{3,2,1,0:T(8,128)(2,1)}, bf16[2,4,16,768]{3,2,1,0:T(8,128)(2,1)S(1)}, u32[]{:S(2)}, u32[]{:S(2)}) collective-permute-start(bf16[2,4,16,768]{3,2,1,0:T(8,128)(2,1)} %get-tuple-element.59), channel_id=1, source_target_pairs={{0,4},{1,5},{2,6},{3,7},{4,0},{5,1},{6,2},{7,3},{8,12},{9,13},{10,... | collective-permute-start | bytes 589832 | tf_op jit(solution)/shard_map/ppermute | solution.py:87
  14.5 6.8 %copy-start.24 = (bf16[2,4,16,768]{3,2,1,0:T(8,128)(2,1)S(1)}, bf16[2,4,16,768]{3,2,1,0:T(8,128)(2,1)}, u32[]{:S(2)}) copy-start(bf16[2,4,16,768]{3,2,1,0:T(8,128)(2,1)} %get-tuple-element.60) | copy-start | bytes 589828
  14.5 8.9 %copy-start.23 = (bf16[2,4,16,768]{3,2,1,0:T(8,128)(2,1)S(1)}, bf16[2,4,16,768]{3,2,1,0:T(8,128)(2,1)}, u32[]{:S(2)}) copy-start(bf16[2,4,16,768]{3,2,1,0:T(8,128)(2,1)} %get-tuple-element.61) | copy-start | bytes 589828
  14.5 22.4 %copy-start.7 = (f32[32]{0:T(128)S(1)}, f32[32]{0:T(128)}, u32[]{:S(2)}) copy-start(f32[32]{0:T(128)} %param.10) | copy-start | bytes 388
  21.3 25.6 %copy-start.14 = (bf16[2,4,16,768]{3,2,1,0:T(8,128)(2,1)}, bf16[2,4,16,768]{3,2,1,0:T(8,128)(2,1)S(1)}, u32[]{:S(2)}) copy-start(bf16[2,4,16,768]{3,2,1,0:T(8,128)(2,1)S(1)} %collective-permute-done.refs_4_) | copy-start | bytes 589828
  21.3 8.9 %collective-permute-start.11 = (bf16[2,4,16,768]{3,2,1,0:T(8,128)(2,1)S(1)}, bf16[2,4,16,768]{3,2,1,0:T(8,128)(2,1)S(1)}, u32[]{:S(2)}, u32[]{:S(2)}) collective-permute-start(bf16[2,4,16,768]{3,2,1,0:T(8,128)(2,1)S(1)} %copy-done.24), channel_id=1, source_target_pairs={{0,5},{1,4},{2,7},{3,6},{4,1},{5,0},{6,3},{7,2},{8,13},{9,12},{10,... | collective-permute-start | bytes 589832 | tf_op jit(solution)/shard_map/ppermute | solution.py:87
  23.4 23.4 %copy-start.15 = (bf16[2,4,16,768]{3,2,1,0:T(8,128)(2,1)}, bf16[2,4,16,768]{3,2,1,0:T(8,128)(2,1)S(1)}, u32[]{:S(2)}) copy-start(bf16[2,4,16,768]{3,2,1,0:T(8,128)(2,1)S(1)} %collective-permute-done.7.refs_1_) | copy-start | bytes 589828
  23.4 9.7 %collective-permute-start.12 = (bf16[2,4,16,768]{3,2,1,0:T(8,128)(2,1)S(1)}, bf16[2,4,16,768]{3,2,1,0:T(8,128)(2,1)S(1)}, u32[]{:S(2)}, u32[]{:S(2)}) collective-permute-start(bf16[2,4,16,768]{3,2,1,0:T(8,128)(2,1)S(1)} %copy-done.23), channel_id=1, source_target_pairs={{0,1},{1,0},{2,3},{3,2},{4,5},{5,4},{6,7},{7,6},{8,9},{9,8},{10,11... | collective-permute-start | bytes 589832 | tf_op jit(solution)/shard_map/ppermute | solution.py:87
  24.1 22.7 %copy-start.16 = (bf16[2,4,16,768]{3,2,1,0:T(8,128)(2,1)}, bf16[2,4,16,768]{3,2,1,0:T(8,128)(2,1)S(1)}, u32[]{:S(2)}) copy-start(bf16[2,4,16,768]{3,2,1,0:T(8,128)(2,1)S(1)} %collective-permute-done.8.refs_2_) | copy-start | bytes 589828
  24.1 10.4 %collective-permute-start.13 = (bf16[2,4,16,768]{3,2,1,0:T(8,128)(2,1)}, bf16[2,4,16,768]{3,2,1,0:T(8,128)(2,1)S(1)}, u32[]{:S(2)}, u32[]{:S(2)}) collective-permute-start(bf16[2,4,16,768]{3,2,1,0:T(8,128)(2,1)} %get-tuple-element.64), channel_id=1, source_target_pairs={{0,2},{1,7},{2,4},{3,1},{4,6},{5,3},{6,0},{7,5},{8,10},{9,15},{10,... | collective-permute-start | bytes 589832 | tf_op jit(solution)/shard_map/ppermute | solution.py:87
  25.6 21.3 %copy-start.17 = (bf16[2,4,16,768]{3,2,1,0:T(8,128)(2,1)}, bf16[2,4,16,768]{3,2,1,0:T(8,128)(2,1)S(1)}, u32[]{:S(2)}) copy-start(bf16[2,4,16,768]{3,2,1,0:T(8,128)(2,1)S(1)} %collective-permute-done.9.refs_3_) | copy-start | bytes 589828
  25.6 9.6 %collective-permute-start.14 = (bf16[2,4,16,768]{3,2,1,0:T(8,128)(2,1)}, bf16[2,4,16,768]{3,2,1,0:T(8,128)(2,1)S(1)}, u32[]{:S(2)}, u32[]{:S(2)}) collective-permute-start(bf16[2,4,16,768]{3,2,1,0:T(8,128)(2,1)} %get-tuple-element.65), channel_id=1, source_target_pairs={{0,6},{1,3},{2,0},{3,5},{4,2},{5,7},{6,4},{7,1},{8,14},{9,11},{10,... | collective-permute-start | bytes 589832 | tf_op jit(solution)/shard_map/ppermute | solution.py:87
  27.5 19.3 %copy-start.18 = (bf16[2,4,16,768]{3,2,1,0:T(8,128)(2,1)}, bf16[2,4,16,768]{3,2,1,0:T(8,128)(2,1)S(1)}, u32[]{:S(2)}) copy-start(bf16[2,4,16,768]{3,2,1,0:T(8,128)(2,1)S(1)} %collective-permute-done.10.refs_5_) | copy-start | bytes 589828
  27.5 9.7 %collective-permute-start.15 = (bf16[2,4,16,768]{3,2,1,0:T(8,128)(2,1)}, bf16[2,4,16,768]{3,2,1,0:T(8,128)(2,1)S(1)}, u32[]{:S(2)}, u32[]{:S(2)}) collective-permute-start(bf16[2,4,16,768]{3,2,1,0:T(8,128)(2,1)} %get-tuple-element.66), channel_id=1, source_target_pairs={{0,3},{1,6},{2,5},{3,0},{4,7},{5,2},{6,1},{7,4},{8,11},{9,14},{10,... | collective-permute-start | bytes 589832 | tf_op jit(solution)/shard_map/ppermute | solution.py:87
  30.2 16.6 %copy-start.19 = (bf16[2,4,16,768]{3,2,1,0:T(8,128)(2,1)}, bf16[2,4,16,768]{3,2,1,0:T(8,128)(2,1)S(1)}, u32[]{:S(2)}) copy-start(bf16[2,4,16,768]{3,2,1,0:T(8,128)(2,1)S(1)} %collective-permute-done.11.refs_6_) | copy-start | bytes 589828
  30.2 10.0 %collective-permute-start.16 = (bf16[2,4,16,768]{3,2,1,0:T(8,128)(2,1)}, bf16[2,4,16,768]{3,2,1,0:T(8,128)(2,1)S(1)}, u32[]{:S(2)}, u32[]{:S(2)}) collective-permute-start(bf16[2,4,16,768]{3,2,1,0:T(8,128)(2,1)} %get-tuple-element.67), channel_id=1, source_target_pairs={{0,7},{1,2},{2,1},{3,4},{4,3},{5,6},{6,5},{7,0},{8,15},{9,10},{10,... | collective-permute-start | bytes 589832 | tf_op jit(solution)/shard_map/ppermute | solution.py:87
  33.1 13.8 %copy-start.20 = (bf16[2,4,16,768]{3,2,1,0:T(8,128)(2,1)}, bf16[2,4,16,768]{3,2,1,0:T(8,128)(2,1)S(1)}, u32[]{:S(2)}) copy-start(bf16[2,4,16,768]{3,2,1,0:T(8,128)(2,1)S(1)} %collective-permute-done.12.refs_7_) | copy-start | bytes 589828
  33.1 10.2 %collective-permute-start.17 = (bf16[2,4,16,768]{3,2,1,0:T(8,128)(2,1)}, bf16[2,4,16,768]{3,2,1,0:T(8,128)(2,1)S(1)}, u32[]{:S(2)}, u32[]{:S(2)}) collective-permute-start(bf16[2,4,16,768]{3,2,1,0:T(8,128)(2,1)} %get-tuple-element.68), channel_id=1, source_target_pairs={{0,4},{1,5},{2,6},{3,7},{4,0},{5,1},{6,2},{7,3},{8,12},{9,13},{10,... | collective-permute-start | bytes 589832 | tf_op jit(solution)/shard_map/ppermute | solution.py:87
  34.5 12.4 %copy-start.21 = (bf16[2,4,16,768]{3,2,1,0:T(8,128)(2,1)}, bf16[2,4,16,768]{3,2,1,0:T(8,128)(2,1)S(1)}, u32[]{:S(2)}) copy-start(bf16[2,4,16,768]{3,2,1,0:T(8,128)(2,1)S(1)} %collective-permute-done.13.refs_9_) | copy-start | bytes 589828
  34.5 12.3 %collective-permute-start.18 = (bf16[2,4,16,768]{3,2,1,0:T(8,128)(2,1)}, bf16[2,4,16,768]{3,2,1,0:T(8,128)(2,1)S(1)}, u32[]{:S(2)}, u32[]{:S(2)}) collective-permute-start(bf16[2,4,16,768]{3,2,1,0:T(8,128)(2,1)} %get-tuple-element.69), channel_id=1, source_target_pairs={{0,5},{1,4},{2,7},{3,6},{4,1},{5,0},{6,3},{7,2},{8,13},{9,12},{10,... | collective-permute-start | bytes 589832 | tf_op jit(solution)/shard_map/ppermute | solution.py:87
  35.2 11.7 %copy-start.22 = (bf16[2,4,16,768]{3,2,1,0:T(8,128)(2,1)}, bf16[2,4,16,768]{3,2,1,0:T(8,128)(2,1)S(1)}, u32[]{:S(2)}) copy-start(bf16[2,4,16,768]{3,2,1,0:T(8,128)(2,1)S(1)} %collective-permute-done.14.refs_10_) | copy-start | bytes 589828
  35.2 11.6 %collective-permute-start.19 = (bf16[2,4,16,768]{3,2,1,0:T(8,128)(2,1)}, bf16[2,4,16,768]{3,2,1,0:T(8,128)(2,1)S(1)}, u32[]{:S(2)}, u32[]{:S(2)}) collective-permute-start(bf16[2,4,16,768]{3,2,1,0:T(8,128)(2,1)} %get-tuple-element.70), channel_id=1, source_target_pairs={{0,1},{1,0},{2,3},{3,2},{4,5},{5,4},{6,7},{7,6},{8,9},{9,8},{10,11... | collective-permute-start | bytes 589832 | tf_op jit(solution)/shard_map/ppermute | solution.py:87
  37.3 9.7 %copy-start.25 = (bf16[2,4,16,768]{3,2,1,0:T(8,128)(2,1)}, bf16[2,4,16,768]{3,2,1,0:T(8,128)(2,1)S(1)}, u32[]{:S(2)}) copy-start(bf16[2,4,16,768]{3,2,1,0:T(8,128)(2,1)S(1)} %collective-permute-done.15.refs_11_) | copy-start | bytes 589828
  37.3 19.1 %collective-permute-start.3 = (f32[1,32]{1,0:T(1,128)S(1)}, f32[1,32]{1,0:T(1,128)S(1)}, u32[]{:S(2)}, u32[]{:S(2)}) collective-permute-start(f32[1,32]{1,0:T(1,128)S(1)} %bitcast.15), channel_id=1, source_target_pairs={{0,24},{8,0},{16,8},{24,16},{1,25},{9,1},{17,9},{25,17},{2,26},{10... | collective-permute-start | bytes 392 | tf_op jit(solution)/shard_map/ppermute | solution.py:558
  40.3 6.6 %copy-start.26 = (bf16[2,4,16,768]{3,2,1,0:T(8,128)(2,1)}, bf16[2,4,16,768]{3,2,1,0:T(8,128)(2,1)S(1)}, u32[]{:S(2)}) copy-start(bf16[2,4,16,768]{3,2,1,0:T(8,128)(2,1)S(1)} %collective-permute-done.16.refs_12_) | copy-start | bytes 589828
  40.3 16.0 %collective-permute-start.2 = (f32[1,32]{1,0:T(1,128)S(1)}, f32[1,32]{1,0:T(1,128)S(1)}, u32[]{:S(2)}, u32[]{:S(2)}) collective-permute-start(f32[1,32]{1,0:T(1,128)S(1)} %bitcast.16), channel_id=1, source_target_pairs={{0,16},{8,24},{16,0},{24,8},{1,17},{9,25},{17,1},{25,9},{2,18},{10... | collective-permute-start | bytes 392 | tf_op jit(solution)/shard_map/ppermute | solution.py:558
  43.3 3.6 %copy-start.27 = (bf16[2,4,16,768]{3,2,1,0:T(8,128)(2,1)}, bf16[2,4,16,768]{3,2,1,0:T(8,128)(2,1)S(1)}, u32[]{:S(2)}) copy-start(bf16[2,4,16,768]{3,2,1,0:T(8,128)(2,1)S(1)} %collective-permute-done.17.refs_13_) | copy-start | bytes 589828
  43.3 13.0 %collective-permute-start.1 = (f32[1,32]{1,0:T(1,128)S(1)}, f32[1,32]{1,0:T(1,128)S(1)}, u32[]{:S(2)}, u32[]{:S(2)}) collective-permute-start(f32[1,32]{1,0:T(1,128)S(1)} %bitcast.17), channel_id=1, source_target_pairs={{0,8},{8,16},{16,24},{24,0},{1,9},{9,17},{17,25},{25,1},{2,10},{10... | collective-permute-start | bytes 392 | tf_op jit(solution)/shard_map/ppermute | solution.py:558
  46.8 0.7 copy-start.28
  46.8 0.8 copy-start.29
  47.6 20.9 %copy-start.6 = (s32[96,128]{1,0:T(8,128)S(1)}, s32[96,128]{1,0:T(8,128)}, u32[]{:S(2)}) copy-start(s32[96,128]{1,0:T(8,128)} %constant.41.clone) | copy-start | bytes 147460
  54.2 13.3 %collective-permute-start.20 = (bf16[4,32,768]{2,1,0:T(8,128)(2,1)}, bf16[4,32,768]{2,1,0:T(8,128)(2,1)S(1)}, u32[]{:S(2)}, u32[]{:S(2)}) collective-permute-start(bf16[4,32,768]{2,1,0:T(8,128)(2,1)} %get-tuple-element.72), channel_id=1, source_target_pairs={{0,6},{1,3},{2,0},{3,5},{4,2},{5,7},{6,4},{7,1},{8,14},{9,11},{10,... | collective-permute-start | bytes 589832 | tf_op jit(solution)/shard_map/ppermute | solution.py:87
  55.4 12.5 %collective-permute-start.21 = (bf16[4,32,768]{2,1,0:T(8,128)(2,1)}, bf16[4,32,768]{2,1,0:T(8,128)(2,1)S(1)}, u32[]{:S(2)}, u32[]{:S(2)}) collective-permute-start(bf16[4,32,768]{2,1,0:T(8,128)(2,1)} %get-tuple-element.73), channel_id=1, source_target_pairs={{0,2},{1,7},{2,4},{3,1},{4,6},{5,3},{6,0},{7,5},{8,10},{9,15},{10,... | collective-permute-start | bytes 589832 | tf_op jit(solution)/shard_map/ppermute | solution.py:87
  56.3 4.6 %copy-start.11 = (f32[1,32]{1,0:T(1,128)}, f32[1,32]{1,0:T(1,128)S(1)}, u32[]{:S(2)}) copy-start(f32[1,32]{1,0:T(1,128)S(1)} %collective-permute-done.3) | copy-start | bytes 388
  56.3 4.6 %copy-start.12 = (f32[1,32]{1,0:T(1,128)}, f32[1,32]{1,0:T(1,128)S(1)}, u32[]{:S(2)}) copy-start(f32[1,32]{1,0:T(1,128)S(1)} %collective-permute-done.2) | copy-start | bytes 388
  56.3 4.6 %copy-start.13 = (f32[1,32]{1,0:T(1,128)}, f32[1,32]{1,0:T(1,128)S(1)}, u32[]{:S(2)}) copy-start(f32[1,32]{1,0:T(1,128)S(1)} %collective-permute-done.1) | copy-start | bytes 388
  56.4 23.6 %copy-start.3 = (f32[4,32]{1,0:T(4,128)}, f32[4,32]{1,0:T(4,128)S(1)}, u32[]{:S(2)}) copy-start(f32[4,32]{1,0:T(4,128)S(1)} %get-tuple-element.84.shell) | copy-start | bytes 1540
  56.4 4.6 %collective-permute-start.6 = (f32[4,32]{1,0:T(4,128)S(1)}, f32[4,32]{1,0:T(4,128)S(1)}, u32[]{:S(2)}, u32[]{:S(2)}) collective-permute-start(f32[4,32]{1,0:T(4,128)S(1)} %get-tuple-element.83), channel_id=1, source_target_pairs={{0,96},{32,0},{64,32},{96,64},{1,97},{33,1},{65,33},{97,65},{2,98}... | collective-permute-start | bytes 1544 | tf_op jit(solution)/shard_map/ppermute | solution.py:558
  59.2 5.1 %collective-permute-start.5 = (f32[4,32]{1,0:T(4,128)S(1)}, f32[4,32]{1,0:T(4,128)S(1)}, u32[]{:S(2)}, u32[]{:S(2)}) collective-permute-start(f32[4,32]{1,0:T(4,128)S(1)} %get-tuple-element.83), channel_id=1, source_target_pairs={{0,64},{32,96},{64,0},{96,32},{1,65},{33,97},{65,1},{97,33},{2,66}... | collective-permute-start | bytes 1544 | tf_op jit(solution)/shard_map/ppermute | solution.py:558
  60.0 4.8 %collective-permute-start.4 = (f32[4,32]{1,0:T(4,128)S(1)}, f32[4,32]{1,0:T(4,128)S(1)}, u32[]{:S(2)}, u32[]{:S(2)}) collective-permute-start(f32[4,32]{1,0:T(4,128)S(1)} %get-tuple-element.83), channel_id=1, source_target_pairs={{0,32},{32,64},{64,96},{96,0},{1,33},{33,65},{65,97},{97,1},{2,34}... | collective-permute-start | bytes 1544 | tf_op jit(solution)/shard_map/ppermute | solution.py:558
  61.0 7.5 %copy-start.8 = (f32[4,32]{1,0:T(4,128)}, f32[4,32]{1,0:T(4,128)S(1)}, u32[]{:S(2)}) copy-start(f32[4,32]{1,0:T(4,128)S(1)} %collective-permute-done.6) | copy-start | bytes 1540
  61.0 14.5 %collective-permute-start.22 = (bf16[4,32,768]{2,1,0:T(8,128)(2,1)}, bf16[4,32,768]{2,1,0:T(8,128)(2,1)}, u32[]{:S(2)}, u32[]{:S(2)}) collective-permute-start(bf16[4,32,768]{2,1,0:T(8,128)(2,1)} %get-tuple-element.74), channel_id=1, source_target_pairs={{0,3},{1,6},{2,5},{3,0},{4,7},{5,2},{6,1},{7,4},{8,11},{9,14},{10,... | collective-permute-start | bytes 589832 | tf_op jit(solution)/shard_map/ppermute | solution.py:87
  64.3 4.2 %copy-start.9 = (f32[4,32]{1,0:T(4,128)}, f32[4,32]{1,0:T(4,128)S(1)}, u32[]{:S(2)}) copy-start(f32[4,32]{1,0:T(4,128)S(1)} %collective-permute-done.5) | copy-start | bytes 1540
  64.3 11.2 %collective-permute-start.23 = (bf16[4,32,768]{2,1,0:T(8,128)(2,1)}, bf16[4,32,768]{2,1,0:T(8,128)(2,1)}, u32[]{:S(2)}, u32[]{:S(2)}) collective-permute-start(bf16[4,32,768]{2,1,0:T(8,128)(2,1)} %get-tuple-element.75), channel_id=1, source_target_pairs={{0,7},{1,2},{2,1},{3,4},{4,3},{5,6},{6,5},{7,0},{8,15},{9,10},{10,... | collective-permute-start | bytes 589832 | tf_op jit(solution)/shard_map/ppermute | solution.py:87
  64.8 3.7 %copy-start.10 = (f32[4,32]{1,0:T(4,128)}, f32[4,32]{1,0:T(4,128)S(1)}, u32[]{:S(2)}) copy-start(f32[4,32]{1,0:T(4,128)S(1)} %collective-permute-done.4) | copy-start | bytes 1540
  64.8 10.7 %collective-permute-start.24 = (bf16[4,32,768]{2,1,0:T(8,128)(2,1)}, bf16[4,32,768]{2,1,0:T(8,128)(2,1)}, u32[]{:S(2)}, u32[]{:S(2)}) collective-permute-start(bf16[4,32,768]{2,1,0:T(8,128)(2,1)} %get-tuple-element.76), channel_id=1, source_target_pairs={{0,4},{1,5},{2,6},{3,7},{4,0},{5,1},{6,2},{7,3},{8,12},{9,13},{10,... | collective-permute-start | bytes 589832 | tf_op jit(solution)/shard_map/ppermute | solution.py:87
  67.5 12.5 %copy-start.4 = (bf16[4,32,768]{2,1,0:T(8,128)(2,1)}, bf16[4,32,768]{2,1,0:T(8,128)(2,1)S(1)}, u32[]{:S(2)}) copy-start(bf16[4,32,768]{2,1,0:T(8,128)(2,1)S(1)} %collective-permute-done.20.refs_1_) | copy-start | bytes 589828
  67.5 12.5 %collective-permute-start.25 = (bf16[4,32,768]{2,1,0:T(8,128)(2,1)}, bf16[4,32,768]{2,1,0:T(8,128)(2,1)}, u32[]{:S(2)}, u32[]{:S(2)}) collective-permute-start(bf16[4,32,768]{2,1,0:T(8,128)(2,1)} %get-tuple-element.77), channel_id=1, source_target_pairs={{0,5},{1,4},{2,7},{3,6},{4,1},{5,0},{6,3},{7,2},{8,13},{9,12},{10,... | collective-permute-start | bytes 589832 | tf_op jit(solution)/shard_map/ppermute | solution.py:87
  68.0 12.0 %copy-start.5 = (bf16[4,32,768]{2,1,0:T(8,128)(2,1)}, bf16[4,32,768]{2,1,0:T(8,128)(2,1)S(1)}, u32[]{:S(2)}) copy-start(bf16[4,32,768]{2,1,0:T(8,128)(2,1)S(1)} %collective-permute-done.21.refs_2_) | copy-start | bytes 589828
  68.0 12.0 %collective-permute-start.26 = (bf16[4,32,768]{2,1,0:T(8,128)(2,1)}, bf16[4,32,768]{2,1,0:T(8,128)(2,1)}, u32[]{:S(2)}, u32[]{:S(2)}) collective-permute-start(bf16[4,32,768]{2,1,0:T(8,128)(2,1)} %get-tuple-element.78), channel_id=1, source_target_pairs={{0,1},{1,0},{2,3},{3,2},{4,5},{5,4},{6,7},{7,6},{8,9},{9,8},{10,11... | collective-permute-start | bytes 589832 | tf_op jit(solution)/shard_map/ppermute | solution.py:87
  69.9 1.1 copy-start.1
  91.5 4.8 %collective-permute-start.29 = (bf16[2,96,128]{2,1,0:T(8,128)(2,1)}, bf16[2,96,128]{2,1,0:T(8,128)(2,1)S(1)}, u32[]{:S(2)}, u32[]{:S(2)}) collective-permute-start(bf16[2,96,128]{2,1,0:T(8,128)(2,1)} %get-tuple-element.79.a), channel_id=1, source_target_pairs={{0,24},{8,0},{16,8},{24,16},{1,25},{9,1},{17,9},{25,17},{2,26},{10... | collective-permute-start | bytes 147464 | tf_op jit(solution)/shard_map/ppermute | solution.py:558
  94.0 5.8 %collective-permute-start.28 = (bf16[2,96,128]{2,1,0:T(8,128)(2,1)}, bf16[2,96,128]{2,1,0:T(8,128)(2,1)S(1)}, u32[]{:S(2)}, u32[]{:S(2)}) collective-permute-start(bf16[2,96,128]{2,1,0:T(8,128)(2,1)} %get-tuple-element.79.a), channel_id=1, source_target_pairs={{0,16},{8,24},{16,0},{24,8},{1,17},{9,25},{17,1},{25,9},{2,18},{10... | collective-permute-start | bytes 147464 | tf_op jit(solution)/shard_map/ppermute | solution.py:558
  95.2 5.5 %collective-permute-start.27 = (bf16[2,96,128]{2,1,0:T(8,128)(2,1)}, bf16[2,96,128]{2,1,0:T(8,128)(2,1)S(1)}, u32[]{:S(2)}, u32[]{:S(2)}) collective-permute-start(bf16[2,96,128]{2,1,0:T(8,128)(2,1)} %get-tuple-element.79.a), channel_id=1, source_target_pairs={{0,8},{8,16},{16,24},{24,0},{1,9},{9,17},{17,25},{25,1},{2,10},{10... | collective-permute-start | bytes 147464 | tf_op jit(solution)/shard_map/ppermute | solution.py:558
  100.7 0.8 copy-start.2
  102.7 4.2 %collective-permute-start.32 = (bf16[2,96,128]{2,1,0:T(8,128)(2,1)S(1)}, bf16[2,96,128]{2,1,0:T(8,128)(2,1)S(1)}, u32[]{:S(2)}, u32[]{:S(2)}) collective-permute-start(bf16[2,96,128]{2,1,0:T(8,128)(2,1)S(1)} %inner_join.1.e), channel_id=1, source_target_pairs={{0,96},{32,0},{64,32},{96,64},{1,97},{33,1},{65,33},{97,65},{2,98}... | collective-permute-start | bytes 147464 | tf_op jit(solution)/shard_map/ppermute | solution.py:558
  104.4 5.6 %collective-permute-start.31 = (bf16[2,96,128]{2,1,0:T(8,128)(2,1)S(1)}, bf16[2,96,128]{2,1,0:T(8,128)(2,1)S(1)}, u32[]{:S(2)}, u32[]{:S(2)}) collective-permute-start(bf16[2,96,128]{2,1,0:T(8,128)(2,1)S(1)} %inner_join.1.e), channel_id=1, source_target_pairs={{0,64},{32,96},{64,0},{96,32},{1,65},{33,97},{65,1},{97,33},{2,66}... | collective-permute-start | bytes 147464 | tf_op jit(solution)/shard_map/ppermute | solution.py:558
  105.3 5.3 %collective-permute-start.30 = (bf16[2,96,128]{2,1,0:T(8,128)(2,1)S(1)}, bf16[2,96,128]{2,1,0:T(8,128)(2,1)S(1)}, u32[]{:S(2)}, u32[]{:S(2)}) collective-permute-start(bf16[2,96,128]{2,1,0:T(8,128)(2,1)S(1)} %inner_join.1.e), channel_id=1, source_target_pairs={{0,32},{32,64},{64,96},{96,0},{1,33},{33,65},{65,97},{97,1},{2,34}... | collective-permute-start | bytes 147464 | tf_op jit(solution)/shard_map/ppermute | solution.py:558
  110.6 1.4 %copy-start = (f32[32,96,128]{2,1,0:T(8,128)S(1)}, f32[32,96,128]{2,1,0:T(8,128)}, u32[]{:S(2)}) copy-start(f32[32,96,128]{2,1,0:T(8,128)} %get-tuple-element.80.solved) | copy-start | bytes 4718596

commit v4 on v3

--- a/solution.py
+++ b/solution.py
@@ -58,7 +58,7 @@
 
 HALF = ORD // 2
 PAIRS_HALF = HALF * HALVES
-AHEAD = 7
+AHEAD = 4
 
 
 def moved(device, k, back):
@@ -66,15 +66,15 @@
     ahead = 1 - 2 * core
     steps, other = (
         (0, 0),
+        (2, 0),
+        (2, 1),
         (ahead, 0),
         (-ahead, 0),
         (ahead, 1),
         (-ahead, 1),
-        (2, 0),
-        (2, 1),
         (0, 1),
     )[k]
-    if back and k in (1, 2):
+    if back and k in (3, 4):
         steps = -steps
     core = 1 - core if other else core
     return (z + steps + 4) % 4 * 2 + core
@@ -266,12 +266,14 @@
 LINKS = 6
 
 
-def level_kernel(where, diffusivity, inner, outer, ordered, factors, links_held, table):
+def level_kernel(where, a, b, c, d, inner, outer, slots, ordered, factors, links_held, table):
     x, y, mode = where[0], where[1], where[2]
+    for n, source in enumerate((a, b, c, d)):
+        slots[n * CHAIN : (n + 1) * CHAIN, :] = source[...]
     for k in range(CHAIN):
         for first in range(8):
             slot = lax.rem(x + CHAIN - first % CHAIN, CHAIN) * CHAIN + lax.rem(y + CHAIN - k, CHAIN)
-            ordered[k, first : first + 1, :] = diffusivity[pl.ds(slot, 1), :]
+            ordered[k, first : first + 1, :] = slots[pl.ds(slot, 1), :]
     degree = lax.broadcasted_iota(jnp.int32, (1, 1, DEGREES), 2).astype(F32)
     angular = degree * (degree + 1.0)
     shape = (CHAIN, 8, 1)
@@ -328,15 +330,16 @@
                 outer[rows, :] = found[count:]
 
 
-def levels(where, diffusivity):
+def levels(where, blocks):
     count = CHAIN * LINKS
     shape = jax.ShapeDtypeStruct((count * ROWS, LANES), F32)
     outs = pl.pallas_call(
         level_kernel,
         out_shape=(shape, shape),
-        in_specs=[whole(pltpu.SMEM), whole()],
+        in_specs=[whole(pltpu.SMEM)] + [whole()] * CHAIN,
         out_specs=(whole(), whole()),
         scratch_shapes=[
+            pltpu.VMEM((CHAIN * CHAIN, SHELLS), F32),
             pltpu.VMEM((CHAIN, 8, SHELLS), F32),
             pltpu.VMEM((2, SHELLS, CHAIN, 8, DEGREES), F32),
             pltpu.VMEM((count, 8, DEGREES), F32),
@@ -345,21 +348,19 @@
         compiler_params=params(20),
         cost_estimate=cost(10_000_000, 8_000_000),
         name="levels",
-    )(where, diffusivity)
+    )(where, *blocks)
     return [out.reshape(CHAIN, LINKS, ROWS, LANES) for out in outs]
 
 
 def forcing_kernel(me, shell, field, pivots, legendre, *refs):
     slots = refs[:NMODE]
-    solved, ends, modes, table, fields, inverses, sems, table_sems = refs[NMODE:]
+    solved, ends, modes, table, sems, table_sems = refs[NMODE:]
     copies = [
         pltpu.make_async_copy(
             slots[k], modes.at[pl.ds(moved(me[0], k, False) * NSHELL, NSHELL)], sems.at[k]
         )
         for k in range(NMODE)
     ]
-    copies.append(pltpu.make_async_copy(field, fields, sems.at[NMODE]))
-    last = pltpu.make_async_copy(pivots, inverses, sems.at[NMODE + 1])
     tables = [
         pltpu.make_async_copy(legendre.at[m], table.at[m], table_sems.at[m]) for m in range(ORD)
     ]
@@ -370,28 +371,25 @@
     for m in range(ORD):
         if m + AHEAD < ORD:
             tables[m + AHEAD].start()
-        if m == ORD // 2:
-            last.start()
         tables[m].wait()
         lat = modes[:, HALVES * m : HALVES * (m + 1), :].reshape(SHELLS * HALVES, NLAT)
         forcing = lax.dot_general(
             lat, table[m], (((1,), (1,)), ((), ())), preferred_element_type=F32
         )
-        right_side = fields[:, m].reshape(SHELLS * HALVES, DEG) + forcing
+        right_side = field[:, m].reshape(SHELLS * HALVES, DEG) + forcing
         for tile in range(TILES):
             row = (m * TILES + tile) * HALVES
             solved[:, row : row + HALVES, :] = right_side[
                 :, tile * LANES : (tile + 1) * LANES
             ].reshape(SHELLS, HALVES, LANES)
-    last.wait()
-    value = solved[0] * inverses[0]
+    value = solved[0] * pivots[0]
     solved[0] = value
     for i in range(1, SHELLS):
-        value = (solved[i] + shell[1, i] * value) * inverses[i]
+        value = (solved[i] + shell[1, i] * value) * pivots[i]
         solved[i] = value
     ends[1] = value.astype(BF16)
     for i in reversed(range(SHELLS - 1)):
-        value = solved[i] + (shell[2, i] * inverses[i]) * value
+        value = solved[i] + (shell[2, i] * pivots[i]) * value
         solved[i] = value
     ends[0] = value.astype(BF16)
 
@@ -403,17 +401,15 @@
             jax.ShapeDtypeStruct((SHELLS, ROWS, LANES), F32),
             jax.ShapeDtypeStruct((2, ROWS, LANES), BF16),
         ),
-        in_specs=[whole(pltpu.SMEM)] * 2 + [whole(pl.ANY)] * (3 + NMODE),
+        in_specs=[whole(pltpu.SMEM)] * 2 + [whole()] * 2 + [whole(pl.ANY)] * (1 + NMODE),
         out_specs=(whole(), whole()),
         scratch_shapes=[
             pltpu.VMEM((SHELLS, PAIRS, NLAT), BF16),
             pltpu.VMEM((ORD, DEG, NLAT), BF16),
-            pltpu.VMEM((SHELLS, ORD, HALVES, DEG), F32),
-            pltpu.VMEM((SHELLS, ROWS, LANES), F32),
-            pltpu.SemaphoreType.DMA((NMODE + 2,)),
+            pltpu.SemaphoreType.DMA((NMODE,)),
             pltpu.SemaphoreType.DMA((ORD,)),
         ],
-        compiler_params=params(58),
+        compiler_params=params(50),
         cost_estimate=cost(2 * 64 * DEG * NLAT * ORD, 16_000_000),
         name="forcing_solve",
     )(me, shell, field, pivots, legendre, *slots)
@@ -590,7 +586,7 @@
     angular = degree * (degree + 1.0)
     pivots, left, right = block_matrix(shell, angular)
     near = jnp.concatenate(ring(diffusivity.reshape(1, SHELLS), RADIAL[1]))
-    blocks = jnp.concatenate(ring(near, RADIAL[0]))
+    blocks = ring(near, RADIAL[0])
     inner, outer = levels(jnp.concatenate([place, mode.reshape(1)]), blocks)
 
     modes = moved_all(grid_product(me, synth, analysis, firsts, seconds), True)

time: 116 us -> 113 us (0.974)
  local copies, waits for them, and re-layouts: 5.47 us -> 2.73 us
  starting transfers between devices: 42.6 us -> 43.9 us
  Pallas kernels: 40.6 us -> 39.4 us
    ppermute x21, starting transfers between devices: 24.5 us -> 26 us  [moved_all(): sent.append(lax.ppermute(arrays[k], MODE, pairs))]
    concatenate x1 -> x0, local copies, waits for them, and re-layouts: 1.39 us -> none  [on_device(): blocks = jnp.concatenate(ring(near, RADIAL[0]))]
    unnamed x60 -> x40, local copies, waits for them, and re-layouts: 4.08 us -> 2.73 us
  transfers between devices with their start and end apart: 33 -> 33, of which waited for: 15 -> 12; matrix products, arithmetic and copies ran while one was open for 1% -> 0% of each run, Pallas kernels for 15% -> 15%
where the time goes in v4:
time: 113 us
  starting transfers between devices  43.9 us (39%)
  Pallas kernels  39.4 us (35%)
  waiting for transfers between devices  26.1 us (23%)
  local copies, waits for them, and re-layouts  2.73 us (2%)
    ppermute x21, starting transfers between devices, moved_all(): sent.append(lax.ppermute(arrays[k], MODE, pairs))  26 us
    ppermute x12, starting transfers between devices, shifted(): lax.ppermute(array, axis, [(i, (i + step) % size) for i in range(size)])  17.9 us
    ppermute x12, waiting for transfers between devices, shifted(): lax.ppermute(array, axis, [(i, (i + step) % size) for i in range(size)])  13.1 us
    ppermute x21, waiting for transfers between devices, moved_all(): sent.append(lax.ppermute(arrays[k], MODE, pairs))  13 us
    pallas_call x2, Pallas kernels, synthesis(): pl.pallas_call(functools.partial(synthesis_kernel, half), out_shape=(shap...  12.3 us
    pallas_call x1, Pallas kernels, forcing_solve(): pl.pallas_call(forcing_kernel, out_shape=(jax.ShapeDtypeStruct((SHELLS, R...  11.3 us
    pallas_call x1, Pallas kernels, grid_product(): pl.pallas_call(grid_kernel, out_shape=(shape,) * NMODE, in_specs=[whole(p...  6.63 us
    pallas_call x1, Pallas kernels, final_join(): pl.pallas_call(final_kernel, out_shape=jax.ShapeDtypeStruct((SHELLS, ORD,...  3.56 us
  transfers between devices with their start and end apart: 33, of which 12 were waited for; matrix products, arithmetic and copies ran while one was open for 0% of the time, Pallas kernels for 15%

profile of v4, /device:TPU:0, one launch (start us, length us, event | category | flops | bytes accessed | tf_op | source)
XLA Modules:
  0.0 112.9 jit_solution(11142037917319895234)
XLA Ops:
  0.0 6.1 %synthesis.2 = (bf16[2,4,16,768]{3,2,1,0:T(8,128)(2,1)}, bf16[2,4,16,768]{3,2,1,0:T(8,128)(2,1)}, bf16[2,4,16,768]{3,2,1,0:T(8,128)(2,1)}, bf16[2,4,16,768]{3,2,...) custom-call(s32[1]{0:T(128)} %bitcast.2.me, ...), custom_call_target="tpu_custom_call" | custom-call | flops 603979776 | bytes 8000000 | tf_op jit(solution)/shard_map/synthesis/pallas_call | solution.py:130
  6.1 4.2 %collective-permute-start = (bf16[2,4,16,768]{3,2,1,0:T(8,128)(2,1)}, bf16[2,4,16,768]{3,2,1,0:T(8,128)(2,1)S(1)}, u32[]{:S(2)}, u32[]{:S(2)}) collective-permute-start(bf16[2,4,16,768]{3,2,1,0:T(8,128)(2,1)} %get-tuple-element.44), channel_id=1, source_target_pairs={{0,6},{1,3},{2,0},{3,5},{4,2},{5,7},{6,4},{7,1},{8,14},{9,11},{10,... | collective-permute-start | bytes 589832 | tf_op jit(solution)/shard_map/ppermute | solution.py:87
  10.3 0.7 collective-permute-start.8
  11.0 1.5 %collective-permute-start.9 = (bf16[2,4,16,768]{3,2,1,0:T(8,128)(2,1)}, bf16[2,4,16,768]{3,2,1,0:T(8,128)(2,1)S(1)}, u32[]{:S(2)}, u32[]{:S(2)}) collective-permute-start(bf16[2,4,16,768]{3,2,1,0:T(8,128)(2,1)} %get-tuple-element.57), channel_id=1, source_target_pairs={{0,2},{1,7},{2,4},{3,1},{4,6},{5,3},{6,0},{7,5},{8,10},{9,15},{10,... | collective-permute-start | bytes 589832 | tf_op jit(solution)/shard_map/ppermute | solution.py:87
  12.5 2.8 %collective-permute-start.10 = (bf16[2,4,16,768]{3,2,1,0:T(8,128)(2,1)}, bf16[2,4,16,768]{3,2,1,0:T(8,128)(2,1)S(1)}, u32[]{:S(2)}, u32[]{:S(2)}) collective-permute-start(bf16[2,4,16,768]{3,2,1,0:T(8,128)(2,1)} %get-tuple-element.59), channel_id=1, source_target_pairs={{0,3},{1,6},{2,5},{3,0},{4,7},{5,2},{6,1},{7,4},{8,11},{9,14},{10,... | collective-permute-start | bytes 589832 | tf_op jit(solution)/shard_map/ppermute | solution.py:87
  15.3 6.2 %synthesis.3 = (bf16[2,4,16,768]{3,2,1,0:T(8,128)(2,1)}, bf16[2,4,16,768]{3,2,1,0:T(8,128)(2,1)}, bf16[2,4,16,768]{3,2,1,0:T(8,128)(2,1)}, bf16[2,4,16,768]{3,2,...) custom-call(s32[1]{0:T(128)} %bitcast.2.me, ...), custom_call_target="tpu_custom_call" | custom-call | flops 603979776 | bytes 8000000 | tf_op jit(solution)/shard_map/synthesis/pallas_call | solution.py:130
  21.5 2.2 %collective-permute-done.refs_4_ = bf16[2,4,16,768]{3,2,1,0:T(8,128)(2,1)S(1)} collective-permute-done((bf16[2,4,16,768]{3,2,1,0:T(8,128)(2,1)}, bf16[2,4,16,768]{3,2,1,0:T(8,128)(2,1)S(1)}, u32[]{:S(2)}, u32[]{:S(2)}) %collective-permute-start) | collective-permute-done | bytes 196640 | tf_op jit(solution)/shard_map/ppermute | solution.py:87
  23.7 0.0 collective-permute-start.11
  23.7 0.0 collective-permute-done.7.refs_1_
  23.7 0.1 collective-permute-start.12
  23.9 5.1 %collective-permute-start.13 = (bf16[2,4,16,768]{3,2,1,0:T(8,128)(2,1)}, bf16[2,4,16,768]{3,2,1,0:T(8,128)(2,1)S(1)}, u32[]{:S(2)}, u32[]{:S(2)}) collective-permute-start(bf16[2,4,16,768]{3,2,1,0:T(8,128)(2,1)} %get-tuple-element.64), channel_id=1, source_target_pairs={{0,4},{1,5},{2,6},{3,7},{4,0},{5,1},{6,2},{7,3},{8,12},{9,13},{10,... | collective-permute-start | bytes 589832 | tf_op jit(solution)/shard_map/ppermute | solution.py:87
  29.0 0.0 collective-permute-done.10.refs_5_
  29.0 0.1 collective-permute-start.15
  29.1 0.9 collective-permute-done.11.refs_6_
  30.0 3.5 %collective-permute-start.16 = (bf16[2,4,16,768]{3,2,1,0:T(8,128)(2,1)}, bf16[2,4,16,768]{3,2,1,0:T(8,128)(2,1)S(1)}, u32[]{:S(2)}, u32[]{:S(2)}) collective-permute-start(bf16[2,4,16,768]{3,2,1,0:T(8,128)(2,1)} %get-tuple-element.67), channel_id=1, source_target_pairs={{0,6},{1,3},{2,0},{3,5},{4,2},{5,7},{6,4},{7,1},{8,14},{9,11},{10,... | collective-permute-start | bytes 589832 | tf_op jit(solution)/shard_map/ppermute | solution.py:87
  33.5 0.3 collective-permute-start.17
  33.8 1.2 %collective-permute-done.13.refs_9_ = bf16[2,4,16,768]{3,2,1,0:T(8,128)(2,1)S(1)} collective-permute-done((bf16[2,4,16,768]{3,2,1,0:T(8,128)(2,1)}, bf16[2,4,16,768]{3,2,1,0:T(8,128)(2,1)S(1)}, u32[]{:S(2)}, u32[]{:S(2)}) %collective-permute-start.13) | collective-permute-done | bytes 196640 | tf_op jit(solution)/shard_map/ppermute | solution.py:87
  35.0 0.7 collective-permute-start.18
  35.7 5.7 %collective-permute-done.14.refs_10_ = bf16[2,4,16,768]{3,2,1,0:T(8,128)(2,1)S(1)} collective-permute-done((bf16[2,4,16,768]{3,2,1,0:T(8,128)(2,1)}, bf16[2,4,16,768]{3,2,1,0:T(8,128)(2,1)S(1)}, u32[]{:S(2)}, u32[]{:S(2)}) %collective-permute-start.14) | collective-permute-done | bytes 196640 | tf_op jit(solution)/shard_map/ppermute | solution.py:87
  41.4 2.9 %collective-permute-done.15.refs_11_ = bf16[2,4,16,768]{3,2,1,0:T(8,128)(2,1)S(1)} collective-permute-done((bf16[2,4,16,768]{3,2,1,0:T(8,128)(2,1)}, bf16[2,4,16,768]{3,2,1,0:T(8,128)(2,1)S(1)}, u32[]{:S(2)}, u32[]{:S(2)}) %collective-permute-start.15) | collective-permute-done | bytes 196640 | tf_op jit(solution)/shard_map/ppermute | solution.py:87
  44.4 3.1 %collective-permute-start.3 = (f32[1,32]{1,0:T(1,128)S(1)}, f32[1,32]{1,0:T(1,128)S(1)}, u32[]{:S(2)}, u32[]{:S(2)}) collective-permute-start(f32[1,32]{1,0:T(1,128)S(1)} %bitcast.14), channel_id=1, source_target_pairs={{0,24},{8,0},{16,8},{24,16},{1,25},{9,1},{17,9},{25,17},{2,26},{10... | collective-permute-start | bytes 392 | tf_op jit(solution)/shard_map/ppermute | solution.py:554
  47.5 0.6 collective-permute-start.2
  48.1 0.0 collective-permute-done.17.refs_13_
  48.1 1.0 collective-permute-start.1
  49.1 0.0 collective-permute-done.18.refs_14_
  49.1 0.0 collective-permute-done.19.refs_15_
  49.2 0.5 copy-done.18
  49.8 0.1 copy-done.19
  49.8 6.6 %grid_product.1 = (bf16[4,32,768]{2,1,0:T(8,128)(2,1)}, bf16[4,32,768]{2,1,0:T(8,128)(2,1)}, bf16[4,32,768]{2,1,0:T(8,128)(2,1)}, bf16[4,32,768]{2,1,0:T(8,128)(...) custom-call(s32[1]{0:T(128)} %bitcast.2.me, ...), custom_call_target="tpu_custom_call" | custom-call | flops 1811939328 | bytes 5000000 | tf_op jit(solution)/shard_map/grid_product/pallas_call | solution.py:180
  56.5 2.0 %collective-permute-start.20 = (bf16[4,32,768]{2,1,0:T(8,128)(2,1)}, bf16[4,32,768]{2,1,0:T(8,128)(2,1)S(1)}, u32[]{:S(2)}, u32[]{:S(2)}) collective-permute-start(bf16[4,32,768]{2,1,0:T(8,128)(2,1)} %get-tuple-element.72), channel_id=1, source_target_pairs={{0,4},{1,5},{2,6},{3,7},{4,0},{5,1},{6,2},{7,3},{8,12},{9,13},{10,... | collective-permute-start | bytes 589832 | tf_op jit(solution)/shard_map/ppermute | solution.py:87
  58.5 1.9 %collective-permute-start.21 = (bf16[4,32,768]{2,1,0:T(8,128)(2,1)}, bf16[4,32,768]{2,1,0:T(8,128)(2,1)S(1)}, u32[]{:S(2)}, u32[]{:S(2)}) collective-permute-start(bf16[4,32,768]{2,1,0:T(8,128)(2,1)} %get-tuple-element.73), channel_id=1, source_target_pairs={{0,5},{1,4},{2,7},{3,6},{4,1},{5,0},{6,3},{7,2},{8,13},{9,12},{10,... | collective-permute-start | bytes 589832 | tf_op jit(solution)/shard_map/ppermute | solution.py:87
  60.5 2.8 %collective-permute-start.6 = (f32[4,32]{1,0:T(4,128)S(1)}, f32[4,32]{1,0:T(4,128)S(1)}, u32[]{:S(2)}, u32[]{:S(2)}) collective-permute-start(f32[4,32]{1,0:T(4,128)S(1)} %get-tuple-element.83.a), channel_id=1, source_target_pairs={{0,96},{32,0},{64,32},{96,64},{1,97},{33,1},{65,33},{97,65},{2,98}... | collective-permute-start | bytes 1544 | tf_op jit(solution)/shard_map/ppermute | solution.py:554
  63.3 0.8 collective-permute-start.5
  64.1 0.9 collective-permute-start.4
  65.0 0.1 pad_add_fusion.1.where
  65.0 0.0 collective-permute-done.6.d
  65.0 0.0 collective-permute-start.22
  65.1 3.3 %collective-permute-done.5.c = f32[4,32]{1,0:T(4,128)S(1)} collective-permute-done((f32[4,32]{1,0:T(4,128)S(1)}, f32[4,32]{1,0:T(4,128)S(1)}, u32[]{:S(2)}, u32[]{:S(2)}) %collective-permute-start.5) | collective-permute-done | bytes 544 | tf_op jit(solution)/shard_map/ppermute | solution.py:554
  68.4 0.5 collective-permute-done.4.b
  68.9 1.8 %collective-permute-start.25 = (bf16[4,32,768]{2,1,0:T(8,128)(2,1)}, bf16[4,32,768]{2,1,0:T(8,128)(2,1)S(1)}, u32[]{:S(2)}, u32[]{:S(2)}) collective-permute-start(bf16[4,32,768]{2,1,0:T(8,128)(2,1)} %get-tuple-element.77), channel_id=1, source_target_pairs={{0,7},{1,2},{2,1},{3,4},{4,3},{5,6},{6,5},{7,0},{8,15},{9,10},{10,... | collective-permute-start | bytes 589832 | tf_op jit(solution)/shard_map/ppermute | solution.py:87
  70.7 0.0 collective-permute-done.21.refs_2_
  70.7 1.3 %collective-permute-start.26 = (bf16[4,32,768]{2,1,0:T(8,128)(2,1)}, bf16[4,32,768]{2,1,0:T(8,128)(2,1)S(1)}, u32[]{:S(2)}, u32[]{:S(2)}) collective-permute-start(bf16[4,32,768]{2,1,0:T(8,128)(2,1)} %get-tuple-element.78), channel_id=1, source_target_pairs={{0,1},{1,0},{2,3},{3,2},{4,5},{5,4},{6,7},{7,6},{8,9},{9,8},{10,11... | collective-permute-start | bytes 589832 | tf_op jit(solution)/shard_map/ppermute | solution.py:87
  72.1 1.4 %block_matrix.1 = (f32[32,96,128]{2,1,0:T(8,128)S(1)}, f32[32,96,128]{2,1,0:T(8,128)S(1)}, f32[32,96,128]{2,1,0:T(8,128)S(1)}) custom-call(f32[4,32]{1,0:T(4,128)S(1)} %get-tuple-element.84.shell, f32[96,128]{1,0:T(8,128)S(1)} %add_multiply_fusion.angular), custom_call_target="tpu_custom_call" | custom-call | flops 10000000 | bytes 6000000 | tf_op jit(solution)/shard_map/block_matrix/pallas_call | solution.py:223
  73.4 0.0 copy-start
  73.5 1.1 %copy-done = f32[32,96,128]{2,1,0:T(8,128)} copy-done((f32[32,96,128]{2,1,0:T(8,128)}, f32[32,96,128]{2,1,0:T(8,128)S(1)}, u32[]{:S(2)}) %copy-start) | copy-done | bytes 1572888
  74.6 3.0 %levels.1 = (f32[2304,128]{1,0:T(8,128)S(1)}, f32[2304,128]{1,0:T(8,128)S(1)}) custom-call(s32[3]{0:T(128)S(1)} %pad_add_fusion.1.where, f32[4,32]{1,0:T(4,128)S(1)} %get-tuple-element.83.a, f32[4,32]{1,0:T(4,128)S(1)} %collective-permute-done.4.b, f32[4,32]{1,0:T(4,128)S(1)} %collective-permute-done.5.c, f32[4,32]{1,0:T(4,128)S(1)} %collective-permute-done.6.d), custom_call_target="tpu_custom_call" | custom-call | flops 10000000 | bytes 8000000 | tf_op jit(solution)/shard_map/levels/pallas_call | solution.py:336
  77.6 0.0 collective-permute-done.22.refs_3_
  77.6 0.0 collective-permute-done.23.refs_4_
  77.7 0.9 copy-done.1
  78.6 11.3 %forcing_solve.1 = (f32[32,96,128]{2,1,0:T(8,128)S(1)}, bf16[2,96,128]{2,1,0:T(8,128)(2,1)S(1)}) custom-call(s32[1]{0:T(128)} %bitcast.2.me, f32[4,32]{1,0:T(4,128)S(1)} %get-tuple-element.84.shell, f32[32,16,2,384]{3,2,1,0:T(2,128)} %field.5, f32[32,96,128]{2,1,0:T(8,128)} %copy-done, bf16[16,384,768]{2,1,0:T(8,128)(2,1)} %legendre.5, ...), custom_call_target="tpu_custom_call" | custom-call | flops 603979776 | bytes 16000000 | tf_op jit(solution)/shard_map/forcing_solve/pallas_call | solution.py:398
  89.9 2.0 %collective-permute-start.29 = (bf16[2,96,128]{2,1,0:T(8,128)(2,1)S(1)}, bf16[2,96,128]{2,1,0:T(8,128)(2,1)S(1)}, u32[]{:S(2)}, u32[]{:S(2)}) collective-permute-start(bf16[2,96,128]{2,1,0:T(8,128)(2,1)S(1)} %get-tuple-element.79.a), channel_id=1, source_target_pairs={{0,24},{8,0},{16,8},{24,16},{1,25},{9,1},{17,9},{25,17},{2,26},{10... | collective-permute-start | bytes 147464 | tf_op jit(solution)/shard_map/ppermute | solution.py:554
  91.9 1.7 %collective-permute-start.28 = (bf16[2,96,128]{2,1,0:T(8,128)(2,1)S(1)}, bf16[2,96,128]{2,1,0:T(8,128)(2,1)S(1)}, u32[]{:S(2)}, u32[]{:S(2)}) collective-permute-start(bf16[2,96,128]{2,1,0:T(8,128)(2,1)S(1)} %get-tuple-element.79.a), channel_id=1, source_target_pairs={{0,16},{8,24},{16,0},{24,8},{1,17},{9,25},{17,1},{25,9},{2,18},{10... | collective-permute-start | bytes 147464 | tf_op jit(solution)/shard_map/ppermute | solution.py:554
  93.6 0.6 collective-permute-start.27
  94.3 0.1 pad_add_fusion.place
  94.4 3.4 %collective-permute-done.28.c = bf16[2,96,128]{2,1,0:T(8,128)(2,1)S(1)} collective-permute-done((bf16[2,96,128]{2,1,0:T(8,128)(2,1)S(1)}, bf16[2,96,128]{2,1,0:T(8,128)(2,1)S(1)}, u32[]{:S(2)}, u32[]{:S(2)}) %collective-permute-start.28) | collective-permute-done | bytes 49184 | tf_op jit(solution)/shard_map/ppermute | solution.py:554
  97.7 1.5 %collective-permute-done.27.b = bf16[2,96,128]{2,1,0:T(8,128)(2,1)S(1)} collective-permute-done((bf16[2,96,128]{2,1,0:T(8,128)(2,1)S(1)}, bf16[2,96,128]{2,1,0:T(8,128)(2,1)S(1)}, u32[]{:S(2)}, u32[]{:S(2)}) %collective-permute-start.27) | collective-permute-done | bytes 49184 | tf_op jit(solution)/shard_map/ppermute | solution.py:554
  99.2 1.2 %inner_join.1.e = bf16[2,96,128]{2,1,0:T(8,128)(2,1)S(1)} custom-call(s32[2]{0:T(128)S(1)} %pad_add_fusion.place, f32[4,6,96,128]{3,2,1,0:T(8,128)S(1)} %bitcast.11, bf16[2,96,128]{2,1,0:T(8,128)(2,1)S(1)} %get-tuple-element.79.a, bf16[2,96,128]{2,1,0:T(8,128)(2,1)S(1)} %collective-permute-done.27.b, bf16[2,96,128]{2,1,0:T(8,128)(2,1)S(1)} %collective-permute-done.28.c, ...), custom_call_target="tpu_custom_call" | custom-call | flops 1000000 | bytes 2000000 | tf_op jit(solution)/shard_map/inner_join/pallas_call | solution.py:468
  100.4 2.4 %collective-permute-start.32 = (bf16[2,96,128]{2,1,0:T(8,128)(2,1)S(1)}, bf16[2,96,128]{2,1,0:T(8,128)(2,1)S(1)}, u32[]{:S(2)}, u32[]{:S(2)}) collective-permute-start(bf16[2,96,128]{2,1,0:T(8,128)(2,1)S(1)} %inner_join.1.e), channel_id=1, source_target_pairs={{0,96},{32,0},{64,32},{96,64},{1,97},{33,1},{65,33},{97,65},{2,98}... | collective-permute-start | bytes 147464 | tf_op jit(solution)/shard_map/ppermute | solution.py:554
  102.8 1.1 collective-permute-start.31
  103.9 0.9 collective-permute-start.30
  104.7 0.2 collective-permute-done.32.h
  104.9 3.5 %collective-permute-done.31.g = bf16[2,96,128]{2,1,0:T(8,128)(2,1)S(1)} collective-permute-done((bf16[2,96,128]{2,1,0:T(8,128)(2,1)S(1)}, bf16[2,96,128]{2,1,0:T(8,128)(2,1)S(1)}, u32[]{:S(2)}, u32[]{:S(2)}) %collective-permute-start.31) | collective-permute-done | bytes 49184 | tf_op jit(solution)/shard_map/ppermute | solution.py:554
  108.4 0.8 collective-permute-done.30.f
  109.2 3.6 %final_join.1 = f32[32,16,2,384]{3,2,1,0:T(2,128)} custom-call(s32[2]{0:T(128)S(1)} %pad_add_fusion.place, f32[4,6,96,128]{3,2,1,0:T(8,128)S(1)} %bitcast.12, f32[4,6,96,128]{3,2,1,0:T(8,128)S(1)} %bitcast.13, bf16[2,96,128]{2,1,0:T(8,128)(2,1)S(1)} %get-tuple-element.79.a, bf16[2,96,128]{2,1,0:T(8,128)(2,1)S(1)} %collective-permute-done.27.b, ...), custom_call_target="tpu_custom_call" | custom-call | flops 3000000 | bytes 9000000 | tf_op jit(solution)/shard_map/final_join/pallas_call | solution.py:529
  (56 shorter events, 0.2 us)
Async XLA Ops:
  6.1 17.6 %collective-permute-start = (bf16[2,4,16,768]{3,2,1,0:T(8,128)(2,1)}, bf16[2,4,16,768]{3,2,1,0:T(8,128)(2,1)S(1)}, u32[]{:S(2)}, u32[]{:S(2)}) collective-permute-start(bf16[2,4,16,768]{3,2,1,0:T(8,128)(2,1)} %get-tuple-element.44), channel_id=1, source_target_pairs={{0,6},{1,3},{2,0},{3,5},{4,2},{5,7},{6,4},{7,1},{8,14},{9,11},{10,... | collective-permute-start | bytes 589832 | tf_op jit(solution)/shard_map/ppermute | solution.py:87
  10.3 13.4 %collective-permute-start.7 = (bf16[2,4,16,768]{3,2,1,0:T(8,128)(2,1)}, bf16[2,4,16,768]{3,2,1,0:T(8,128)(2,1)S(1)}, u32[]{:S(2)}, u32[]{:S(2)}) collective-permute-start(bf16[2,4,16,768]{3,2,1,0:T(8,128)(2,1)} %get-tuple-element.55), channel_id=1, source_target_pairs={{0,4},{1,5},{2,6},{3,7},{4,0},{5,1},{6,2},{7,3},{8,12},{9,13},{10,... | collective-permute-start | bytes 589832 | tf_op jit(solution)/shard_map/ppermute | solution.py:87
  10.3 13.5 %collective-permute-start.8 = (bf16[2,4,16,768]{3,2,1,0:T(8,128)(2,1)}, bf16[2,4,16,768]{3,2,1,0:T(8,128)(2,1)S(1)}, u32[]{:S(2)}, u32[]{:S(2)}) collective-permute-start(bf16[2,4,16,768]{3,2,1,0:T(8,128)(2,1)} %get-tuple-element.56), channel_id=1, source_target_pairs={{0,5},{1,4},{2,7},{3,6},{4,1},{5,0},{6,3},{7,2},{8,13},{9,12},{10,... | collective-permute-start | bytes 589832 | tf_op jit(solution)/shard_map/ppermute | solution.py:87
  11.0 18.0 %collective-permute-start.9 = (bf16[2,4,16,768]{3,2,1,0:T(8,128)(2,1)}, bf16[2,4,16,768]{3,2,1,0:T(8,128)(2,1)S(1)}, u32[]{:S(2)}, u32[]{:S(2)}) collective-permute-start(bf16[2,4,16,768]{3,2,1,0:T(8,128)(2,1)} %get-tuple-element.57), channel_id=1, source_target_pairs={{0,2},{1,7},{2,4},{3,1},{4,6},{5,3},{6,0},{7,5},{8,10},{9,15},{10,... | collective-permute-start | bytes 589832 | tf_op jit(solution)/shard_map/ppermute | solution.py:87
  12.5 16.5 %collective-permute-start.10 = (bf16[2,4,16,768]{3,2,1,0:T(8,128)(2,1)}, bf16[2,4,16,768]{3,2,1,0:T(8,128)(2,1)S(1)}, u32[]{:S(2)}, u32[]{:S(2)}) collective-permute-start(bf16[2,4,16,768]{3,2,1,0:T(8,128)(2,1)} %get-tuple-element.59), channel_id=1, source_target_pairs={{0,3},{1,6},{2,5},{3,0},{4,7},{5,2},{6,1},{7,4},{8,11},{9,14},{10,... | collective-permute-start | bytes 589832 | tf_op jit(solution)/shard_map/ppermute | solution.py:87
  15.3 8.4 %copy-start.14 = (bf16[2,4,16,768]{3,2,1,0:T(8,128)(2,1)S(1)}, bf16[2,4,16,768]{3,2,1,0:T(8,128)(2,1)}, u32[]{:S(2)}) copy-start(bf16[2,4,16,768]{3,2,1,0:T(8,128)(2,1)} %get-tuple-element.60) | copy-start | bytes 589828
  15.3 8.4 %copy-start.13 = (bf16[2,4,16,768]{3,2,1,0:T(8,128)(2,1)S(1)}, bf16[2,4,16,768]{3,2,1,0:T(8,128)(2,1)}, u32[]{:S(2)}) copy-start(bf16[2,4,16,768]{3,2,1,0:T(8,128)(2,1)} %get-tuple-element.61) | copy-start | bytes 589828
  15.3 26.1 %copy-start.3 = (f32[32]{0:T(128)S(1)}, f32[32]{0:T(128)}, u32[]{:S(2)}) copy-start(f32[32]{0:T(128)} %param.10) | copy-start | bytes 388
  23.7 25.4 %copy-start.4 = (bf16[2,4,16,768]{3,2,1,0:T(8,128)(2,1)}, bf16[2,4,16,768]{3,2,1,0:T(8,128)(2,1)S(1)}, u32[]{:S(2)}) copy-start(bf16[2,4,16,768]{3,2,1,0:T(8,128)(2,1)S(1)} %collective-permute-done.refs_4_) | copy-start | bytes 589828
  23.7 6.3 %collective-permute-start.11 = (bf16[2,4,16,768]{3,2,1,0:T(8,128)(2,1)S(1)}, bf16[2,4,16,768]{3,2,1,0:T(8,128)(2,1)S(1)}, u32[]{:S(2)}, u32[]{:S(2)}) collective-permute-start(bf16[2,4,16,768]{3,2,1,0:T(8,128)(2,1)S(1)} %copy-done.14), channel_id=1, source_target_pairs={{0,7},{1,2},{2,1},{3,4},{4,3},{5,6},{6,5},{7,0},{8,15},{9,10},{10,... | collective-permute-start | bytes 589832 | tf_op jit(solution)/shard_map/ppermute | solution.py:87
  23.7 25.4 %copy-start.5 = (bf16[2,4,16,768]{3,2,1,0:T(8,128)(2,1)}, bf16[2,4,16,768]{3,2,1,0:T(8,128)(2,1)S(1)}, u32[]{:S(2)}) copy-start(bf16[2,4,16,768]{3,2,1,0:T(8,128)(2,1)S(1)} %collective-permute-done.7.refs_1_) | copy-start | bytes 589828
  23.7 9.8 %collective-permute-start.12 = (bf16[2,4,16,768]{3,2,1,0:T(8,128)(2,1)S(1)}, bf16[2,4,16,768]{3,2,1,0:T(8,128)(2,1)S(1)}, u32[]{:S(2)}, u32[]{:S(2)}) collective-permute-start(bf16[2,4,16,768]{3,2,1,0:T(8,128)(2,1)S(1)} %copy-done.13), channel_id=1, source_target_pairs={{0,1},{1,0},{2,3},{3,2},{4,5},{5,4},{6,7},{7,6},{8,9},{9,8},{10,11... | collective-permute-start | bytes 589832 | tf_op jit(solution)/shard_map/ppermute | solution.py:87
  23.8 25.3 %copy-start.6 = (bf16[2,4,16,768]{3,2,1,0:T(8,128)(2,1)}, bf16[2,4,16,768]{3,2,1,0:T(8,128)(2,1)S(1)}, u32[]{:S(2)}) copy-start(bf16[2,4,16,768]{3,2,1,0:T(8,128)(2,1)S(1)} %collective-permute-done.8.refs_2_) | copy-start | bytes 589828
  23.9 11.2 %collective-permute-start.13 = (bf16[2,4,16,768]{3,2,1,0:T(8,128)(2,1)}, bf16[2,4,16,768]{3,2,1,0:T(8,128)(2,1)S(1)}, u32[]{:S(2)}, u32[]{:S(2)}) collective-permute-start(bf16[2,4,16,768]{3,2,1,0:T(8,128)(2,1)} %get-tuple-element.64), channel_id=1, source_target_pairs={{0,4},{1,5},{2,6},{3,7},{4,0},{5,1},{6,2},{7,3},{8,12},{9,13},{10,... | collective-permute-start | bytes 589832 | tf_op jit(solution)/shard_map/ppermute | solution.py:87
  29.0 20.2 %copy-start.7 = (bf16[2,4,16,768]{3,2,1,0:T(8,128)(2,1)}, bf16[2,4,16,768]{3,2,1,0:T(8,128)(2,1)S(1)}, u32[]{:S(2)}) copy-start(bf16[2,4,16,768]{3,2,1,0:T(8,128)(2,1)S(1)} %collective-permute-done.9.refs_3_) | copy-start | bytes 589828
  29.0 12.4 %collective-permute-start.14 = (bf16[2,4,16,768]{3,2,1,0:T(8,128)(2,1)}, bf16[2,4,16,768]{3,2,1,0:T(8,128)(2,1)S(1)}, u32[]{:S(2)}, u32[]{:S(2)}) collective-permute-start(bf16[2,4,16,768]{3,2,1,0:T(8,128)(2,1)} %get-tuple-element.65), channel_id=1, source_target_pairs={{0,5},{1,4},{2,7},{3,6},{4,1},{5,0},{6,3},{7,2},{8,13},{9,12},{10,... | collective-permute-start | bytes 589832 | tf_op jit(solution)/shard_map/ppermute | solution.py:87
  29.0 20.1 %copy-start.8 = (bf16[2,4,16,768]{3,2,1,0:T(8,128)(2,1)}, bf16[2,4,16,768]{3,2,1,0:T(8,128)(2,1)S(1)}, u32[]{:S(2)}) copy-start(bf16[2,4,16,768]{3,2,1,0:T(8,128)(2,1)S(1)} %collective-permute-done.10.refs_5_) | copy-start | bytes 589828
  29.0 15.4 %collective-permute-start.15 = (bf16[2,4,16,768]{3,2,1,0:T(8,128)(2,1)}, bf16[2,4,16,768]{3,2,1,0:T(8,128)(2,1)S(1)}, u32[]{:S(2)}, u32[]{:S(2)}) collective-permute-start(bf16[2,4,16,768]{3,2,1,0:T(8,128)(2,1)} %get-tuple-element.66), channel_id=1, source_target_pairs={{0,2},{1,7},{2,4},{3,1},{4,6},{5,3},{6,0},{7,5},{8,10},{9,15},{10,... | collective-permute-start | bytes 589832 | tf_op jit(solution)/shard_map/ppermute | solution.py:87
  30.0 19.1 %copy-start.9 = (bf16[2,4,16,768]{3,2,1,0:T(8,128)(2,1)}, bf16[2,4,16,768]{3,2,1,0:T(8,128)(2,1)S(1)}, u32[]{:S(2)}) copy-start(bf16[2,4,16,768]{3,2,1,0:T(8,128)(2,1)S(1)} %collective-permute-done.11.refs_6_) | copy-start | bytes 589828
  30.0 17.5 %collective-permute-start.16 = (bf16[2,4,16,768]{3,2,1,0:T(8,128)(2,1)}, bf16[2,4,16,768]{3,2,1,0:T(8,128)(2,1)S(1)}, u32[]{:S(2)}, u32[]{:S(2)}) collective-permute-start(bf16[2,4,16,768]{3,2,1,0:T(8,128)(2,1)} %get-tuple-element.67), channel_id=1, source_target_pairs={{0,6},{1,3},{2,0},{3,5},{4,2},{5,7},{6,4},{7,1},{8,14},{9,11},{10,... | collective-permute-start | bytes 589832 | tf_op jit(solution)/shard_map/ppermute | solution.py:87
  33.5 15.7 %copy-start.10 = (bf16[2,4,16,768]{3,2,1,0:T(8,128)(2,1)}, bf16[2,4,16,768]{3,2,1,0:T(8,128)(2,1)S(1)}, u32[]{:S(2)}) copy-start(bf16[2,4,16,768]{3,2,1,0:T(8,128)(2,1)S(1)} %collective-permute-done.12.refs_7_) | copy-start | bytes 589828
  33.5 14.6 %collective-permute-start.17 = (bf16[2,4,16,768]{3,2,1,0:T(8,128)(2,1)}, bf16[2,4,16,768]{3,2,1,0:T(8,128)(2,1)S(1)}, u32[]{:S(2)}, u32[]{:S(2)}) collective-permute-start(bf16[2,4,16,768]{3,2,1,0:T(8,128)(2,1)} %get-tuple-element.68), channel_id=1, source_target_pairs={{0,3},{1,6},{2,5},{3,0},{4,7},{5,2},{6,1},{7,4},{8,11},{9,14},{10,... | collective-permute-start | bytes 589832 | tf_op jit(solution)/shard_map/ppermute | solution.py:87
  35.0 14.2 %copy-start.11 = (bf16[2,4,16,768]{3,2,1,0:T(8,128)(2,1)}, bf16[2,4,16,768]{3,2,1,0:T(8,128)(2,1)S(1)}, u32[]{:S(2)}) copy-start(bf16[2,4,16,768]{3,2,1,0:T(8,128)(2,1)S(1)} %collective-permute-done.13.refs_9_) | copy-start | bytes 589828
  35.0 14.1 %collective-permute-start.18 = (bf16[2,4,16,768]{3,2,1,0:T(8,128)(2,1)}, bf16[2,4,16,768]{3,2,1,0:T(8,128)(2,1)S(1)}, u32[]{:S(2)}, u32[]{:S(2)}) collective-permute-start(bf16[2,4,16,768]{3,2,1,0:T(8,128)(2,1)} %get-tuple-element.69), channel_id=1, source_target_pairs={{0,7},{1,2},{2,1},{3,4},{4,3},{5,6},{6,5},{7,0},{8,15},{9,10},{10,... | collective-permute-start | bytes 589832 | tf_op jit(solution)/shard_map/ppermute | solution.py:87
  41.4 7.8 %copy-start.12 = (bf16[2,4,16,768]{3,2,1,0:T(8,128)(2,1)}, bf16[2,4,16,768]{3,2,1,0:T(8,128)(2,1)S(1)}, u32[]{:S(2)}) copy-start(bf16[2,4,16,768]{3,2,1,0:T(8,128)(2,1)S(1)} %collective-permute-done.14.refs_10_) | copy-start | bytes 589828
  41.4 7.7 %collective-permute-start.19 = (bf16[2,4,16,768]{3,2,1,0:T(8,128)(2,1)}, bf16[2,4,16,768]{3,2,1,0:T(8,128)(2,1)S(1)}, u32[]{:S(2)}, u32[]{:S(2)}) collective-permute-start(bf16[2,4,16,768]{3,2,1,0:T(8,128)(2,1)} %get-tuple-element.70), channel_id=1, source_target_pairs={{0,1},{1,0},{2,3},{3,2},{4,5},{5,4},{6,7},{7,6},{8,9},{9,8},{10,11... | collective-permute-start | bytes 589832 | tf_op jit(solution)/shard_map/ppermute | solution.py:87
  44.4 4.8 %copy-start.15 = (bf16[2,4,16,768]{3,2,1,0:T(8,128)(2,1)}, bf16[2,4,16,768]{3,2,1,0:T(8,128)(2,1)S(1)}, u32[]{:S(2)}) copy-start(bf16[2,4,16,768]{3,2,1,0:T(8,128)(2,1)S(1)} %collective-permute-done.15.refs_11_) | copy-start | bytes 589828
  44.4 16.0 %collective-permute-start.3 = (f32[1,32]{1,0:T(1,128)S(1)}, f32[1,32]{1,0:T(1,128)S(1)}, u32[]{:S(2)}, u32[]{:S(2)}) collective-permute-start(f32[1,32]{1,0:T(1,128)S(1)} %bitcast.14), channel_id=1, source_target_pairs={{0,24},{8,0},{16,8},{24,16},{1,25},{9,1},{17,9},{25,17},{2,26},{10... | collective-permute-start | bytes 392 | tf_op jit(solution)/shard_map/ppermute | solution.py:554
  47.5 1.7 %copy-start.16 = (bf16[2,4,16,768]{3,2,1,0:T(8,128)(2,1)}, bf16[2,4,16,768]{3,2,1,0:T(8,128)(2,1)S(1)}, u32[]{:S(2)}) copy-start(bf16[2,4,16,768]{3,2,1,0:T(8,128)(2,1)S(1)} %collective-permute-done.16.refs_12_) | copy-start | bytes 589828
  47.5 12.9 %collective-permute-start.2 = (f32[1,32]{1,0:T(1,128)S(1)}, f32[1,32]{1,0:T(1,128)S(1)}, u32[]{:S(2)}, u32[]{:S(2)}) collective-permute-start(f32[1,32]{1,0:T(1,128)S(1)} %bitcast.15), channel_id=1, source_target_pairs={{0,16},{8,24},{16,0},{24,8},{1,17},{9,25},{17,1},{25,9},{2,18},{10... | collective-permute-start | bytes 392 | tf_op jit(solution)/shard_map/ppermute | solution.py:554
  48.1 1.1 copy-start.17
  48.1 12.3 %collective-permute-start.1 = (f32[1,32]{1,0:T(1,128)S(1)}, f32[1,32]{1,0:T(1,128)S(1)}, u32[]{:S(2)}, u32[]{:S(2)}) collective-permute-start(f32[1,32]{1,0:T(1,128)S(1)} %bitcast.16), channel_id=1, source_target_pairs={{0,8},{8,16},{16,24},{24,0},{1,9},{9,17},{17,25},{25,1},{2,10},{10... | collective-permute-start | bytes 392 | tf_op jit(solution)/shard_map/ppermute | solution.py:554
  49.1 0.7 copy-start.18
  49.1 0.7 copy-start.19
  49.8 22.2 %copy-start.2 = (s32[96,128]{1,0:T(8,128)S(1)}, s32[96,128]{1,0:T(8,128)}, u32[]{:S(2)}) copy-start(s32[96,128]{1,0:T(8,128)} %constant.41.clone) | copy-start | bytes 147460
  56.5 12.4 %collective-permute-start.20 = (bf16[4,32,768]{2,1,0:T(8,128)(2,1)}, bf16[4,32,768]{2,1,0:T(8,128)(2,1)S(1)}, u32[]{:S(2)}, u32[]{:S(2)}) collective-permute-start(bf16[4,32,768]{2,1,0:T(8,128)(2,1)} %get-tuple-element.72), channel_id=1, source_target_pairs={{0,4},{1,5},{2,6},{3,7},{4,0},{5,1},{6,2},{7,3},{8,12},{9,13},{10,... | collective-permute-start | bytes 589832 | tf_op jit(solution)/shard_map/ppermute | solution.py:87
  58.5 12.2 %collective-permute-start.21 = (bf16[4,32,768]{2,1,0:T(8,128)(2,1)}, bf16[4,32,768]{2,1,0:T(8,128)(2,1)S(1)}, u32[]{:S(2)}, u32[]{:S(2)}) collective-permute-start(bf16[4,32,768]{2,1,0:T(8,128)(2,1)} %get-tuple-element.73), channel_id=1, source_target_pairs={{0,5},{1,4},{2,7},{3,6},{4,1},{5,0},{6,3},{7,2},{8,13},{9,12},{10,... | collective-permute-start | bytes 589832 | tf_op jit(solution)/shard_map/ppermute | solution.py:87
  60.5 4.6 %collective-permute-start.6 = (f32[4,32]{1,0:T(4,128)S(1)}, f32[4,32]{1,0:T(4,128)S(1)}, u32[]{:S(2)}, u32[]{:S(2)}) collective-permute-start(f32[4,32]{1,0:T(4,128)S(1)} %get-tuple-element.83.a), channel_id=1, source_target_pairs={{0,96},{32,0},{64,32},{96,64},{1,97},{33,1},{65,33},{97,65},{2,98}... | collective-permute-start | bytes 1544 | tf_op jit(solution)/shard_map/ppermute | solution.py:554
  63.3 5.1 %collective-permute-start.5 = (f32[4,32]{1,0:T(4,128)S(1)}, f32[4,32]{1,0:T(4,128)S(1)}, u32[]{:S(2)}, u32[]{:S(2)}) collective-permute-start(f32[4,32]{1,0:T(4,128)S(1)} %get-tuple-element.83.a), channel_id=1, source_target_pairs={{0,64},{32,96},{64,0},{96,32},{1,65},{33,97},{65,1},{97,33},{2,66}... | collective-permute-start | bytes 1544 | tf_op jit(solution)/shard_map/ppermute | solution.py:554
  64.1 4.8 %collective-permute-start.4 = (f32[4,32]{1,0:T(4,128)S(1)}, f32[4,32]{1,0:T(4,128)S(1)}, u32[]{:S(2)}, u32[]{:S(2)}) collective-permute-start(f32[4,32]{1,0:T(4,128)S(1)} %get-tuple-element.83.a), channel_id=1, source_target_pairs={{0,32},{32,64},{64,96},{96,0},{1,33},{33,65},{65,97},{97,1},{2,34}... | collective-permute-start | bytes 1544 | tf_op jit(solution)/shard_map/ppermute | solution.py:554
  65.0 12.6 %collective-permute-start.22 = (bf16[4,32,768]{2,1,0:T(8,128)(2,1)}, bf16[4,32,768]{2,1,0:T(8,128)(2,1)S(1)}, u32[]{:S(2)}, u32[]{:S(2)}) collective-permute-start(bf16[4,32,768]{2,1,0:T(8,128)(2,1)} %get-tuple-element.74), channel_id=1, source_target_pairs={{0,6},{1,3},{2,0},{3,5},{4,2},{5,7},{6,4},{7,1},{8,14},{9,11},{10,... | collective-permute-start | bytes 589832 | tf_op jit(solution)/shard_map/ppermute | solution.py:87
  68.4 9.3 %collective-permute-start.23 = (bf16[4,32,768]{2,1,0:T(8,128)(2,1)}, bf16[4,32,768]{2,1,0:T(8,128)(2,1)S(1)}, u32[]{:S(2)}, u32[]{:S(2)}) collective-permute-start(bf16[4,32,768]{2,1,0:T(8,128)(2,1)} %get-tuple-element.75), channel_id=1, source_target_pairs={{0,2},{1,7},{2,4},{3,1},{4,6},{5,3},{6,0},{7,5},{8,10},{9,15},{10,... | collective-permute-start | bytes 589832 | tf_op jit(solution)/shard_map/ppermute | solution.py:87
  68.9 8.8 %collective-permute-start.24 = (bf16[4,32,768]{2,1,0:T(8,128)(2,1)}, bf16[4,32,768]{2,1,0:T(8,128)(2,1)S(1)}, u32[]{:S(2)}, u32[]{:S(2)}) collective-permute-start(bf16[4,32,768]{2,1,0:T(8,128)(2,1)} %get-tuple-element.76), channel_id=1, source_target_pairs={{0,3},{1,6},{2,5},{3,0},{4,7},{5,2},{6,1},{7,4},{8,11},{9,14},{10,... | collective-permute-start | bytes 589832 | tf_op jit(solution)/shard_map/ppermute | solution.py:87
  68.9 8.8 %collective-permute-start.25 = (bf16[4,32,768]{2,1,0:T(8,128)(2,1)}, bf16[4,32,768]{2,1,0:T(8,128)(2,1)S(1)}, u32[]{:S(2)}, u32[]{:S(2)}) collective-permute-start(bf16[4,32,768]{2,1,0:T(8,128)(2,1)} %get-tuple-element.77), channel_id=1, source_target_pairs={{0,7},{1,2},{2,1},{3,4},{4,3},{5,6},{6,5},{7,0},{8,15},{9,10},{10,... | collective-permute-start | bytes 589832 | tf_op jit(solution)/shard_map/ppermute | solution.py:87
  70.7 7.0 %collective-permute-start.26 = (bf16[4,32,768]{2,1,0:T(8,128)(2,1)}, bf16[4,32,768]{2,1,0:T(8,128)(2,1)S(1)}, u32[]{:S(2)}, u32[]{:S(2)}) collective-permute-start(bf16[4,32,768]{2,1,0:T(8,128)(2,1)} %get-tuple-element.78), channel_id=1, source_target_pairs={{0,1},{1,0},{2,3},{3,2},{4,5},{5,4},{6,7},{7,6},{8,9},{9,8},{10,11... | collective-permute-start | bytes 589832 | tf_op jit(solution)/shard_map/ppermute | solution.py:87
  73.4 1.1 %copy-start = (f32[32,96,128]{2,1,0:T(8,128)}, f32[32,96,128]{2,1,0:T(8,128)S(1)}, u32[]{:S(2)}) copy-start(f32[32,96,128]{2,1,0:T(8,128)S(1)} %get-tuple-element.52.pivots) | copy-start | bytes 4718596
  77.7 0.9 copy-start.1
  89.9 4.4 %collective-permute-start.29 = (bf16[2,96,128]{2,1,0:T(8,128)(2,1)S(1)}, bf16[2,96,128]{2,1,0:T(8,128)(2,1)S(1)}, u32[]{:S(2)}, u32[]{:S(2)}) collective-permute-start(bf16[2,96,128]{2,1,0:T(8,128)(2,1)S(1)} %get-tuple-element.79.a), channel_id=1, source_target_pairs={{0,24},{8,0},{16,8},{24,16},{1,25},{9,1},{17,9},{25,17},{2,26},{10... | collective-permute-start | bytes 147464 | tf_op jit(solution)/shard_map/ppermute | solution.py:554
  91.9 5.8 %collective-permute-start.28 = (bf16[2,96,128]{2,1,0:T(8,128)(2,1)S(1)}, bf16[2,96,128]{2,1,0:T(8,128)(2,1)S(1)}, u32[]{:S(2)}, u32[]{:S(2)}) collective-permute-start(bf16[2,96,128]{2,1,0:T(8,128)(2,1)S(1)} %get-tuple-element.79.a), channel_id=1, source_target_pairs={{0,16},{8,24},{16,0},{24,8},{1,17},{9,25},{17,1},{25,9},{2,18},{10... | collective-permute-start | bytes 147464 | tf_op jit(solution)/shard_map/ppermute | solution.py:554
  93.6 5.6 %collective-permute-start.27 = (bf16[2,96,128]{2,1,0:T(8,128)(2,1)S(1)}, bf16[2,96,128]{2,1,0:T(8,128)(2,1)S(1)}, u32[]{:S(2)}, u32[]{:S(2)}) collective-permute-start(bf16[2,96,128]{2,1,0:T(8,128)(2,1)S(1)} %get-tuple-element.79.a), channel_id=1, source_target_pairs={{0,8},{8,16},{16,24},{24,0},{1,9},{9,17},{17,25},{25,1},{2,10},{10... | collective-permute-start | bytes 147464 | tf_op jit(solution)/shard_map/ppermute | solution.py:554
  100.4 4.5 %collective-permute-start.32 = (bf16[2,96,128]{2,1,0:T(8,128)(2,1)S(1)}, bf16[2,96,128]{2,1,0:T(8,128)(2,1)S(1)}, u32[]{:S(2)}, u32[]{:S(2)}) collective-permute-start(bf16[2,96,128]{2,1,0:T(8,128)(2,1)S(1)} %inner_join.1.e), channel_id=1, source_target_pairs={{0,96},{32,0},{64,32},{96,64},{1,97},{33,1},{65,33},{97,65},{2,98}... | collective-permute-start | bytes 147464 | tf_op jit(solution)/shard_map/ppermute | solution.py:554
  102.8 5.6 %collective-permute-start.31 = (bf16[2,96,128]{2,1,0:T(8,128)(2,1)S(1)}, bf16[2,96,128]{2,1,0:T(8,128)(2,1)S(1)}, u32[]{:S(2)}, u32[]{:S(2)}) collective-permute-start(bf16[2,96,128]{2,1,0:T(8,128)(2,1)S(1)} %inner_join.1.e), channel_id=1, source_target_pairs={{0,64},{32,96},{64,0},{96,32},{1,65},{33,97},{65,1},{97,33},{2,66}... | collective-permute-start | bytes 147464 | tf_op jit(solution)/shard_map/ppermute | solution.py:554
  103.9 5.3 %collective-permute-start.30 = (bf16[2,96,128]{2,1,0:T(8,128)(2,1)S(1)}, bf16[2,96,128]{2,1,0:T(8,128)(2,1)S(1)}, u32[]{:S(2)}, u32[]{:S(2)}) collective-permute-start(bf16[2,96,128]{2,1,0:T(8,128)(2,1)S(1)} %inner_join.1.e), channel_id=1, source_target_pairs={{0,32},{32,64},{64,96},{96,0},{1,33},{33,65},{65,97},{97,1},{2,34}... | collective-permute-start | bytes 147464 | tf_op jit(solution)/shard_map/ppermute | solution.py:554

commit v5 on v4

--- a/solution.py
+++ b/solution.py
@@ -354,27 +354,21 @@
 
 def forcing_kernel(me, shell, field, pivots, legendre, *refs):
     slots = refs[:NMODE]
-    solved, ends, modes, table, sems, table_sems = refs[NMODE:]
+    solved, ends, modes, sems = refs[NMODE:]
     copies = [
         pltpu.make_async_copy(
             slots[k], modes.at[pl.ds(moved(me[0], k, False) * NSHELL, NSHELL)], sems.at[k]
         )
         for k in range(NMODE)
     ]
-    tables = [
-        pltpu.make_async_copy(legendre.at[m], table.at[m], table_sems.at[m]) for m in range(ORD)
-    ]
-    for copy in copies + tables[:AHEAD]:
+    for copy in copies:
         copy.start()
     for copy in copies:
         copy.wait()
     for m in range(ORD):
-        if m + AHEAD < ORD:
-            tables[m + AHEAD].start()
-        tables[m].wait()
         lat = modes[:, HALVES * m : HALVES * (m + 1), :].reshape(SHELLS * HALVES, NLAT)
         forcing = lax.dot_general(
-            lat, table[m], (((1,), (1,)), ((), ())), preferred_element_type=F32
+            lat, legendre[m], (((1,), (1,)), ((), ())), preferred_element_type=F32
         )
         right_side = field[:, m].reshape(SHELLS * HALVES, DEG) + forcing
         for tile in range(TILES):
@@ -401,15 +395,13 @@
             jax.ShapeDtypeStruct((SHELLS, ROWS, LANES), F32),
             jax.ShapeDtypeStruct((2, ROWS, LANES), BF16),
         ),
-        in_specs=[whole(pltpu.SMEM)] * 2 + [whole()] * 2 + [whole(pl.ANY)] * (1 + NMODE),
+        in_specs=[whole(pltpu.SMEM)] * 2 + [whole()] * 3 + [whole(pl.ANY)] * NMODE,
         out_specs=(whole(), whole()),
         scratch_shapes=[
             pltpu.VMEM((SHELLS, PAIRS, NLAT), BF16),
-            pltpu.VMEM((ORD, DEG, NLAT), BF16),
             pltpu.SemaphoreType.DMA((NMODE,)),
-            pltpu.SemaphoreType.DMA((ORD,)),
         ],
-        compiler_params=params(50),
+        compiler_params=params(20),
         cost_estimate=cost(2 * 64 * DEG * NLAT * ORD, 16_000_000),
         name="forcing_solve",
     )(me, shell, field, pivots, legendre, *slots)

time: 113 us -> 112 us (level)
  Pallas kernels: 39.4 us -> 34.4 us
  local copies, waits for them, and re-layouts: 2.73 us -> 5.27 us
    pallas_call x1, Pallas kernels: 11.3 us -> 6.23 us  [forcing_solve(): pl.pallas_call(forcing_kernel, out_shape=(jax.ShapeDtypeStruct((SHELLS, R...]
    unnamed x40 -> x42, local copies, waits for them, and re-layouts: 2.73 us -> 5.27 us
where the time goes in v5:
time: 112 us
  starting transfers between devices  44.1 us (39%)
  Pallas kernels  34.4 us (31%)
  waiting for transfers between devices  27.1 us (24%)
  local copies, waits for them, and re-layouts  5.27 us (5%)
    ppermute x21, starting transfers between devices, moved_all(): sent.append(lax.ppermute(arrays[k], MODE, pairs))  26 us
    ppermute x12, starting transfers between devices, shifted(): lax.ppermute(array, axis, [(i, (i + step) % size) for i in range(size)])  18.1 us
    ppermute x21, waiting for transfers between devices, moved_all(): sent.append(lax.ppermute(arrays[k], MODE, pairs))  14.1 us
    ppermute x12, waiting for transfers between devices, shifted(): lax.ppermute(array, axis, [(i, (i + step) % size) for i in range(size)])  13 us
    pallas_call x2, Pallas kernels, synthesis(): pl.pallas_call(functools.partial(synthesis_kernel, half), out_shape=(shap...  12.3 us
    pallas_call x1, Pallas kernels, grid_product(): pl.pallas_call(grid_kernel, out_shape=(shape,) * NMODE, in_specs=[whole(p...  6.73 us
    pallas_call x1, Pallas kernels, forcing_solve(): pl.pallas_call(forcing_kernel, out_shape=(jax.ShapeDtypeStruct((SHELLS, R...  6.23 us
    unnamed x42, local copies, waits for them, and re-layouts  5.27 us
  transfers between devices with their start and end apart: 33, of which 12 were waited for; matrix products, arithmetic and copies ran while one was open for 0% of the time, Pallas kernels for 15%

profile of v5, /device:TPU:0, one launch (start us, length us, event | category | flops | bytes accessed | tf_op | source)
XLA Modules:
  0.0 111.6 jit_solution(12834027972171756309)
XLA Ops:
  0.0 6.1 %synthesis.2 = (bf16[2,4,16,768]{3,2,1,0:T(8,128)(2,1)}, bf16[2,4,16,768]{3,2,1,0:T(8,128)(2,1)}, bf16[2,4,16,768]{3,2,1,0:T(8,128)(2,1)}, bf16[2,4,16,768]{3,2,...) custom-call(s32[1]{0:T(128)} %bitcast.2.me, ...), custom_call_target="tpu_custom_call" | custom-call | flops 603979776 | bytes 8000000 | tf_op jit(solution)/shard_map/synthesis/pallas_call | solution.py:130
  6.1 4.2 %collective-permute-start = (bf16[2,4,16,768]{3,2,1,0:T(8,128)(2,1)}, bf16[2,4,16,768]{3,2,1,0:T(8,128)(2,1)S(1)}, u32[]{:S(2)}, u32[]{:S(2)}) collective-permute-start(bf16[2,4,16,768]{3,2,1,0:T(8,128)(2,1)} %get-tuple-element.44), channel_id=1, source_target_pairs={{0,6},{1,3},{2,0},{3,5},{4,2},{5,7},{6,4},{7,1},{8,14},{9,11},{10,... | collective-permute-start | bytes 589832 | tf_op jit(solution)/shard_map/ppermute | solution.py:87
  10.3 0.7 collective-permute-start.8
  11.0 1.5 %collective-permute-start.9 = (bf16[2,4,16,768]{3,2,1,0:T(8,128)(2,1)}, bf16[2,4,16,768]{3,2,1,0:T(8,128)(2,1)S(1)}, u32[]{:S(2)}, u32[]{:S(2)}) collective-permute-start(bf16[2,4,16,768]{3,2,1,0:T(8,128)(2,1)} %get-tuple-element.57), channel_id=1, source_target_pairs={{0,2},{1,7},{2,4},{3,1},{4,6},{5,3},{6,0},{7,5},{8,10},{9,15},{10,... | collective-permute-start | bytes 589832 | tf_op jit(solution)/shard_map/ppermute | solution.py:87
  12.5 2.8 %collective-permute-start.10 = (bf16[2,4,16,768]{3,2,1,0:T(8,128)(2,1)}, bf16[2,4,16,768]{3,2,1,0:T(8,128)(2,1)S(1)}, u32[]{:S(2)}, u32[]{:S(2)}) collective-permute-start(bf16[2,4,16,768]{3,2,1,0:T(8,128)(2,1)} %get-tuple-element.59), channel_id=1, source_target_pairs={{0,3},{1,6},{2,5},{3,0},{4,7},{5,2},{6,1},{7,4},{8,11},{9,14},{10,... | collective-permute-start | bytes 589832 | tf_op jit(solution)/shard_map/ppermute | solution.py:87
  15.3 6.2 %synthesis.3 = (bf16[2,4,16,768]{3,2,1,0:T(8,128)(2,1)}, bf16[2,4,16,768]{3,2,1,0:T(8,128)(2,1)}, bf16[2,4,16,768]{3,2,1,0:T(8,128)(2,1)}, bf16[2,4,16,768]{3,2,...) custom-call(s32[1]{0:T(128)} %bitcast.2.me, ...), custom_call_target="tpu_custom_call" | custom-call | flops 603979776 | bytes 8000000 | tf_op jit(solution)/shard_map/synthesis/pallas_call | solution.py:130
  21.5 2.2 %collective-permute-done.refs_4_ = bf16[2,4,16,768]{3,2,1,0:T(8,128)(2,1)S(1)} collective-permute-done((bf16[2,4,16,768]{3,2,1,0:T(8,128)(2,1)}, bf16[2,4,16,768]{3,2,1,0:T(8,128)(2,1)S(1)}, u32[]{:S(2)}, u32[]{:S(2)}) %collective-permute-start) | collective-permute-done | bytes 196640 | tf_op jit(solution)/shard_map/ppermute | solution.py:87
  23.7 0.0 collective-permute-start.11
  23.7 0.0 collective-permute-done.7.refs_1_
  23.7 0.1 collective-permute-start.12
  23.8 0.0 collective-permute-done.8.refs_2_
  23.9 5.1 %collective-permute-start.13 = (bf16[2,4,16,768]{3,2,1,0:T(8,128)(2,1)}, bf16[2,4,16,768]{3,2,1,0:T(8,128)(2,1)S(1)}, u32[]{:S(2)}, u32[]{:S(2)}) collective-permute-start(bf16[2,4,16,768]{3,2,1,0:T(8,128)(2,1)} %get-tuple-element.64), channel_id=1, source_target_pairs={{0,4},{1,5},{2,6},{3,7},{4,0},{5,1},{6,2},{7,3},{8,12},{9,13},{10,... | collective-permute-start | bytes 589832 | tf_op jit(solution)/shard_map/ppermute | solution.py:87
  29.0 0.0 collective-permute-done.9.refs_3_
  29.0 0.0 collective-permute-start.14
  29.0 0.0 collective-permute-done.10.refs_5_
  29.0 0.1 collective-permute-start.15
  29.1 0.9 collective-permute-done.11.refs_6_
  30.0 3.5 %collective-permute-start.16 = (bf16[2,4,16,768]{3,2,1,0:T(8,128)(2,1)}, bf16[2,4,16,768]{3,2,1,0:T(8,128)(2,1)S(1)}, u32[]{:S(2)}, u32[]{:S(2)}) collective-permute-start(bf16[2,4,16,768]{3,2,1,0:T(8,128)(2,1)} %get-tuple-element.67), channel_id=1, source_target_pairs={{0,6},{1,3},{2,0},{3,5},{4,2},{5,7},{6,4},{7,1},{8,14},{9,11},{10,... | collective-permute-start | bytes 589832 | tf_op jit(solution)/shard_map/ppermute | solution.py:87
  33.5 0.0 collective-permute-done.12.refs_7_
  33.5 0.3 collective-permute-start.17
  33.8 1.2 %collective-permute-done.13.refs_9_ = bf16[2,4,16,768]{3,2,1,0:T(8,128)(2,1)S(1)} collective-permute-done((bf16[2,4,16,768]{3,2,1,0:T(8,128)(2,1)}, bf16[2,4,16,768]{3,2,1,0:T(8,128)(2,1)S(1)}, u32[]{:S(2)}, u32[]{:S(2)}) %collective-permute-start.13) | collective-permute-done | bytes 196640 | tf_op jit(solution)/shard_map/ppermute | solution.py:87
  35.0 0.7 collective-permute-start.18
  35.7 5.7 %collective-permute-done.14.refs_10_ = bf16[2,4,16,768]{3,2,1,0:T(8,128)(2,1)S(1)} collective-permute-done((bf16[2,4,16,768]{3,2,1,0:T(8,128)(2,1)}, bf16[2,4,16,768]{3,2,1,0:T(8,128)(2,1)S(1)}, u32[]{:S(2)}, u32[]{:S(2)}) %collective-permute-start.14) | collective-permute-done | bytes 196640 | tf_op jit(solution)/shard_map/ppermute | solution.py:87
  41.4 2.9 %collective-permute-done.15.refs_11_ = bf16[2,4,16,768]{3,2,1,0:T(8,128)(2,1)S(1)} collective-permute-done((bf16[2,4,16,768]{3,2,1,0:T(8,128)(2,1)}, bf16[2,4,16,768]{3,2,1,0:T(8,128)(2,1)S(1)}, u32[]{:S(2)}, u32[]{:S(2)}) %collective-permute-start.15) | collective-permute-done | bytes 196640 | tf_op jit(solution)/shard_map/ppermute | solution.py:87
  44.4 3.1 %collective-permute-start.3 = (f32[1,32]{1,0:T(1,128)S(1)}, f32[1,32]{1,0:T(1,128)S(1)}, u32[]{:S(2)}, u32[]{:S(2)}) collective-permute-start(f32[1,32]{1,0:T(1,128)S(1)} %bitcast.14), channel_id=1, source_target_pairs={{0,24},{8,0},{16,8},{24,16},{1,25},{9,1},{17,9},{25,17},{2,26},{10... | collective-permute-start | bytes 392 | tf_op jit(solution)/shard_map/ppermute | solution.py:546
  47.5 0.0 collective-permute-done.16.refs_12_
  47.5 0.6 collective-permute-start.2
  48.1 1.0 collective-permute-start.1
  49.2 0.5 copy-done.19
  49.8 0.1 copy-done.20
  49.8 6.7 %grid_product.1 = (bf16[4,32,768]{2,1,0:T(8,128)(2,1)}, bf16[4,32,768]{2,1,0:T(8,128)(2,1)}, bf16[4,32,768]{2,1,0:T(8,128)(2,1)}, bf16[4,32,768]{2,1,0:T(8,128)(...) custom-call(s32[1]{0:T(128)} %bitcast.2.me, ...), custom_call_target="tpu_custom_call" | custom-call | flops 1811939328 | bytes 5000000 | tf_op jit(solution)/shard_map/grid_product/pallas_call | solution.py:180
  56.6 2.0 %collective-permute-start.20 = (bf16[4,32,768]{2,1,0:T(8,128)(2,1)}, bf16[4,32,768]{2,1,0:T(8,128)(2,1)S(1)}, u32[]{:S(2)}, u32[]{:S(2)}) collective-permute-start(bf16[4,32,768]{2,1,0:T(8,128)(2,1)} %get-tuple-element.72), channel_id=1, source_target_pairs={{0,4},{1,5},{2,6},{3,7},{4,0},{5,1},{6,2},{7,3},{8,12},{9,13},{10,... | collective-permute-start | bytes 589832 | tf_op jit(solution)/shard_map/ppermute | solution.py:87
  58.6 1.9 %collective-permute-start.21 = (bf16[4,32,768]{2,1,0:T(8,128)(2,1)}, bf16[4,32,768]{2,1,0:T(8,128)(2,1)S(1)}, u32[]{:S(2)}, u32[]{:S(2)}) collective-permute-start(bf16[4,32,768]{2,1,0:T(8,128)(2,1)} %get-tuple-element.73), channel_id=1, source_target_pairs={{0,5},{1,4},{2,7},{3,6},{4,1},{5,0},{6,3},{7,2},{8,13},{9,12},{10,... | collective-permute-start | bytes 589832 | tf_op jit(solution)/shard_map/ppermute | solution.py:87
  60.5 0.0 collective-permute-done.3
  60.5 0.0 collective-permute-done.2
  60.5 2.8 %collective-permute-start.6 = (f32[4,32]{1,0:T(4,128)S(1)}, f32[4,32]{1,0:T(4,128)S(1)}, u32[]{:S(2)}, u32[]{:S(2)}) collective-permute-start(f32[4,32]{1,0:T(4,128)S(1)} %get-tuple-element.83.a), channel_id=1, source_target_pairs={{0,96},{32,0},{64,32},{96,64},{1,97},{33,1},{65,33},{97,65},{2,98}... | collective-permute-start | bytes 1544 | tf_op jit(solution)/shard_map/ppermute | solution.py:546
  63.4 0.8 collective-permute-start.5
  64.2 0.9 collective-permute-start.4
  65.1 0.1 pad_add_fusion.1.where
  65.1 0.0 collective-permute-start.22
  65.2 3.3 %collective-permute-done.5.c = f32[4,32]{1,0:T(4,128)S(1)} collective-permute-done((f32[4,32]{1,0:T(4,128)S(1)}, f32[4,32]{1,0:T(4,128)S(1)}, u32[]{:S(2)}, u32[]{:S(2)}) %collective-permute-start.5) | collective-permute-done | bytes 544 | tf_op jit(solution)/shard_map/ppermute | solution.py:546
  68.5 0.5 collective-permute-done.4.b
  69.0 1.8 %collective-permute-start.25 = (bf16[4,32,768]{2,1,0:T(8,128)(2,1)}, bf16[4,32,768]{2,1,0:T(8,128)(2,1)S(1)}, u32[]{:S(2)}, u32[]{:S(2)}) collective-permute-start(bf16[4,32,768]{2,1,0:T(8,128)(2,1)} %get-tuple-element.77), channel_id=1, source_target_pairs={{0,7},{1,2},{2,1},{3,4},{4,3},{5,6},{6,5},{7,0},{8,15},{9,10},{10,... | collective-permute-start | bytes 589832 | tf_op jit(solution)/shard_map/ppermute | solution.py:87
  70.8 1.3 %collective-permute-start.26 = (bf16[4,32,768]{2,1,0:T(8,128)(2,1)}, bf16[4,32,768]{2,1,0:T(8,128)(2,1)S(1)}, u32[]{:S(2)}, u32[]{:S(2)}) collective-permute-start(bf16[4,32,768]{2,1,0:T(8,128)(2,1)} %get-tuple-element.78), channel_id=1, source_target_pairs={{0,1},{1,0},{2,3},{3,2},{4,5},{5,4},{6,7},{7,6},{8,9},{9,8},{10,11... | collective-permute-start | bytes 589832 | tf_op jit(solution)/shard_map/ppermute | solution.py:87
  72.1 1.4 %block_matrix.1 = (f32[32,96,128]{2,1,0:T(8,128)S(1)}, f32[32,96,128]{2,1,0:T(8,128)S(1)}, f32[32,96,128]{2,1,0:T(8,128)S(1)}) custom-call(f32[4,32]{1,0:T(4,128)S(1)} %get-tuple-element.84.shell, f32[96,128]{1,0:T(8,128)S(1)} %add_multiply_fusion.angular), custom_call_target="tpu_custom_call" | custom-call | flops 10000000 | bytes 6000000 | tf_op jit(solution)/shard_map/block_matrix/pallas_call | solution.py:223
  73.5 3.0 %levels.1 = (f32[2304,128]{1,0:T(8,128)S(1)}, f32[2304,128]{1,0:T(8,128)S(1)}) custom-call(s32[3]{0:T(128)S(1)} %pad_add_fusion.1.where, f32[4,32]{1,0:T(4,128)S(1)} %get-tuple-element.83.a, f32[4,32]{1,0:T(4,128)S(1)} %collective-permute-done.4.b, f32[4,32]{1,0:T(4,128)S(1)} %collective-permute-done.5.c, f32[4,32]{1,0:T(4,128)S(1)} %collective-permute-done.6.d), custom_call_target="tpu_custom_call" | custom-call | flops 10000000 | bytes 8000000 | tf_op jit(solution)/shard_map/levels/pallas_call | solution.py:336
  76.6 1.0 collective-permute-done.23.refs_4_
  77.6 0.0 copy-start
  77.6 3.7 %copy-done = bf16[16,384,768]{2,1,0:T(8,128)(2,1)S(1)} copy-done((bf16[16,384,768]{2,1,0:T(8,128)(2,1)S(1)}, bf16[16,384,768]{2,1,0:T(8,128)(2,1)}, u32[]{:S(2)}) %copy-start) | copy-done | bytes 9437208
  81.3 0.9 copy-done.2
  82.2 6.2 %forcing_solve.1 = (f32[32,96,128]{2,1,0:T(8,128)S(1)}, bf16[2,96,128]{2,1,0:T(8,128)(2,1)S(1)}) custom-call(s32[1]{0:T(128)} %bitcast.2.me, f32[4,32]{1,0:T(4,128)S(1)} %get-tuple-element.84.shell, f32[32,16,2,384]{3,2,1,0:T(2,128)S(1)} %copy-done.1, f32[32,96,128]{2,1,0:T(8,128)S(1)} %get-tuple-element.52.pivots, bf16[16,384,768]{2,1,0:T(8,128)(2,1)S(1)} %copy-done, ...), custom_call_target="tpu_custom_call" | custom-call | flops 603979776 | bytes 16000000 | tf_op jit(solution)/shard_map/forcing_solve/pallas_call | solution.py:392
  88.5 2.2 %collective-permute-start.29 = (bf16[2,96,128]{2,1,0:T(8,128)(2,1)S(1)}, bf16[2,96,128]{2,1,0:T(8,128)(2,1)S(1)}, u32[]{:S(2)}, u32[]{:S(2)}) collective-permute-start(bf16[2,96,128]{2,1,0:T(8,128)(2,1)S(1)} %get-tuple-element.79.a), channel_id=1, source_target_pairs={{0,24},{8,0},{16,8},{24,16},{1,25},{9,1},{17,9},{25,17},{2,26},{10... | collective-permute-start | bytes 147464 | tf_op jit(solution)/shard_map/ppermute | solution.py:546
  90.6 1.6 %collective-permute-start.28 = (bf16[2,96,128]{2,1,0:T(8,128)(2,1)S(1)}, bf16[2,96,128]{2,1,0:T(8,128)(2,1)S(1)}, u32[]{:S(2)}, u32[]{:S(2)}) collective-permute-start(bf16[2,96,128]{2,1,0:T(8,128)(2,1)S(1)} %get-tuple-element.79.a), channel_id=1, source_target_pairs={{0,16},{8,24},{16,0},{24,8},{1,17},{9,25},{17,1},{25,9},{2,18},{10... | collective-permute-start | bytes 147464 | tf_op jit(solution)/shard_map/ppermute | solution.py:546
  92.2 0.7 collective-permute-start.27
  92.9 0.1 pad_add_fusion.place
  92.9 3.5 %collective-permute-done.28.c = bf16[2,96,128]{2,1,0:T(8,128)(2,1)S(1)} collective-permute-done((bf16[2,96,128]{2,1,0:T(8,128)(2,1)S(1)}, bf16[2,96,128]{2,1,0:T(8,128)(2,1)S(1)}, u32[]{:S(2)}, u32[]{:S(2)}) %collective-permute-start.28) | collective-permute-done | bytes 49184 | tf_op jit(solution)/shard_map/ppermute | solution.py:546
  96.4 1.3 %collective-permute-done.27.b = bf16[2,96,128]{2,1,0:T(8,128)(2,1)S(1)} collective-permute-done((bf16[2,96,128]{2,1,0:T(8,128)(2,1)S(1)}, bf16[2,96,128]{2,1,0:T(8,128)(2,1)S(1)}, u32[]{:S(2)}, u32[]{:S(2)}) %collective-permute-start.27) | collective-permute-done | bytes 49184 | tf_op jit(solution)/shard_map/ppermute | solution.py:546
  97.7 1.2 %inner_join.1.e = bf16[2,96,128]{2,1,0:T(8,128)(2,1)S(1)} custom-call(s32[2]{0:T(128)S(1)} %pad_add_fusion.place, f32[4,6,96,128]{3,2,1,0:T(8,128)S(1)} %bitcast.11, bf16[2,96,128]{2,1,0:T(8,128)(2,1)S(1)} %get-tuple-element.79.a, bf16[2,96,128]{2,1,0:T(8,128)(2,1)S(1)} %collective-permute-done.27.b, bf16[2,96,128]{2,1,0:T(8,128)(2,1)S(1)} %collective-permute-done.28.c, ...), custom_call_target="tpu_custom_call" | custom-call | flops 1000000 | bytes 2000000 | tf_op jit(solution)/shard_map/inner_join/pallas_call | solution.py:460
  98.9 2.6 %collective-permute-start.32 = (bf16[2,96,128]{2,1,0:T(8,128)(2,1)S(1)}, bf16[2,96,128]{2,1,0:T(8,128)(2,1)S(1)}, u32[]{:S(2)}, u32[]{:S(2)}) collective-permute-start(bf16[2,96,128]{2,1,0:T(8,128)(2,1)S(1)} %inner_join.1.e), channel_id=1, source_target_pairs={{0,96},{32,0},{64,32},{96,64},{1,97},{33,1},{65,33},{97,65},{2,98}... | collective-permute-start | bytes 147464 | tf_op jit(solution)/shard_map/ppermute | solution.py:546
  101.5 1.0 collective-permute-start.31
  102.5 0.9 collective-permute-start.30
  103.4 3.7 %collective-permute-done.31.g = bf16[2,96,128]{2,1,0:T(8,128)(2,1)S(1)} collective-permute-done((bf16[2,96,128]{2,1,0:T(8,128)(2,1)S(1)}, bf16[2,96,128]{2,1,0:T(8,128)(2,1)S(1)}, u32[]{:S(2)}, u32[]{:S(2)}) %collective-permute-start.31) | collective-permute-done | bytes 49184 | tf_op jit(solution)/shard_map/ppermute | solution.py:546
  107.1 0.8 collective-permute-done.30.f
  107.8 3.6 %final_join.1 = f32[32,16,2,384]{3,2,1,0:T(2,128)} custom-call(s32[2]{0:T(128)S(1)} %pad_add_fusion.place, f32[4,6,96,128]{3,2,1,0:T(8,128)S(1)} %bitcast.12, f32[4,6,96,128]{3,2,1,0:T(8,128)S(1)} %bitcast.13, bf16[2,96,128]{2,1,0:T(8,128)(2,1)S(1)} %get-tuple-element.79.a, bf16[2,96,128]{2,1,0:T(8,128)(2,1)S(1)} %collective-permute-done.27.b, ...), custom_call_target="tpu_custom_call" | custom-call | flops 3000000 | bytes 9000000 | tf_op jit(solution)/shard_map/final_join/pallas_call | solution.py:521
  (58 shorter events, 0.2 us)
Async XLA Ops:
  6.1 17.6 %collective-permute-start = (bf16[2,4,16,768]{3,2,1,0:T(8,128)(2,1)}, bf16[2,4,16,768]{3,2,1,0:T(8,128)(2,1)S(1)}, u32[]{:S(2)}, u32[]{:S(2)}) collective-permute-start(bf16[2,4,16,768]{3,2,1,0:T(8,128)(2,1)} %get-tuple-element.44), channel_id=1, source_target_pairs={{0,6},{1,3},{2,0},{3,5},{4,2},{5,7},{6,4},{7,1},{8,14},{9,11},{10,... | collective-permute-start | bytes 589832 | tf_op jit(solution)/shard_map/ppermute | solution.py:87
  10.3 13.4 %collective-permute-start.7 = (bf16[2,4,16,768]{3,2,1,0:T(8,128)(2,1)}, bf16[2,4,16,768]{3,2,1,0:T(8,128)(2,1)S(1)}, u32[]{:S(2)}, u32[]{:S(2)}) collective-permute-start(bf16[2,4,16,768]{3,2,1,0:T(8,128)(2,1)} %get-tuple-element.55), channel_id=1, source_target_pairs={{0,4},{1,5},{2,6},{3,7},{4,0},{5,1},{6,2},{7,3},{8,12},{9,13},{10,... | collective-permute-start | bytes 589832 | tf_op jit(solution)/shard_map/ppermute | solution.py:87
  10.3 13.5 %collective-permute-start.8 = (bf16[2,4,16,768]{3,2,1,0:T(8,128)(2,1)}, bf16[2,4,16,768]{3,2,1,0:T(8,128)(2,1)S(1)}, u32[]{:S(2)}, u32[]{:S(2)}) collective-permute-start(bf16[2,4,16,768]{3,2,1,0:T(8,128)(2,1)} %get-tuple-element.56), channel_id=1, source_target_pairs={{0,5},{1,4},{2,7},{3,6},{4,1},{5,0},{6,3},{7,2},{8,13},{9,12},{10,... | collective-permute-start | bytes 589832 | tf_op jit(solution)/shard_map/ppermute | solution.py:87
  11.0 18.0 %collective-permute-start.9 = (bf16[2,4,16,768]{3,2,1,0:T(8,128)(2,1)}, bf16[2,4,16,768]{3,2,1,0:T(8,128)(2,1)S(1)}, u32[]{:S(2)}, u32[]{:S(2)}) collective-permute-start(bf16[2,4,16,768]{3,2,1,0:T(8,128)(2,1)} %get-tuple-element.57), channel_id=1, source_target_pairs={{0,2},{1,7},{2,4},{3,1},{4,6},{5,3},{6,0},{7,5},{8,10},{9,15},{10,... | collective-permute-start | bytes 589832 | tf_op jit(solution)/shard_map/ppermute | solution.py:87
  12.5 16.5 %collective-permute-start.10 = (bf16[2,4,16,768]{3,2,1,0:T(8,128)(2,1)}, bf16[2,4,16,768]{3,2,1,0:T(8,128)(2,1)S(1)}, u32[]{:S(2)}, u32[]{:S(2)}) collective-permute-start(bf16[2,4,16,768]{3,2,1,0:T(8,128)(2,1)} %get-tuple-element.59), channel_id=1, source_target_pairs={{0,3},{1,6},{2,5},{3,0},{4,7},{5,2},{6,1},{7,4},{8,11},{9,14},{10,... | collective-permute-start | bytes 589832 | tf_op jit(solution)/shard_map/ppermute | solution.py:87
  15.3 8.4 %copy-start.15 = (bf16[2,4,16,768]{3,2,1,0:T(8,128)(2,1)S(1)}, bf16[2,4,16,768]{3,2,1,0:T(8,128)(2,1)}, u32[]{:S(2)}) copy-start(bf16[2,4,16,768]{3,2,1,0:T(8,128)(2,1)} %get-tuple-element.60) | copy-start | bytes 589828
  15.3 8.4 %copy-start.14 = (bf16[2,4,16,768]{3,2,1,0:T(8,128)(2,1)S(1)}, bf16[2,4,16,768]{3,2,1,0:T(8,128)(2,1)}, u32[]{:S(2)}) copy-start(bf16[2,4,16,768]{3,2,1,0:T(8,128)(2,1)} %get-tuple-element.61) | copy-start | bytes 589828
  15.3 26.1 %copy-start.4 = (f32[32]{0:T(128)S(1)}, f32[32]{0:T(128)}, u32[]{:S(2)}) copy-start(f32[32]{0:T(128)} %param.10) | copy-start | bytes 388
  23.7 25.4 %copy-start.5 = (bf16[2,4,16,768]{3,2,1,0:T(8,128)(2,1)}, bf16[2,4,16,768]{3,2,1,0:T(8,128)(2,1)S(1)}, u32[]{:S(2)}) copy-start(bf16[2,4,16,768]{3,2,1,0:T(8,128)(2,1)S(1)} %collective-permute-done.refs_4_) | copy-start | bytes 589828
  23.7 6.3 %collective-permute-start.11 = (bf16[2,4,16,768]{3,2,1,0:T(8,128)(2,1)S(1)}, bf16[2,4,16,768]{3,2,1,0:T(8,128)(2,1)S(1)}, u32[]{:S(2)}, u32[]{:S(2)}) collective-permute-start(bf16[2,4,16,768]{3,2,1,0:T(8,128)(2,1)S(1)} %copy-done.15), channel_id=1, source_target_pairs={{0,7},{1,2},{2,1},{3,4},{4,3},{5,6},{6,5},{7,0},{8,15},{9,10},{10,... | collective-permute-start | bytes 589832 | tf_op jit(solution)/shard_map/ppermute | solution.py:87
  23.7 25.4 %copy-start.6 = (bf16[2,4,16,768]{3,2,1,0:T(8,128)(2,1)}, bf16[2,4,16,768]{3,2,1,0:T(8,128)(2,1)S(1)}, u32[]{:S(2)}) copy-start(bf16[2,4,16,768]{3,2,1,0:T(8,128)(2,1)S(1)} %collective-permute-done.7.refs_1_) | copy-start | bytes 589828
  23.7 9.8 %collective-permute-start.12 = (bf16[2,4,16,768]{3,2,1,0:T(8,128)(2,1)S(1)}, bf16[2,4,16,768]{3,2,1,0:T(8,128)(2,1)S(1)}, u32[]{:S(2)}, u32[]{:S(2)}) collective-permute-start(bf16[2,4,16,768]{3,2,1,0:T(8,128)(2,1)S(1)} %copy-done.14), channel_id=1, source_target_pairs={{0,1},{1,0},{2,3},{3,2},{4,5},{5,4},{6,7},{7,6},{8,9},{9,8},{10,11... | collective-permute-start | bytes 589832 | tf_op jit(solution)/shard_map/ppermute | solution.py:87
  23.8 25.3 %copy-start.7 = (bf16[2,4,16,768]{3,2,1,0:T(8,128)(2,1)}, bf16[2,4,16,768]{3,2,1,0:T(8,128)(2,1)S(1)}, u32[]{:S(2)}) copy-start(bf16[2,4,16,768]{3,2,1,0:T(8,128)(2,1)S(1)} %collective-permute-done.8.refs_2_) | copy-start | bytes 589828
  23.9 11.2 %collective-permute-start.13 = (bf16[2,4,16,768]{3,2,1,0:T(8,128)(2,1)}, bf16[2,4,16,768]{3,2,1,0:T(8,128)(2,1)S(1)}, u32[]{:S(2)}, u32[]{:S(2)}) collective-permute-start(bf16[2,4,16,768]{3,2,1,0:T(8,128)(2,1)} %get-tuple-element.64), channel_id=1, source_target_pairs={{0,4},{1,5},{2,6},{3,7},{4,0},{5,1},{6,2},{7,3},{8,12},{9,13},{10,... | collective-permute-start | bytes 589832 | tf_op jit(solution)/shard_map/ppermute | solution.py:87
  29.0 20.2 %copy-start.8 = (bf16[2,4,16,768]{3,2,1,0:T(8,128)(2,1)}, bf16[2,4,16,768]{3,2,1,0:T(8,128)(2,1)S(1)}, u32[]{:S(2)}) copy-start(bf16[2,4,16,768]{3,2,1,0:T(8,128)(2,1)S(1)} %collective-permute-done.9.refs_3_) | copy-start | bytes 589828
  29.0 12.4 %collective-permute-start.14 = (bf16[2,4,16,768]{3,2,1,0:T(8,128)(2,1)}, bf16[2,4,16,768]{3,2,1,0:T(8,128)(2,1)S(1)}, u32[]{:S(2)}, u32[]{:S(2)}) collective-permute-start(bf16[2,4,16,768]{3,2,1,0:T(8,128)(2,1)} %get-tuple-element.65), channel_id=1, source_target_pairs={{0,5},{1,4},{2,7},{3,6},{4,1},{5,0},{6,3},{7,2},{8,13},{9,12},{10,... | collective-permute-start | bytes 589832 | tf_op jit(solution)/shard_map/ppermute | solution.py:87
  29.0 20.1 %copy-start.9 = (bf16[2,4,16,768]{3,2,1,0:T(8,128)(2,1)}, bf16[2,4,16,768]{3,2,1,0:T(8,128)(2,1)S(1)}, u32[]{:S(2)}) copy-start(bf16[2,4,16,768]{3,2,1,0:T(8,128)(2,1)S(1)} %collective-permute-done.10.refs_5_) | copy-start | bytes 589828
  29.0 15.4 %collective-permute-start.15 = (bf16[2,4,16,768]{3,2,1,0:T(8,128)(2,1)}, bf16[2,4,16,768]{3,2,1,0:T(8,128)(2,1)S(1)}, u32[]{:S(2)}, u32[]{:S(2)}) collective-permute-start(bf16[2,4,16,768]{3,2,1,0:T(8,128)(2,1)} %get-tuple-element.66), channel_id=1, source_target_pairs={{0,2},{1,7},{2,4},{3,1},{4,6},{5,3},{6,0},{7,5},{8,10},{9,15},{10,... | collective-permute-start | bytes 589832 | tf_op jit(solution)/shard_map/ppermute | solution.py:87
  30.0 19.1 %copy-start.10 = (bf16[2,4,16,768]{3,2,1,0:T(8,128)(2,1)}, bf16[2,4,16,768]{3,2,1,0:T(8,128)(2,1)S(1)}, u32[]{:S(2)}) copy-start(bf16[2,4,16,768]{3,2,1,0:T(8,128)(2,1)S(1)} %collective-permute-done.11.refs_6_) | copy-start | bytes 589828
  30.0 17.5 %collective-permute-start.16 = (bf16[2,4,16,768]{3,2,1,0:T(8,128)(2,1)}, bf16[2,4,16,768]{3,2,1,0:T(8,128)(2,1)S(1)}, u32[]{:S(2)}, u32[]{:S(2)}) collective-permute-start(bf16[2,4,16,768]{3,2,1,0:T(8,128)(2,1)} %get-tuple-element.67), channel_id=1, source_target_pairs={{0,6},{1,3},{2,0},{3,5},{4,2},{5,7},{6,4},{7,1},{8,14},{9,11},{10,... | collective-permute-start | bytes 589832 | tf_op jit(solution)/shard_map/ppermute | solution.py:87
  33.5 15.7 %copy-start.11 = (bf16[2,4,16,768]{3,2,1,0:T(8,128)(2,1)}, bf16[2,4,16,768]{3,2,1,0:T(8,128)(2,1)S(1)}, u32[]{:S(2)}) copy-start(bf16[2,4,16,768]{3,2,1,0:T(8,128)(2,1)S(1)} %collective-permute-done.12.refs_7_) | copy-start | bytes 589828
  33.5 14.6 %collective-permute-start.17 = (bf16[2,4,16,768]{3,2,1,0:T(8,128)(2,1)}, bf16[2,4,16,768]{3,2,1,0:T(8,128)(2,1)S(1)}, u32[]{:S(2)}, u32[]{:S(2)}) collective-permute-start(bf16[2,4,16,768]{3,2,1,0:T(8,128)(2,1)} %get-tuple-element.68), channel_id=1, source_target_pairs={{0,3},{1,6},{2,5},{3,0},{4,7},{5,2},{6,1},{7,4},{8,11},{9,14},{10,... | collective-permute-start | bytes 589832 | tf_op jit(solution)/shard_map/ppermute | solution.py:87
  35.0 14.2 %copy-start.12 = (bf16[2,4,16,768]{3,2,1,0:T(8,128)(2,1)}, bf16[2,4,16,768]{3,2,1,0:T(8,128)(2,1)S(1)}, u32[]{:S(2)}) copy-start(bf16[2,4,16,768]{3,2,1,0:T(8,128)(2,1)S(1)} %collective-permute-done.13.refs_9_) | copy-start | bytes 589828
  35.0 14.1 %collective-permute-start.18 = (bf16[2,4,16,768]{3,2,1,0:T(8,128)(2,1)}, bf16[2,4,16,768]{3,2,1,0:T(8,128)(2,1)S(1)}, u32[]{:S(2)}, u32[]{:S(2)}) collective-permute-start(bf16[2,4,16,768]{3,2,1,0:T(8,128)(2,1)} %get-tuple-element.69), channel_id=1, source_target_pairs={{0,7},{1,2},{2,1},{3,4},{4,3},{5,6},{6,5},{7,0},{8,15},{9,10},{10,... | collective-permute-start | bytes 589832 | tf_op jit(solution)/shard_map/ppermute | solution.py:87
  41.4 7.8 %copy-start.13 = (bf16[2,4,16,768]{3,2,1,0:T(8,128)(2,1)}, bf16[2,4,16,768]{3,2,1,0:T(8,128)(2,1)S(1)}, u32[]{:S(2)}) copy-start(bf16[2,4,16,768]{3,2,1,0:T(8,128)(2,1)S(1)} %collective-permute-done.14.refs_10_) | copy-start | bytes 589828
  41.4 7.7 %collective-permute-start.19 = (bf16[2,4,16,768]{3,2,1,0:T(8,128)(2,1)}, bf16[2,4,16,768]{3,2,1,0:T(8,128)(2,1)S(1)}, u32[]{:S(2)}, u32[]{:S(2)}) collective-permute-start(bf16[2,4,16,768]{3,2,1,0:T(8,128)(2,1)} %get-tuple-element.70), channel_id=1, source_target_pairs={{0,1},{1,0},{2,3},{3,2},{4,5},{5,4},{6,7},{7,6},{8,9},{9,8},{10,11... | collective-permute-start | bytes 589832 | tf_op jit(solution)/shard_map/ppermute | solution.py:87
  44.4 4.8 %copy-start.16 = (bf16[2,4,16,768]{3,2,1,0:T(8,128)(2,1)}, bf16[2,4,16,768]{3,2,1,0:T(8,128)(2,1)S(1)}, u32[]{:S(2)}) copy-start(bf16[2,4,16,768]{3,2,1,0:T(8,128)(2,1)S(1)} %collective-permute-done.15.refs_11_) | copy-start | bytes 589828
  44.4 16.1 %collective-permute-start.3 = (f32[1,32]{1,0:T(1,128)S(1)}, f32[1,32]{1,0:T(1,128)S(1)}, u32[]{:S(2)}, u32[]{:S(2)}) collective-permute-start(f32[1,32]{1,0:T(1,128)S(1)} %bitcast.14), channel_id=1, source_target_pairs={{0,24},{8,0},{16,8},{24,16},{1,25},{9,1},{17,9},{25,17},{2,26},{10... | collective-permute-start | bytes 392 | tf_op jit(solution)/shard_map/ppermute | solution.py:546
  47.5 1.7 %copy-start.17 = (bf16[2,4,16,768]{3,2,1,0:T(8,128)(2,1)}, bf16[2,4,16,768]{3,2,1,0:T(8,128)(2,1)S(1)}, u32[]{:S(2)}) copy-start(bf16[2,4,16,768]{3,2,1,0:T(8,128)(2,1)S(1)} %collective-permute-done.16.refs_12_) | copy-start | bytes 589828
  47.5 13.0 %collective-permute-start.2 = (f32[1,32]{1,0:T(1,128)S(1)}, f32[1,32]{1,0:T(1,128)S(1)}, u32[]{:S(2)}, u32[]{:S(2)}) collective-permute-start(f32[1,32]{1,0:T(1,128)S(1)} %bitcast.15), channel_id=1, source_target_pairs={{0,16},{8,24},{16,0},{24,8},{1,17},{9,25},{17,1},{25,9},{2,18},{10... | collective-permute-start | bytes 392 | tf_op jit(solution)/shard_map/ppermute | solution.py:546
  48.1 1.1 copy-start.18
  48.1 12.4 %collective-permute-start.1 = (f32[1,32]{1,0:T(1,128)S(1)}, f32[1,32]{1,0:T(1,128)S(1)}, u32[]{:S(2)}, u32[]{:S(2)}) collective-permute-start(f32[1,32]{1,0:T(1,128)S(1)} %bitcast.16), channel_id=1, source_target_pairs={{0,8},{8,16},{16,24},{24,0},{1,9},{9,17},{17,25},{25,1},{2,10},{10... | collective-permute-start | bytes 392 | tf_op jit(solution)/shard_map/ppermute | solution.py:546
  49.1 0.7 copy-start.19
  49.1 0.7 copy-start.20
  49.8 22.3 %copy-start.3 = (s32[96,128]{1,0:T(8,128)S(1)}, s32[96,128]{1,0:T(8,128)}, u32[]{:S(2)}) copy-start(s32[96,128]{1,0:T(8,128)} %constant.41.clone) | copy-start | bytes 147460
  49.8 27.8 %copy-start.1 = (f32[32,16,2,384]{3,2,1,0:T(2,128)S(1)}, f32[32,16,2,384]{3,2,1,0:T(2,128)}, u32[]{:S(2)}) copy-start(f32[32,16,2,384]{3,2,1,0:T(2,128)} %field.5) | copy-start | bytes 4718596
  56.6 12.4 %collective-permute-start.20 = (bf16[4,32,768]{2,1,0:T(8,128)(2,1)}, bf16[4,32,768]{2,1,0:T(8,128)(2,1)S(1)}, u32[]{:S(2)}, u32[]{:S(2)}) collective-permute-start(bf16[4,32,768]{2,1,0:T(8,128)(2,1)} %get-tuple-element.72), channel_id=1, source_target_pairs={{0,4},{1,5},{2,6},{3,7},{4,0},{5,1},{6,2},{7,3},{8,12},{9,13},{10,... | collective-permute-start | bytes 589832 | tf_op jit(solution)/shard_map/ppermute | solution.py:87
  58.6 12.2 %collective-permute-start.21 = (bf16[4,32,768]{2,1,0:T(8,128)(2,1)}, bf16[4,32,768]{2,1,0:T(8,128)(2,1)S(1)}, u32[]{:S(2)}, u32[]{:S(2)}) collective-permute-start(bf16[4,32,768]{2,1,0:T(8,128)(2,1)} %get-tuple-element.73), channel_id=1, source_target_pairs={{0,5},{1,4},{2,7},{3,6},{4,1},{5,0},{6,3},{7,2},{8,13},{9,12},{10,... | collective-permute-start | bytes 589832 | tf_op jit(solution)/shard_map/ppermute | solution.py:87
  60.5 4.6 %collective-permute-start.6 = (f32[4,32]{1,0:T(4,128)S(1)}, f32[4,32]{1,0:T(4,128)S(1)}, u32[]{:S(2)}, u32[]{:S(2)}) collective-permute-start(f32[4,32]{1,0:T(4,128)S(1)} %get-tuple-element.83.a), channel_id=1, source_target_pairs={{0,96},{32,0},{64,32},{96,64},{1,97},{33,1},{65,33},{97,65},{2,98}... | collective-permute-start | bytes 1544 | tf_op jit(solution)/shard_map/ppermute | solution.py:546
  63.4 5.1 %collective-permute-start.5 = (f32[4,32]{1,0:T(4,128)S(1)}, f32[4,32]{1,0:T(4,128)S(1)}, u32[]{:S(2)}, u32[]{:S(2)}) collective-permute-start(f32[4,32]{1,0:T(4,128)S(1)} %get-tuple-element.83.a), channel_id=1, source_target_pairs={{0,64},{32,96},{64,0},{96,32},{1,65},{33,97},{65,1},{97,33},{2,66}... | collective-permute-start | bytes 1544 | tf_op jit(solution)/shard_map/ppermute | solution.py:546
  64.2 4.8 %collective-permute-start.4 = (f32[4,32]{1,0:T(4,128)S(1)}, f32[4,32]{1,0:T(4,128)S(1)}, u32[]{:S(2)}, u32[]{:S(2)}) collective-permute-start(f32[4,32]{1,0:T(4,128)S(1)} %get-tuple-element.83.a), channel_id=1, source_target_pairs={{0,32},{32,64},{64,96},{96,0},{1,33},{33,65},{65,97},{97,1},{2,34}... | collective-permute-start | bytes 1544 | tf_op jit(solution)/shard_map/ppermute | solution.py:546
  65.1 11.4 %collective-permute-start.22 = (bf16[4,32,768]{2,1,0:T(8,128)(2,1)}, bf16[4,32,768]{2,1,0:T(8,128)(2,1)S(1)}, u32[]{:S(2)}, u32[]{:S(2)}) collective-permute-start(bf16[4,32,768]{2,1,0:T(8,128)(2,1)} %get-tuple-element.74), channel_id=1, source_target_pairs={{0,6},{1,3},{2,0},{3,5},{4,2},{5,7},{6,4},{7,1},{8,14},{9,11},{10,... | collective-permute-start | bytes 589832 | tf_op jit(solution)/shard_map/ppermute | solution.py:87
  68.5 9.1 %collective-permute-start.23 = (bf16[4,32,768]{2,1,0:T(8,128)(2,1)}, bf16[4,32,768]{2,1,0:T(8,128)(2,1)S(1)}, u32[]{:S(2)}, u32[]{:S(2)}) collective-permute-start(bf16[4,32,768]{2,1,0:T(8,128)(2,1)} %get-tuple-element.75), channel_id=1, source_target_pairs={{0,2},{1,7},{2,4},{3,1},{4,6},{5,3},{6,0},{7,5},{8,10},{9,15},{10,... | collective-permute-start | bytes 589832 | tf_op jit(solution)/shard_map/ppermute | solution.py:87
  69.0 8.6 %collective-permute-start.24 = (bf16[4,32,768]{2,1,0:T(8,128)(2,1)}, bf16[4,32,768]{2,1,0:T(8,128)(2,1)S(1)}, u32[]{:S(2)}, u32[]{:S(2)}) collective-permute-start(bf16[4,32,768]{2,1,0:T(8,128)(2,1)} %get-tuple-element.76), channel_id=1, source_target_pairs={{0,3},{1,6},{2,5},{3,0},{4,7},{5,2},{6,1},{7,4},{8,11},{9,14},{10,... | collective-permute-start | bytes 589832 | tf_op jit(solution)/shard_map/ppermute | solution.py:87
  69.0 8.6 %collective-permute-start.25 = (bf16[4,32,768]{2,1,0:T(8,128)(2,1)}, bf16[4,32,768]{2,1,0:T(8,128)(2,1)S(1)}, u32[]{:S(2)}, u32[]{:S(2)}) collective-permute-start(bf16[4,32,768]{2,1,0:T(8,128)(2,1)} %get-tuple-element.77), channel_id=1, source_target_pairs={{0,7},{1,2},{2,1},{3,4},{4,3},{5,6},{6,5},{7,0},{8,15},{9,10},{10,... | collective-permute-start | bytes 589832 | tf_op jit(solution)/shard_map/ppermute | solution.py:87
  70.8 6.8 %collective-permute-start.26 = (bf16[4,32,768]{2,1,0:T(8,128)(2,1)}, bf16[4,32,768]{2,1,0:T(8,128)(2,1)S(1)}, u32[]{:S(2)}, u32[]{:S(2)}) collective-permute-start(bf16[4,32,768]{2,1,0:T(8,128)(2,1)} %get-tuple-element.78), channel_id=1, source_target_pairs={{0,1},{1,0},{2,3},{3,2},{4,5},{5,4},{6,7},{7,6},{8,9},{9,8},{10,11... | collective-permute-start | bytes 589832 | tf_op jit(solution)/shard_map/ppermute | solution.py:87
  77.6 3.7 %copy-start = (bf16[16,384,768]{2,1,0:T(8,128)(2,1)S(1)}, bf16[16,384,768]{2,1,0:T(8,128)(2,1)}, u32[]{:S(2)}) copy-start(bf16[16,384,768]{2,1,0:T(8,128)(2,1)} %legendre.5) | copy-start | bytes 28311556
  81.3 0.9 copy-start.2
  88.5 4.5 %collective-permute-start.29 = (bf16[2,96,128]{2,1,0:T(8,128)(2,1)S(1)}, bf16[2,96,128]{2,1,0:T(8,128)(2,1)S(1)}, u32[]{:S(2)}, u32[]{:S(2)}) collective-permute-start(bf16[2,96,128]{2,1,0:T(8,128)(2,1)S(1)} %get-tuple-element.79.a), channel_id=1, source_target_pairs={{0,24},{8,0},{16,8},{24,16},{1,25},{9,1},{17,9},{25,17},{2,26},{10... | collective-permute-start | bytes 147464 | tf_op jit(solution)/shard_map/ppermute | solution.py:546
  90.6 5.8 %collective-permute-start.28 = (bf16[2,96,128]{2,1,0:T(8,128)(2,1)S(1)}, bf16[2,96,128]{2,1,0:T(8,128)(2,1)S(1)}, u32[]{:S(2)}, u32[]{:S(2)}) collective-permute-start(bf16[2,96,128]{2,1,0:T(8,128)(2,1)S(1)} %get-tuple-element.79.a), channel_id=1, source_target_pairs={{0,16},{8,24},{16,0},{24,8},{1,17},{9,25},{17,1},{25,9},{2,18},{10... | collective-permute-start | bytes 147464 | tf_op jit(solution)/shard_map/ppermute | solution.py:546
  92.2 5.5 %collective-permute-start.27 = (bf16[2,96,128]{2,1,0:T(8,128)(2,1)S(1)}, bf16[2,96,128]{2,1,0:T(8,128)(2,1)S(1)}, u32[]{:S(2)}, u32[]{:S(2)}) collective-permute-start(bf16[2,96,128]{2,1,0:T(8,128)(2,1)S(1)} %get-tuple-element.79.a), channel_id=1, source_target_pairs={{0,8},{8,16},{16,24},{24,0},{1,9},{9,17},{17,25},{25,1},{2,10},{10... | collective-permute-start | bytes 147464 | tf_op jit(solution)/shard_map/ppermute | solution.py:546
  98.9 4.5 %collective-permute-start.32 = (bf16[2,96,128]{2,1,0:T(8,128)(2,1)S(1)}, bf16[2,96,128]{2,1,0:T(8,128)(2,1)S(1)}, u32[]{:S(2)}, u32[]{:S(2)}) collective-permute-start(bf16[2,96,128]{2,1,0:T(8,128)(2,1)S(1)} %inner_join.1.e), channel_id=1, source_target_pairs={{0,96},{32,0},{64,32},{96,64},{1,97},{33,1},{65,33},{97,65},{2,98}... | collective-permute-start | bytes 147464 | tf_op jit(solution)/shard_map/ppermute | solution.py:546
  101.5 5.6 %collective-permute-start.31 = (bf16[2,96,128]{2,1,0:T(8,128)(2,1)S(1)}, bf16[2,96,128]{2,1,0:T(8,128)(2,1)S(1)}, u32[]{:S(2)}, u32[]{:S(2)}) collective-permute-start(bf16[2,96,128]{2,1,0:T(8,128)(2,1)S(1)} %inner_join.1.e), channel_id=1, source_target_pairs={{0,64},{32,96},{64,0},{96,32},{1,65},{33,97},{65,1},{97,33},{2,66}... | collective-permute-start | bytes 147464 | tf_op jit(solution)/shard_map/ppermute | solution.py:546
  102.5 5.3 %collective-permute-start.30 = (bf16[2,96,128]{2,1,0:T(8,128)(2,1)S(1)}, bf16[2,96,128]{2,1,0:T(8,128)(2,1)S(1)}, u32[]{:S(2)}, u32[]{:S(2)}) collective-permute-start(bf16[2,96,128]{2,1,0:T(8,128)(2,1)S(1)} %inner_join.1.e), channel_id=1, source_target_pairs={{0,32},{32,64},{64,96},{96,0},{1,33},{33,65},{65,97},{97,1},{2,34}... | collective-permute-start | bytes 147464 | tf_op jit(solution)/shard_map/ppermute | solution.py:546
